TPU v7x, 128 devices: a whole 4x4x4 slice. The times are simulated.
128 devices in a mesh: dp: 4 (over z), ctx: 32 (over y, x, core).
Axes of the slice: x: 4, y: 4, z: 4, core: 2. Of those that a mesh axis runs over, the one named last changes fastest.
Arguments:
- queries: bfloat16 [32768, 4096], P(('dp', 'ctx')), parts along dimension 0, may hold values from -10 to 10
- keys: bfloat16 [32768, 1024], P(('dp', 'ctx')), parts along dimension 0, may hold values from -6 to 6
- values: bfloat16 [32768, 1024], P(('dp', 'ctx')), parts along dimension 0, may hold values from -6 to 6
- doc_lengths: int32 [64], P('dp'), parts along dimension 0, may hold values from 1 to 4352, 8192 in all
Outputs:
- attended: bfloat16 [32768, 4096], P(('dp', 'ctx')), parts along dimension 0
There are 4 independent parts, one for each index of `dp`. A program takes and returns all parts, laid end to end along the dimension named above; each array names one. Nothing has to cross between parts.
All inputs are finite; a program needn't handle non-finite values.
Results may differ from a plain program's by a relative error of at most 0.0055.
Values may be sent and summed in bfloat16 or wider, within the bound.
No kernel may reach another device: no remote copies, remote signals or barrier semaphores. Data moves between devices by JAX's collectives and lax.ppermute only.
A program may use at most 128 MiB of HBM per device.

v0:
```python
import math

import jax
import jax.numpy as jnp
from jax import lax
from jax.sharding import PartitionSpec as P

H = 32
KVH = 8
DH = 128


NEG_FILL = -1e30


def pick_rows():
    for tile_rows in (512, 256, 128, 64, 32, 16, 8, 4, 2, 1):
        return tile_rows
    return 1


def doc_firsts(doc_lengths, count):
    doc_end = jnp.cumsum(doc_lengths)
    doc_first = doc_end - doc_lengths
    positions = jnp.arange(count, dtype=jnp.int32)
    inside = (doc_first[None, :] <= positions[:, None]) & (positions[:, None] < doc_end[None, :])
    return jnp.sum(jnp.where(inside, doc_first[None, :], 0), axis=1)


def tile_update(carry, q_block, k_tile, v_tile, q_pos, q_first, k_pos, scaling):
    running_max, totals, summed = carry
    scores = (
        jnp.einsum("qkgd,rkd->kgqr", q_block, k_tile, preferred_element_type=jnp.float32) * scaling
    )
    visible = (k_pos[None, :] <= q_pos[:, None]) & (k_pos[None, :] >= q_first[:, None])
    scores = jnp.where(visible, scores, NEG_FILL)
    new_max = jnp.maximum(running_max, jnp.max(scores, axis=-1))
    weights = jnp.where(visible, jnp.exp(scores - new_max[..., None]), 0.0)
    rescale = jnp.exp(running_max - new_max)
    totals = totals * rescale + jnp.sum(weights, axis=-1)
    summed = summed * rescale[..., None] + jnp.einsum(
        "kgqr,rkd->kgqd", weights.astype(jnp.bfloat16), v_tile, preferred_element_type=jnp.float32
    )
    return (new_max, totals, summed)


def visit_tile(carry, q_block, k_tile, v_tile, q_pos, q_first, k_pos, scaling):
    visible = (k_pos[None, :] <= q_pos[:, None]) & (k_pos[None, :] >= q_first[:, None])
    return lax.cond(
        jnp.any(visible),
        lambda state: tile_update(state, q_block, k_tile, v_tile, q_pos, q_first, k_pos, scaling),
        lambda state: state,
        carry,
    )


def empty_carry(kv_heads, q_per_kv, row_count):
    return (
        jnp.full((kv_heads, q_per_kv, row_count), NEG_FILL, jnp.float32),
        jnp.zeros((kv_heads, q_per_kv, row_count), jnp.float32),
        jnp.zeros((kv_heads, q_per_kv, row_count, DH), jnp.float32),
    )


def finish(carry, row_count):
    running_max, totals, summed = carry
    result = summed / totals[..., None]
    return jnp.transpose(result, (2, 0, 1, 3)).reshape(row_count, -1).astype(jnp.bfloat16)


def per_device(queries, keys, values, doc_lengths):
    local_rows = queries.shape[0]
    devices_ctx = lax.axis_size("ctx")
    seq_rows = local_rows * devices_ctx
    q_per_kv = H // KVH
    scaling = 1.0 / math.sqrt(DH)
    doc_first = doc_firsts(doc_lengths, seq_rows)
    my_rank = lax.axis_index("ctx")
    q_pos = my_rank * local_rows + jnp.arange(local_rows, dtype=jnp.int32)
    q_first = lax.dynamic_slice_in_dim(doc_first, my_rank * local_rows, local_rows, 0)
    query_heads = queries.reshape(local_rows, KVH, q_per_kv, DH)
    key_piece = lax.all_gather(keys, "ctx", axis=0, tiled=True)
    value_piece = lax.all_gather(values, "ctx", axis=0, tiled=True)
    row_count = key_piece.shape[0]
    tile_rows = pick_rows()
    key_heads = key_piece.reshape(row_count, KVH, DH)
    value_heads = value_piece.reshape(row_count, KVH, DH)

    def advance(tile_id, state):
        key_row = tile_id * tile_rows
        k_tile = lax.dynamic_slice_in_dim(key_heads, key_row, tile_rows, 0)
        v_tile = lax.dynamic_slice_in_dim(value_heads, key_row, tile_rows, 0)
        k_pos = key_row + jnp.arange(tile_rows, dtype=jnp.int32)
        return visit_tile(state, query_heads, k_tile, v_tile, q_pos, q_first, k_pos, scaling)

    carry = lax.fori_loop(
        0, row_count // tile_rows, advance, empty_carry(KVH, q_per_kv, local_rows)
    )
    return finish(carry, local_rows)


def solution(mesh):
    placed = (P(("dp", "ctx"), None), P(("dp", "ctx"), None), P(("dp", "ctx"), None), P("dp"))
    return jax.shard_map(
        per_device, mesh=mesh, in_specs=placed, out_specs=P(("dp", "ctx"), None), check_vma=False
    )
```

profile of v0, /device:TPU:25, one launch (start us, length us, event | category | flops | bytes accessed | tf_op | source)
XLA Modules:
  0.0 399.3 jit_solution(12955195001146600502)
XLA Ops:
  6.5 2.0 copy.19
  8.6 2.0 copy.21
  12.3 3.3 copy.20
  15.5 2.4 copy.23
  18.2 74.5 %all-gather.3.cloned.1.call-done = bf16[8192,1024]{0,1:T(8,128)(2,1)} async-done(((bf16[256,1024]{0,1:T(8,128)(2,1)}), bf16[8192,1024]{0,1:T(8,128)(2,1)}) %all-gather.3.cloned.1.call-update) | async-done | bytes 16777232 | tf_op jit(solution)/shard_map/all_gather | solution.py:82
  92.7 21.4 %copy.22 = bf16[8192,8,128]{2,0,1:T(8,128)(2,1)} copy(bf16[8192,8,128]{0,2,1:T(8,128)(2,1)} %bitcast.38) | data formatting | bytes 33554432
  114.0 61.9 %all-gather.5.cloned.1.call-done = bf16[8192,1024]{0,1:T(8,128)(2,1)} async-done(((bf16[256,1024]{0,1:T(8,128)(2,1)}), bf16[8192,1024]{0,1:T(8,128)(2,1)}) %all-gather.5.cloned.1.call-update) | async-done | bytes 16777232 | tf_op jit(solution)/shard_map/all_gather | solution.py:83
  176.0 21.2 %copy.24 = bf16[8192,8,128]{2,0,1:T(8,128)(2,1)} copy(bf16[8192,8,128]{0,2,1:T(8,128)(2,1)} %bitcast.39) | data formatting | bytes 33554432
  197.2 2.5 broadcast_in_dim.64
  199.7 185.4 %while.18 = (s32[]{:T(128)}, f32[8,4,256]{2,1,0:T(4,128)S(1)}, f32[8,4,256]{2,1,0:T(4,128)S(1)}, f32[8,4,256,128]{3,2,1,0:T(8,128)}, s32[256]{0:T(256)S(1)}, /*i...) while((s32[]{:T(128)}, f32[8,4,256]{2,1,0:T(4,128)S(1)}, ...), condition=%wide.region_8.9_spmd.clone, body=%wide.region_2.8_spmd.clone.sunk | while | flops 2205041920 | bytes 63980856 | solution.py:96
  207.7 17.8 %conditional.3 = ((f32[8,4,256]{2,1,0:T(4,128)S(1)}, f32[8,4,256]{2,1,0:T(4,128)S(1)}, f32[8,4,256,128]{3,2,1,0:T(8,128)})) conditional(s32[]{:T(128)} %convert_element_type.34, (f32[8,4,256]{2,1,0:T(4,128)S(1)}, f32[8,4,256]{2,1,0:T(4,128)S(1)}, f32[8,4,256,128]{3,2,1,0:T(8,128)}) %tuple.56, (s32[]{:T(128)}, s32[512]{0:T(512)S(1)}, ...), branch_computations={%region_4.4_spmd, %region_5.7_spmd} | conditional | flops 2204516864 | bytes 63971404 | solution.py:49
  207.9 4.3 %fusion.2 = (f32[8,4,256]{2,1,0:T(4,128)S(1)}, f32[8,512,256,4]{2,1,3,0:T(8,128)S(1)}) fusion(pred[256,512]{0,1:T(8,128)(4,1)S(1)} %compare_and_fusion, bf16[256,8,4,128]{3,0,2,1:T(8,128)(2,1)} %get-tuple-element.274, bf16[8192,8,128]{2,0,1:T(8,128)(2,1)} %get-tuple-element.273, s32[]{:T(128)S(6)} %select_n.25), kind=kOutput, calls=%fused_computation.3 | convolution fusion | flops 1086316544 | bytes 20086788 | tf_op jit(solution)/shard_map/while/body/eval_jaxpr/cond/branch_1_fun/qkgd,rkd->kgqr/dot_general | solution.py:33
  212.3 4.3 %fusion.4 = f32[8,4,256]{2,1,0:T(4,128)S(1)} fusion(f32[8,512,256,4]{2,1,3,0:T(8,128)S(1)} %get-tuple-element.358, f32[8,4,256]{2,1,0:T(4,128)S(1)} %max.5, pred[256,512]{0,1:T(8,128)(4,1)S(1)} %compare_and_fusion), kind=kLoop, calls=%fused_computation.5 | loop fusion | flops 20963328 | bytes 16973824 | tf_op jit(solution)/shard_map/while/body/eval_jaxpr/cond/branch_1_fun/reduce_sum | solution.py:40
  216.6 8.9 %multiply_add_fusion = f32[8,4,256,128]{3,2,1,0:T(8,128)} fusion(f32[8,4,256,128]{3,2,1,0:T(8,128)} %get-tuple-element.276, f32[8,4,256]{2,1,0:T(4,128)S(1)} %bitcast.46, f32[8,512,256,4]{2,1,3,0:T(8,128)S(1)} %get-tuple-element.358, f32[8,4,256]{2,1,0:T(4,128)S(1)} %max.5, pred[256,512]{0,1:T(8,128)(4,1)S(1)} %compare_and_fusion, ...), kind=kOutput, calls=%fused_computation.8 | convolution fusion | flops 1096810496 | bytes 26411012 | tf_op jit(solution)/shard_map/while/body/eval_jaxpr/cond/branch_1_fun/kgqr,rkd->kgqd/dot_general | solution.py:41
  227.1 17.8 %conditional.3 = ((f32[8,4,256]{2,1,0:T(4,128)S(1)}, f32[8,4,256]{2,1,0:T(4,128)S(1)}, f32[8,4,256,128]{3,2,1,0:T(8,128)})) conditional(s32[]{:T(128)} %convert_element_type.34, (f32[8,4,256]{2,1,0:T(4,128)S(1)}, f32[8,4,256]{2,1,0:T(4,128)S(1)}, f32[8,4,256,128]{3,2,1,0:T(8,128)}) %tuple.56, (s32[]{:T(128)}, s32[512]{0:T(512)S(1)}, ...), branch_computations={%region_4.4_spmd, %region_5.7_spmd} | conditional | flops 2204516864 | bytes 63971404 | solution.py:49
  227.3 4.3 %fusion.2 = (f32[8,4,256]{2,1,0:T(4,128)S(1)}, f32[8,512,256,4]{2,1,3,0:T(8,128)S(1)}) fusion(pred[256,512]{0,1:T(8,128)(4,1)S(1)} %compare_and_fusion, bf16[256,8,4,128]{3,0,2,1:T(8,128)(2,1)} %get-tuple-element.274, bf16[8192,8,128]{2,0,1:T(8,128)(2,1)} %get-tuple-element.273, s32[]{:T(128)S(6)} %select_n.25), kind=kOutput, calls=%fused_computation.3 | convolution fusion | flops 1086316544 | bytes 20086788 | tf_op jit(solution)/shard_map/while/body/eval_jaxpr/cond/branch_1_fun/qkgd,rkd->kgqr/dot_general | solution.py:33
  231.6 4.3 %fusion.4 = f32[8,4,256]{2,1,0:T(4,128)S(1)} fusion(f32[8,512,256,4]{2,1,3,0:T(8,128)S(1)} %get-tuple-element.358, f32[8,4,256]{2,1,0:T(4,128)S(1)} %max.5, pred[256,512]{0,1:T(8,128)(4,1)S(1)} %compare_and_fusion), kind=kLoop, calls=%fused_computation.5 | loop fusion | flops 20963328 | bytes 16973824 | tf_op jit(solution)/shard_map/while/body/eval_jaxpr/cond/branch_1_fun/reduce_sum | solution.py:40
  235.9 8.9 %multiply_add_fusion = f32[8,4,256,128]{3,2,1,0:T(8,128)} fusion(f32[8,4,256,128]{3,2,1,0:T(8,128)} %get-tuple-element.276, f32[8,4,256]{2,1,0:T(4,128)S(1)} %bitcast.46, f32[8,512,256,4]{2,1,3,0:T(8,128)S(1)} %get-tuple-element.358, f32[8,4,256]{2,1,0:T(4,128)S(1)} %max.5, pred[256,512]{0,1:T(8,128)(4,1)S(1)} %compare_and_fusion, ...), kind=kOutput, calls=%fused_computation.8 | convolution fusion | flops 1096810496 | bytes 26411012 | tf_op jit(solution)/shard_map/while/body/eval_jaxpr/cond/branch_1_fun/kgqr,rkd->kgqd/dot_general | solution.py:41
  246.4 17.8 %conditional.3 = ((f32[8,4,256]{2,1,0:T(4,128)S(1)}, f32[8,4,256]{2,1,0:T(4,128)S(1)}, f32[8,4,256,128]{3,2,1,0:T(8,128)})) conditional(s32[]{:T(128)} %convert_element_type.34, (f32[8,4,256]{2,1,0:T(4,128)S(1)}, f32[8,4,256]{2,1,0:T(4,128)S(1)}, f32[8,4,256,128]{3,2,1,0:T(8,128)}) %tuple.56, (s32[]{:T(128)}, s32[512]{0:T(512)S(1)}, ...), branch_computations={%region_4.4_spmd, %region_5.7_spmd} | conditional | flops 2204516864 | bytes 63971404 | solution.py:49
  246.6 4.3 %fusion.2 = (f32[8,4,256]{2,1,0:T(4,128)S(1)}, f32[8,512,256,4]{2,1,3,0:T(8,128)S(1)}) fusion(pred[256,512]{0,1:T(8,128)(4,1)S(1)} %compare_and_fusion, bf16[256,8,4,128]{3,0,2,1:T(8,128)(2,1)} %get-tuple-element.274, bf16[8192,8,128]{2,0,1:T(8,128)(2,1)} %get-tuple-element.273, s32[]{:T(128)S(6)} %select_n.25), kind=kOutput, calls=%fused_computation.3 | convolution fusion | flops 1086316544 | bytes 20086788 | tf_op jit(solution)/shard_map/while/body/eval_jaxpr/cond/branch_1_fun/qkgd,rkd->kgqr/dot_general | solution.py:33
  251.0 4.3 %fusion.4 = f32[8,4,256]{2,1,0:T(4,128)S(1)} fusion(f32[8,512,256,4]{2,1,3,0:T(8,128)S(1)} %get-tuple-element.358, f32[8,4,256]{2,1,0:T(4,128)S(1)} %max.5, pred[256,512]{0,1:T(8,128)(4,1)S(1)} %compare_and_fusion), kind=kLoop, calls=%fused_computation.5 | loop fusion | flops 20963328 | bytes 16973824 | tf_op jit(solution)/shard_map/while/body/eval_jaxpr/cond/branch_1_fun/reduce_sum | solution.py:40
  255.3 8.9 %multiply_add_fusion = f32[8,4,256,128]{3,2,1,0:T(8,128)} fusion(f32[8,4,256,128]{3,2,1,0:T(8,128)} %get-tuple-element.276, f32[8,4,256]{2,1,0:T(4,128)S(1)} %bitcast.46, f32[8,512,256,4]{2,1,3,0:T(8,128)S(1)} %get-tuple-element.358, f32[8,4,256]{2,1,0:T(4,128)S(1)} %max.5, pred[256,512]{0,1:T(8,128)(4,1)S(1)} %compare_and_fusion, ...), kind=kOutput, calls=%fused_computation.8 | convolution fusion | flops 1096810496 | bytes 26411012 | tf_op jit(solution)/shard_map/while/body/eval_jaxpr/cond/branch_1_fun/kgqr,rkd->kgqd/dot_general | solution.py:41
  265.8 17.8 %conditional.3 = ((f32[8,4,256]{2,1,0:T(4,128)S(1)}, f32[8,4,256]{2,1,0:T(4,128)S(1)}, f32[8,4,256,128]{3,2,1,0:T(8,128)})) conditional(s32[]{:T(128)} %convert_element_type.34, (f32[8,4,256]{2,1,0:T(4,128)S(1)}, f32[8,4,256]{2,1,0:T(4,128)S(1)}, f32[8,4,256,128]{3,2,1,0:T(8,128)}) %tuple.56, (s32[]{:T(128)}, s32[512]{0:T(512)S(1)}, ...), branch_computations={%region_4.4_spmd, %region_5.7_spmd} | conditional | flops 2204516864 | bytes 63971404 | solution.py:49
  266.0 4.3 %fusion.2 = (f32[8,4,256]{2,1,0:T(4,128)S(1)}, f32[8,512,256,4]{2,1,3,0:T(8,128)S(1)}) fusion(pred[256,512]{0,1:T(8,128)(4,1)S(1)} %compare_and_fusion, bf16[256,8,4,128]{3,0,2,1:T(8,128)(2,1)} %get-tuple-element.274, bf16[8192,8,128]{2,0,1:T(8,128)(2,1)} %get-tuple-element.273, s32[]{:T(128)S(6)} %select_n.25), kind=kOutput, calls=%fused_computation.3 | convolution fusion | flops 1086316544 | bytes 20086788 | tf_op jit(solution)/shard_map/while/body/eval_jaxpr/cond/branch_1_fun/qkgd,rkd->kgqr/dot_general | solution.py:33
  270.3 4.3 %fusion.4 = f32[8,4,256]{2,1,0:T(4,128)S(1)} fusion(f32[8,512,256,4]{2,1,3,0:T(8,128)S(1)} %get-tuple-element.358, f32[8,4,256]{2,1,0:T(4,128)S(1)} %max.5, pred[256,512]{0,1:T(8,128)(4,1)S(1)} %compare_and_fusion), kind=kLoop, calls=%fused_computation.5 | loop fusion | flops 20963328 | bytes 16973824 | tf_op jit(solution)/shard_map/while/body/eval_jaxpr/cond/branch_1_fun/reduce_sum | solution.py:40
  274.6 8.9 %multiply_add_fusion = f32[8,4,256,128]{3,2,1,0:T(8,128)} fusion(f32[8,4,256,128]{3,2,1,0:T(8,128)} %get-tuple-element.276, f32[8,4,256]{2,1,0:T(4,128)S(1)} %bitcast.46, f32[8,512,256,4]{2,1,3,0:T(8,128)S(1)} %get-tuple-element.358, f32[8,4,256]{2,1,0:T(4,128)S(1)} %max.5, pred[256,512]{0,1:T(8,128)(4,1)S(1)} %compare_and_fusion, ...), kind=kOutput, calls=%fused_computation.8 | convolution fusion | flops 1096810496 | bytes 26411012 | tf_op jit(solution)/shard_map/while/body/eval_jaxpr/cond/branch_1_fun/kgqr,rkd->kgqd/dot_general | solution.py:41
  285.1 17.8 %conditional.3 = ((f32[8,4,256]{2,1,0:T(4,128)S(1)}, f32[8,4,256]{2,1,0:T(4,128)S(1)}, f32[8,4,256,128]{3,2,1,0:T(8,128)})) conditional(s32[]{:T(128)} %convert_element_type.34, (f32[8,4,256]{2,1,0:T(4,128)S(1)}, f32[8,4,256]{2,1,0:T(4,128)S(1)}, f32[8,4,256,128]{3,2,1,0:T(8,128)}) %tuple.56, (s32[]{:T(128)}, s32[512]{0:T(512)S(1)}, ...), branch_computations={%region_4.4_spmd, %region_5.7_spmd} | conditional | flops 2204516864 | bytes 63971404 | solution.py:49
  285.3 4.3 %fusion.2 = (f32[8,4,256]{2,1,0:T(4,128)S(1)}, f32[8,512,256,4]{2,1,3,0:T(8,128)S(1)}) fusion(pred[256,512]{0,1:T(8,128)(4,1)S(1)} %compare_and_fusion, bf16[256,8,4,128]{3,0,2,1:T(8,128)(2,1)} %get-tuple-element.274, bf16[8192,8,128]{2,0,1:T(8,128)(2,1)} %get-tuple-element.273, s32[]{:T(128)S(6)} %select_n.25), kind=kOutput, calls=%fused_computation.3 | convolution fusion | flops 1086316544 | bytes 20086788 | tf_op jit(solution)/shard_map/while/body/eval_jaxpr/cond/branch_1_fun/qkgd,rkd->kgqr/dot_general | solution.py:33
  289.7 4.3 %fusion.4 = f32[8,4,256]{2,1,0:T(4,128)S(1)} fusion(f32[8,512,256,4]{2,1,3,0:T(8,128)S(1)} %get-tuple-element.358, f32[8,4,256]{2,1,0:T(4,128)S(1)} %max.5, pred[256,512]{0,1:T(8,128)(4,1)S(1)} %compare_and_fusion), kind=kLoop, calls=%fused_computation.5 | loop fusion | flops 20963328 | bytes 16973824 | tf_op jit(solution)/shard_map/while/body/eval_jaxpr/cond/branch_1_fun/reduce_sum | solution.py:40
  294.0 8.9 %multiply_add_fusion = f32[8,4,256,128]{3,2,1,0:T(8,128)} fusion(f32[8,4,256,128]{3,2,1,0:T(8,128)} %get-tuple-element.276, f32[8,4,256]{2,1,0:T(4,128)S(1)} %bitcast.46, f32[8,512,256,4]{2,1,3,0:T(8,128)S(1)} %get-tuple-element.358, f32[8,4,256]{2,1,0:T(4,128)S(1)} %max.5, pred[256,512]{0,1:T(8,128)(4,1)S(1)} %compare_and_fusion, ...), kind=kOutput, calls=%fused_computation.8 | convolution fusion | flops 1096810496 | bytes 26411012 | tf_op jit(solution)/shard_map/while/body/eval_jaxpr/cond/branch_1_fun/kgqr,rkd->kgqd/dot_general | solution.py:41
  304.5 17.8 %conditional.3 = ((f32[8,4,256]{2,1,0:T(4,128)S(1)}, f32[8,4,256]{2,1,0:T(4,128)S(1)}, f32[8,4,256,128]{3,2,1,0:T(8,128)})) conditional(s32[]{:T(128)} %convert_element_type.34, (f32[8,4,256]{2,1,0:T(4,128)S(1)}, f32[8,4,256]{2,1,0:T(4,128)S(1)}, f32[8,4,256,128]{3,2,1,0:T(8,128)}) %tuple.56, (s32[]{:T(128)}, s32[512]{0:T(512)S(1)}, ...), branch_computations={%region_4.4_spmd, %region_5.7_spmd} | conditional | flops 2204516864 | bytes 63971404 | solution.py:49
  304.7 4.3 %fusion.2 = (f32[8,4,256]{2,1,0:T(4,128)S(1)}, f32[8,512,256,4]{2,1,3,0:T(8,128)S(1)}) fusion(pred[256,512]{0,1:T(8,128)(4,1)S(1)} %compare_and_fusion, bf16[256,8,4,128]{3,0,2,1:T(8,128)(2,1)} %get-tuple-element.274, bf16[8192,8,128]{2,0,1:T(8,128)(2,1)} %get-tuple-element.273, s32[]{:T(128)S(6)} %select_n.25), kind=kOutput, calls=%fused_computation.3 | convolution fusion | flops 1086316544 | bytes 20086788 | tf_op jit(solution)/shard_map/while/body/eval_jaxpr/cond/branch_1_fun/qkgd,rkd->kgqr/dot_general | solution.py:33
  309.0 4.3 %fusion.4 = f32[8,4,256]{2,1,0:T(4,128)S(1)} fusion(f32[8,512,256,4]{2,1,3,0:T(8,128)S(1)} %get-tuple-element.358, f32[8,4,256]{2,1,0:T(4,128)S(1)} %max.5, pred[256,512]{0,1:T(8,128)(4,1)S(1)} %compare_and_fusion), kind=kLoop, calls=%fused_computation.5 | loop fusion | flops 20963328 | bytes 16973824 | tf_op jit(solution)/shard_map/while/body/eval_jaxpr/cond/branch_1_fun/reduce_sum | solution.py:40
  313.3 8.9 %multiply_add_fusion = f32[8,4,256,128]{3,2,1,0:T(8,128)} fusion(f32[8,4,256,128]{3,2,1,0:T(8,128)} %get-tuple-element.276, f32[8,4,256]{2,1,0:T(4,128)S(1)} %bitcast.46, f32[8,512,256,4]{2,1,3,0:T(8,128)S(1)} %get-tuple-element.358, f32[8,4,256]{2,1,0:T(4,128)S(1)} %max.5, pred[256,512]{0,1:T(8,128)(4,1)S(1)} %compare_and_fusion, ...), kind=kOutput, calls=%fused_computation.8 | convolution fusion | flops 1096810496 | bytes 26411012 | tf_op jit(solution)/shard_map/while/body/eval_jaxpr/cond/branch_1_fun/kgqr,rkd->kgqd/dot_general | solution.py:41
  323.8 17.8 %conditional.3 = ((f32[8,4,256]{2,1,0:T(4,128)S(1)}, f32[8,4,256]{2,1,0:T(4,128)S(1)}, f32[8,4,256,128]{3,2,1,0:T(8,128)})) conditional(s32[]{:T(128)} %convert_element_type.34, (f32[8,4,256]{2,1,0:T(4,128)S(1)}, f32[8,4,256]{2,1,0:T(4,128)S(1)}, f32[8,4,256,128]{3,2,1,0:T(8,128)}) %tuple.56, (s32[]{:T(128)}, s32[512]{0:T(512)S(1)}, ...), branch_computations={%region_4.4_spmd, %region_5.7_spmd} | conditional | flops 2204516864 | bytes 63971404 | solution.py:49
  324.0 4.3 %fusion.2 = (f32[8,4,256]{2,1,0:T(4,128)S(1)}, f32[8,512,256,4]{2,1,3,0:T(8,128)S(1)}) fusion(pred[256,512]{0,1:T(8,128)(4,1)S(1)} %compare_and_fusion, bf16[256,8,4,128]{3,0,2,1:T(8,128)(2,1)} %get-tuple-element.274, bf16[8192,8,128]{2,0,1:T(8,128)(2,1)} %get-tuple-element.273, s32[]{:T(128)S(6)} %select_n.25), kind=kOutput, calls=%fused_computation.3 | convolution fusion | flops 1086316544 | bytes 20086788 | tf_op jit(solution)/shard_map/while/body/eval_jaxpr/cond/branch_1_fun/qkgd,rkd->kgqr/dot_general | solution.py:33
  328.4 4.3 %fusion.4 = f32[8,4,256]{2,1,0:T(4,128)S(1)} fusion(f32[8,512,256,4]{2,1,3,0:T(8,128)S(1)} %get-tuple-element.358, f32[8,4,256]{2,1,0:T(4,128)S(1)} %max.5, pred[256,512]{0,1:T(8,128)(4,1)S(1)} %compare_and_fusion), kind=kLoop, calls=%fused_computation.5 | loop fusion | flops 20963328 | bytes 16973824 | tf_op jit(solution)/shard_map/while/body/eval_jaxpr/cond/branch_1_fun/reduce_sum | solution.py:40
  332.7 8.9 %multiply_add_fusion = f32[8,4,256,128]{3,2,1,0:T(8,128)} fusion(f32[8,4,256,128]{3,2,1,0:T(8,128)} %get-tuple-element.276, f32[8,4,256]{2,1,0:T(4,128)S(1)} %bitcast.46, f32[8,512,256,4]{2,1,3,0:T(8,128)S(1)} %get-tuple-element.358, f32[8,4,256]{2,1,0:T(4,128)S(1)} %max.5, pred[256,512]{0,1:T(8,128)(4,1)S(1)} %compare_and_fusion, ...), kind=kOutput, calls=%fused_computation.8 | convolution fusion | flops 1096810496 | bytes 26411012 | tf_op jit(solution)/shard_map/while/body/eval_jaxpr/cond/branch_1_fun/kgqr,rkd->kgqd/dot_general | solution.py:41
  343.2 17.8 %conditional.3 = ((f32[8,4,256]{2,1,0:T(4,128)S(1)}, f32[8,4,256]{2,1,0:T(4,128)S(1)}, f32[8,4,256,128]{3,2,1,0:T(8,128)})) conditional(s32[]{:T(128)} %convert_element_type.34, (f32[8,4,256]{2,1,0:T(4,128)S(1)}, f32[8,4,256]{2,1,0:T(4,128)S(1)}, f32[8,4,256,128]{3,2,1,0:T(8,128)}) %tuple.56, (s32[]{:T(128)}, s32[512]{0:T(512)S(1)}, ...), branch_computations={%region_4.4_spmd, %region_5.7_spmd} | conditional | flops 2204516864 | bytes 63971404 | solution.py:49
  343.4 4.3 %fusion.2 = (f32[8,4,256]{2,1,0:T(4,128)S(1)}, f32[8,512,256,4]{2,1,3,0:T(8,128)S(1)}) fusion(pred[256,512]{0,1:T(8,128)(4,1)S(1)} %compare_and_fusion, bf16[256,8,4,128]{3,0,2,1:T(8,128)(2,1)} %get-tuple-element.274, bf16[8192,8,128]{2,0,1:T(8,128)(2,1)} %get-tuple-element.273, s32[]{:T(128)S(6)} %select_n.25), kind=kOutput, calls=%fused_computation.3 | convolution fusion | flops 1086316544 | bytes 20086788 | tf_op jit(solution)/shard_map/while/body/eval_jaxpr/cond/branch_1_fun/qkgd,rkd->kgqr/dot_general | solution.py:33
  347.7 4.3 %fusion.4 = f32[8,4,256]{2,1,0:T(4,128)S(1)} fusion(f32[8,512,256,4]{2,1,3,0:T(8,128)S(1)} %get-tuple-element.358, f32[8,4,256]{2,1,0:T(4,128)S(1)} %max.5, pred[256,512]{0,1:T(8,128)(4,1)S(1)} %compare_and_fusion), kind=kLoop, calls=%fused_computation.5 | loop fusion | flops 20963328 | bytes 16973824 | tf_op jit(solution)/shard_map/while/body/eval_jaxpr/cond/branch_1_fun/reduce_sum | solution.py:40
  352.0 8.9 %multiply_add_fusion = f32[8,4,256,128]{3,2,1,0:T(8,128)} fusion(f32[8,4,256,128]{3,2,1,0:T(8,128)} %get-tuple-element.276, f32[8,4,256]{2,1,0:T(4,128)S(1)} %bitcast.46, f32[8,512,256,4]{2,1,3,0:T(8,128)S(1)} %get-tuple-element.358, f32[8,4,256]{2,1,0:T(4,128)S(1)} %max.5, pred[256,512]{0,1:T(8,128)(4,1)S(1)} %compare_and_fusion, ...), kind=kOutput, calls=%fused_computation.8 | convolution fusion | flops 1096810496 | bytes 26411012 | tf_op jit(solution)/shard_map/while/body/eval_jaxpr/cond/branch_1_fun/kgqr,rkd->kgqd/dot_general | solution.py:41
  362.5 17.8 %conditional.3 = ((f32[8,4,256]{2,1,0:T(4,128)S(1)}, f32[8,4,256]{2,1,0:T(4,128)S(1)}, f32[8,4,256,128]{3,2,1,0:T(8,128)})) conditional(s32[]{:T(128)} %convert_element_type.34, (f32[8,4,256]{2,1,0:T(4,128)S(1)}, f32[8,4,256]{2,1,0:T(4,128)S(1)}, f32[8,4,256,128]{3,2,1,0:T(8,128)}) %tuple.56, (s32[]{:T(128)}, s32[512]{0:T(512)S(1)}, ...), branch_computations={%region_4.4_spmd, %region_5.7_spmd} | conditional | flops 2204516864 | bytes 63971404 | solution.py:49
  362.7 4.3 %fusion.2 = (f32[8,4,256]{2,1,0:T(4,128)S(1)}, f32[8,512,256,4]{2,1,3,0:T(8,128)S(1)}) fusion(pred[256,512]{0,1:T(8,128)(4,1)S(1)} %compare_and_fusion, bf16[256,8,4,128]{3,0,2,1:T(8,128)(2,1)} %get-tuple-element.274, bf16[8192,8,128]{2,0,1:T(8,128)(2,1)} %get-tuple-element.273, s32[]{:T(128)S(6)} %select_n.25), kind=kOutput, calls=%fused_computation.3 | convolution fusion | flops 1086316544 | bytes 20086788 | tf_op jit(solution)/shard_map/while/body/eval_jaxpr/cond/branch_1_fun/qkgd,rkd->kgqr/dot_general | solution.py:33
  367.1 4.3 %fusion.4 = f32[8,4,256]{2,1,0:T(4,128)S(1)} fusion(f32[8,512,256,4]{2,1,3,0:T(8,128)S(1)} %get-tuple-element.358, f32[8,4,256]{2,1,0:T(4,128)S(1)} %max.5, pred[256,512]{0,1:T(8,128)(4,1)S(1)} %compare_and_fusion), kind=kLoop, calls=%fused_computation.5 | loop fusion | flops 20963328 | bytes 16973824 | tf_op jit(solution)/shard_map/while/body/eval_jaxpr/cond/branch_1_fun/reduce_sum | solution.py:40
  371.4 8.9 %multiply_add_fusion = f32[8,4,256,128]{3,2,1,0:T(8,128)} fusion(f32[8,4,256,128]{3,2,1,0:T(8,128)} %get-tuple-element.276, f32[8,4,256]{2,1,0:T(4,128)S(1)} %bitcast.46, f32[8,512,256,4]{2,1,3,0:T(8,128)S(1)} %get-tuple-element.358, f32[8,4,256]{2,1,0:T(4,128)S(1)} %max.5, pred[256,512]{0,1:T(8,128)(4,1)S(1)} %compare_and_fusion, ...), kind=kOutput, calls=%fused_computation.8 | convolution fusion | flops 1096810496 | bytes 26411012 | tf_op jit(solution)/shard_map/while/body/eval_jaxpr/cond/branch_1_fun/kgqr,rkd->kgqd/dot_general | solution.py:41
  385.1 2.9 fusion.20
  389.6 2.8 convert_element_type.24
  (129 shorter events, 20.1 us)
Async XLA Ops:
  6.5 86.1 %all-gather.3.cloned.1.call-start = ((), (), s32[]{:S(2)}) async-start(), calls=%async_computation | async-start | bytes 17301504 | tf_op jit(solution)/shard_map/all_gather | solution.py:82
  8.6 167.4 %all-gather.5.cloned.1.call-start = ((), (), s32[]{:S(2)}) async-start(), calls=%async_computation.1 | async-start | bytes 17301504 | tf_op jit(solution)/shard_map/all_gather | solution.py:83
Sparse Core Ops, SparseCore 0:
  9.5 83.0 all-gather.2
  94.9 81.0 all-gather.4
where the time goes:
time: 402 us; the launch traced here: 399 us
  waiting for transfers between devices  136 us (34%)
  matrix products  119 us (30%)
  local copies, waits for them, and re-layouts  60.1 us (15%)
  other arithmetic  58.8 us (15%)
  between operations  13.4 us (3%)
  loops' own time  11.4 us (3%)
    dot_general x9, matrix products, tile_update(): jnp.einsum('kgqr,rkd->kgqd', weights.astype(jnp.bfloat16), v_tile, prefer...  80.2 us
    all_gather x1, waiting for transfers between devices, per_device(): key_piece = lax.all_gather(keys, 'ctx', axis=0, tiled=True)  74.5 us
    all_gather x1, waiting for transfers between devices, per_device(): value_piece = lax.all_gather(values, 'ctx', axis=0, tiled=True)  61.9 us
    unnamed x6, local copies, waits for them, and re-layouts  52.3 us
    dot_general x9, matrix products, tile_update(): jnp.einsum('qkgd,rkd->kgqr', q_block, k_tile, preferred_element_type=jnp....  38.8 us
    reduce_sum x9, other arithmetic, tile_update(): totals = totals * rescale + jnp.sum(weights, axis=-1)  38.5 us
    reduce_or x16, other arithmetic, visit_tile(): jnp.any(visible)  14.4 us
    another operation x1, loops' own time, per_device(): lax.fori_loop(0, row_count // tile_rows, advance, empty_carry(KVH, q_per_...  10.7 us
  transfers between devices with their start and end apart: 2, of which 2 were waited for; matrix products, arithmetic and copies ran while one was open for 8% of the time, Pallas kernels for 0%

commit v1 on v0

v1 whole, which is shorter than its diff:
```python
import functools
import math

import jax
import jax.numpy as jnp
from jax import lax
from jax.experimental import pallas as pl
from jax.experimental.pallas import tpu as pltpu
from jax.sharding import PartitionSpec as P

H = 32
KVH = 8
DH = 128
QPK = H // KVH
GROUP = QPK * DH

YS = 4
XS = 4
CS = 2

UNIT = 256
TAIL = 512
WIDE = 2048
STACK = 512
MARK = 128.0
NEG_FILL = -1e30
LOG2_SCALE = math.log2(math.e) / math.sqrt(DH)


STEPS = [(dy, dc) for dc in range(CS) for dy in range(YS)]


def ctx_index(y, x, c):
    return ((y % YS) * XS + x % XS) * CS + c % CS


def shift(dy, dx, dc):
    return [
        (ctx_index(y, x, c), ctx_index(y + dy, x + dx, c + dc))
        for y in range(YS)
        for x in range(XS)
        for c in range(CS)
    ]


def head_groups():
    return [[ctx_index(y, x, c) for y in range(YS) for c in range(CS)] for x in range(XS)]


def place(rank):
    return rank >> 3, (rank >> 1) & (XS - 1), rank & (CS - 1)


def group_at(y, c, dy, dc):
    return (((y + dy) & (YS - 1)) << 1) + (c ^ dc)


def split_kernel(rank, queries, keys, values, k_out, v_out, *q_out):
    y, _, c = place(rank[0])
    for h in range(KVH):
        k_out[h] = keys[:, h * DH : (h + 1) * DH]
        v_out[h] = values[:, h * DH : (h + 1) * DH]
    for (dy, dc), out in zip(STEPS, q_out, strict=True):
        column = pl.multiple_of(group_at(y, c, dy, dc) * GROUP, GROUP)
        out[...] = queries[:, pl.ds(column, GROUP)]


def split(rank, queries, keys, values):
    rows = queries.shape[0]
    vmem = pl.BlockSpec(memory_space=pltpu.VMEM)
    by_head = jax.ShapeDtypeStruct((KVH, rows, DH), jnp.bfloat16)
    return pl.pallas_call(
        split_kernel,
        out_shape=[by_head] * 2 + [jax.ShapeDtypeStruct((rows, GROUP), jnp.bfloat16)] * len(STEPS),
        in_specs=[pl.BlockSpec(memory_space=pltpu.SMEM)] + [vmem] * 3,
        out_specs=[vmem] * (2 + len(STEPS)),
    )(rank, queries, keys, values)


def join_kernel(rank, *refs):
    pieces, out, sems = refs[: len(STEPS)], refs[-2], refs[-1]
    y, _, c = place(rank[0])
    copies = []
    for i, (dy, dc) in enumerate(STEPS):
        column = pl.multiple_of(group_at(y, c, dy, dc) * GROUP, GROUP)
        copies.append(
            pltpu.make_async_copy(pieces[i], out.at[:, pl.ds(column, GROUP)], sems.at[i])
        )
    for copy in copies:
        copy.start()
    for copy in copies:
        copy.wait()


def join(rank, pieces):
    vmem = pl.BlockSpec(memory_space=pltpu.VMEM)
    return pl.pallas_call(
        join_kernel,
        out_shape=jax.ShapeDtypeStruct((pieces[0].shape[0], H * DH), jnp.bfloat16),
        in_specs=[pl.BlockSpec(memory_space=pltpu.SMEM)] + [vmem] * len(pieces),
        out_specs=pl.BlockSpec(memory_space=pl.ANY),
        scratch_shapes=[pltpu.SemaphoreType.DMA((len(pieces),))],
    )(rank, *pieces)


def attend_kernel(pieces, dc, rank, doc_lengths, marks, keys, values, *refs):
    q_refs, o_refs = refs[:pieces], refs[pieces : 2 * pieces]
    q_all, o_all, acc, top = refs[2 * pieces :]
    rows = UNIT
    y, x, c = place(rank[0])

    for p in range(pieces):
        for h in range(QPK):
            q_all[p, h * rows : (h + 1) * rows, :DH] = q_refs[p][:, h * DH : (h + 1) * DH]

    def tile(p, start, key_tile, size, hidden):
        at_key = pl.ds(pl.multiple_of(key_tile * UNIT, UNIT), size)
        k_tile = jnp.concatenate([keys[at_key, :], marks[at_key, :]], axis=1)
        v_tile = jnp.concatenate([values[at_key, :], jnp.ones((size, DH), jnp.bfloat16)], axis=1)
        count = QPK * rows // STACK
        stacks = [slice(i * STACK, (i + 1) * STACK) for i in range(count)]

        def multiply(i):
            return lax.dot_general(
                q_all[p, stacks[i], :],
                k_tile,
                (((1,), (1,)), ((), ())),
                preferred_element_type=jnp.float32,
            )

        def weigh(i, scores):
            if hidden:
                ahead = key_tile * UNIT + size - hidden - start
                q_row = lax.broadcasted_iota(jnp.int32, (STACK, hidden), 0) % rows - ahead
                keep = lax.broadcasted_iota(jnp.int32, (STACK, hidden), 1) <= q_row
                last = jnp.where(keep, scores[:, size - hidden :], NEG_FILL)
                if hidden == size:
                    scores = last
                else:
                    scores = jnp.concatenate([scores[:, : size - hidden], last], axis=1)
            old = top[stacks[i], :]
            new = jnp.maximum(old, jnp.max(scores, axis=1, keepdims=True))
            weights = jnp.exp2((scores - jnp.tile(new, (1, size // DH))) * LOG2_SCALE)
            top[stacks[i], :] = new
            return weights.astype(jnp.bfloat16), jnp.exp2((old - new) * LOG2_SCALE)

        def add(i, weights, rescale):
            acc[stacks[i], :] = acc[stacks[i], :] * jnp.tile(rescale, (1, 2)) + jnp.dot(
                weights, v_tile, preferred_element_type=jnp.float32
            )

        coming, ready = multiply(0), None
        for i in range(count):
            scores = coming
            if i + 1 < count:
                coming = multiply(i + 1)
            weighed = weigh(i, scores)
            if ready is not None:
                add(i - 1, *ready)
            ready = weighed
        add(count - 1, *ready)

    @pl.loop(0, pieces)
    def _(p):
        start = ((((y - p) & (YS - 1)) * XS + x) * CS + (c ^ dc)) * rows

        def document(d, so_far):
            first, end = so_far
            after = end + doc_lengths[d]
            return jnp.where(end <= start, end, first), after

        first, _ = lax.fori_loop(0, doc_lengths.shape[0], document, (0, 0), unroll=True)
        lo, hi = first // UNIT, start // UNIT + 1
        mark = marks[pl.ds(pl.multiple_of(start, UNIT), rows), :]
        for h in range(QPK):
            q_all[p, h * rows : (h + 1) * rows, DH:] = mark + mark
        top[...] = jnp.full(top.shape, NEG_FILL, top.dtype)
        acc[...] = jnp.zeros(acc.shape, acc.dtype)

        tail, wide = TAIL // UNIT, WIDE // UNIT
        rest = jnp.maximum(hi - tail - lo, 0)
        odd = rest % tail
        begin = lo + odd
        wides = (rest - odd) // wide
        alone = jnp.where(hi == 1, 1, odd)

        @pl.loop(0, alone)
        def _(t):
            tile(p, start, lo, UNIT, UNIT)

        @pl.loop(0, wides)
        def _(t):
            tile(p, start, begin + t * wide, WIDE, 0)

        @pl.loop(0, (rest - odd - wides * wide) // tail)
        def _(t):
            tile(p, start, begin + wides * wide + t * tail, TAIL, 0)

        @pl.when(hi > 1)
        def _():
            tile(p, start, hi - tail, TAIL, UNIT)

        for h in range(QPK):
            at = slice(h * rows, (h + 1) * rows)
            o_all[p, :, h * DH : (h + 1) * DH] = (acc[at, :DH] / acc[at, DH:]).astype(jnp.bfloat16)

    for p in range(pieces):
        o_refs[p][...] = o_all[p]


def attend(dc, rank, doc_lengths, marks, keys, values, q_pieces):
    pieces = len(q_pieces)
    seq = keys.shape[0]
    vmem = pl.BlockSpec(memory_space=pltpu.VMEM)
    smem = pl.BlockSpec(memory_space=pltpu.SMEM)
    return pl.pallas_call(
        functools.partial(attend_kernel, pieces, dc),
        out_shape=[jax.ShapeDtypeStruct((UNIT, GROUP), jnp.bfloat16)] * pieces,
        in_specs=[smem] * 2 + [vmem] * (3 + pieces),
        out_specs=[vmem] * pieces,
        scratch_shapes=[
            pltpu.VMEM((pieces, QPK * UNIT, 2 * DH), jnp.bfloat16),
            pltpu.VMEM((pieces, UNIT, GROUP), jnp.bfloat16),
            pltpu.VMEM((QPK * UNIT, 2 * DH), jnp.float32),
            pltpu.VMEM((QPK * UNIT, DH), jnp.float32),
        ],
        compiler_params=pltpu.CompilerParams(vmem_limit_bytes=40 * 1024 * 1024),
        cost_estimate=pl.CostEstimate(
            flops=pieces * 4 * QPK * UNIT * seq // 4 * DH,
            bytes_accessed=8 * 1024 * 1024,
            transcendentals=pieces * QPK * UNIT * seq // 4,
        ),
    )(rank, doc_lengths, marks, keys, values, *q_pieces)


def per_device(queries, keys, values, doc_lengths):
    rows = queries.shape[0]
    seq = rows * YS * XS * CS
    run = CS * rows
    rank = lax.axis_index("ctx").astype(jnp.int32)
    y, x, c = place(rank)
    rank = rank[None]

    keys, values, *sent = split(rank, queries, keys, values)
    sent = dict(zip(STEPS, sent, strict=True))

    def to_heads(part):
        return lax.all_to_all(
            part, "ctx", split_axis=0, concat_axis=0, tiled=True, axis_index_groups=head_groups()
        ).reshape(YS, run, DH)

    def along(part, dx):
        return lax.ppermute(part, "ctx", shift(0, dx, 0))

    k_own = to_heads(keys)
    doc_lengths, values, k_own = lax.optimization_barrier((doc_lengths, values, k_own))
    k_left, k_right = along(k_own, 1), along(k_own, XS - 1)
    v_own = to_heads(values)
    v_left, v_right = along(v_own, 1), along(v_own, XS - 1)

    def send(dy, dc):
        part = sent[dy, dc]
        return lax.ppermute(part, "ctx", shift(dy, 0, dc)) if dy or dc else part

    sent, k_left, k_right = lax.optimization_barrier((sent, k_left, k_right))
    got = {(dy, 0): send(dy, 0) for dy in range(YS)}
    k_left, k_right, v_left, v_right = lax.optimization_barrier(
        (k_left, k_right, v_left, v_right)
    )
    k_far, v_far = along(k_left, 1), along(v_right, XS - 1)
    sent, got, k_far, v_far = lax.optimization_barrier((sent, got, k_far, v_far))
    got |= {(dy, 1): send(dy, 1) for dy in range(YS)}

    doc_end = jnp.cumsum(doc_lengths)
    doc_first = doc_end - doc_lengths
    positions = jnp.arange(seq, dtype=jnp.int32)[:, None]
    inside = (doc_first[None, :] <= positions) & (positions < doc_end[None, :])
    marks = jnp.where(inside, MARK, 0.0).astype(jnp.bfloat16)
    marks = jnp.pad(marks, ((0, 0), (0, DH - marks.shape[1])))

    def in_order(own, left, right, far):
        whole = jnp.zeros((YS, XS, run, DH), jnp.bfloat16)
        for part, dx in ((own, 0), (left, XS - 1), (right, 1), (far, 2)):
            at = ((x + dx) & (XS - 1)).astype(jnp.uint32)
            zero = jnp.uint32(0)
            whole = lax.dynamic_update_slice(whole, part[:, None], (zero, at, zero, zero))
        return whole.reshape(seq, DH)

    k_all = in_order(k_own, k_left, k_right, k_far)
    v_all = in_order(v_own, v_left, v_right, v_far)

    outs = []
    for dc in range(CS):
        pieces = [got[dy, dc] for dy in range(YS)]
        done = attend(dc, rank, doc_lengths, marks, k_all, v_all, pieces)
        for dy, piece in enumerate(done):
            if dy or dc:
                piece = lax.ppermute(piece, "ctx", shift(YS - dy, 0, dc))
            outs.append(piece)
    return join(rank, outs)


def solution(mesh):
    placed = (P(("dp", "ctx"), None), P(("dp", "ctx"), None), P(("dp", "ctx"), None), P("dp"))
    return jax.shard_map(
        per_device, mesh=mesh, in_specs=placed, out_specs=P(("dp", "ctx"), None), check_vma=False
    )
```

time: 402 us -> 126 us (0.31)
  the two profiles are of different devices: /device:TPU:25 before, /device:TPU:103 now
where the time goes in v1:
time: 126 us
  waiting for transfers between devices  41.5 us (33%)
  Pallas kernels  37.5 us (30%)
  starting transfers between devices  27.8 us (22%)
  blocking collectives  14.5 us (12%)
  local copies, waits for them, and re-layouts  3.3 us (3%)
    pallas_call x2, Pallas kernels, attend(): pl.pallas_call(functools.partial(attend_kernel, pieces, dc), out_shape=[j...  30.7 us
    ppermute x6, waiting for transfers between devices, along(): return lax.ppermute(part, 'ctx', shift(0, dx, 0))  19.3 us
    all_to_all x1, blocking collectives, to_heads(): lax.all_to_all(part, 'ctx', split_axis=0, concat_axis=0, tiled=True, axis...  14.5 us
    ppermute x7, waiting for transfers between devices, per_device(): piece = lax.ppermute(piece, 'ctx', shift(YS - dy, 0, dc))  14.3 us
    ppermute x7, starting transfers between devices, send(): return lax.ppermute(part, 'ctx', shift(dy, 0, dc)) if dy or dc else part  12.1 us
    all_to_all x1, waiting for transfers between devices, to_heads(): lax.all_to_all(part, 'ctx', split_axis=0, concat_axis=0, tiled=True, axis...  7.78 us
    ppermute x7, starting transfers between devices, per_device(): piece = lax.ppermute(piece, 'ctx', shift(YS - dy, 0, dc))  6.9 us
    all_to_all x1, starting transfers between devices, to_heads(): lax.all_to_all(part, 'ctx', split_axis=0, concat_axis=0, tiled=True, axis...  4.43 us
  transfers between devices with their start and end apart: 21, of which 11 were waited for; matrix products, arithmetic and copies ran while one was open for 2% of the time, Pallas kernels for 24%

profile of v1, /device:TPU:103, one launch (start us, length us, event | category | flops | bytes accessed | tf_op | source)
XLA Modules:
  0.0 126.0 jit_solution(4597073916565367082)
XLA Ops:
  0.0 3.9 %shard_map.46 = (bf16[8,256,128]{2,1,0:T(8,128)(2,1)}, bf16[8,256,128]{2,1,0:T(8,128)(2,1)}, bf16[256,512]{1,0:T(8,128)(2,1)}, bf16[256,512]{1,0:T(8,128)(2,1)},...) custom-call(s32[1]{0:T(128)} %bitcast.rank, ...), custom_call_target="tpu_custom_call" | custom-call | tf_op jit(solution)/shard_map/pallas_call | solution.py:72
  3.9 14.5 %all_to_all.10 = bf16[8,256,128]{2,1,0:T(8,128)(2,1)S(1)} all-to-all(bf16[8,256,128]{2,1,0:T(8,128)(2,1)} %get-tuple-element.51), channel_id=1, replica_groups={{0,1,8,9,16,17,24,25},{2,3,10,11,18,19,26,27},{4,5,12,13,20,21,28,29},{..., dimensions={0} | all-to-all | bytes 1048576 | tf_op jit(solution)/shard_map/all_to_all | solution.py:248
  18.4 4.4 %all-to-all-start.1 = ((bf16[8,256,128]{2,1,0:T(8,128)(2,1)}), bf16[8,256,128]{2,1,0:T(8,128)(2,1)S(1)}, u32[]{:S(2)}, u32[]{:S(2)}) async-start(bf16[8,256,128]{2,1,0:T(8,128)(2,1)} %get-tuple-element.64), calls=%async_computation.1 | async-start | bytes 1048576 | tf_op jit(solution)/shard_map/all_to_all | solution.py:248
  22.8 0.2 collective-permute-start
  23.0 1.3 %collective-permute-start.1 = (bf16[4,512,128]{2,1,0:T(8,128)(2,1)S(1)}, bf16[4,512,128]{2,1,0:T(8,128)(2,1)S(1)}, u32[]{:S(2)}, u32[]{:S(2)}) collective-permute-start(bf16[4,512,128]{2,1,0:T(8,128)(2,1)S(1)} %bitcast.42), channel_id=1, source_target_pairs={{0,6},{1,7},{2,0},{3,1},{4,2},{5,3},{6,4},{7,5},{8,14},{9,15},{10,... | collective-permute-start | bytes 1572872 | tf_op jit(solution)/shard_map/ppermute | solution.py:253
  24.3 0.1 copy.12
  24.4 0.1 reduce
  24.5 7.8 %all-to-all-done.1 = bf16[8,256,128]{2,1,0:T(8,128)(2,1)S(1)} async-done(((bf16[8,256,128]{2,1,0:T(8,128)(2,1)}), bf16[8,256,128]{2,1,0:T(8,128)(2,1)S(1)}, u32[]{:S(2)}, u32[]{:S(2)}) %all-to-all-start.1) | async-done | bytes 524320 | tf_op jit(solution)/shard_map/all_to_all | solution.py:248
  32.3 0.2 collective-permute-start.2
  32.5 1.3 %collective-permute-start.3 = (bf16[4,512,128]{2,1,0:T(8,128)(2,1)S(1)}, bf16[4,512,128]{2,1,0:T(8,128)(2,1)S(1)}, u32[]{:S(2)}, u32[]{:S(2)}) collective-permute-start(bf16[4,512,128]{2,1,0:T(8,128)(2,1)S(1)} %bitcast.39), channel_id=1, source_target_pairs={{0,6},{1,7},{2,0},{3,1},{4,2},{5,3},{6,4},{7,5},{8,14},{9,15},{10,... | collective-permute-start | bytes 1572872 | tf_op jit(solution)/shard_map/ppermute | solution.py:253
  33.8 0.8 select_convert_fusion
  34.6 0.4 pad.4.marks
  35.0 0.4 broadcast.6.clone.1
  35.4 0.1 bitcast_dynamic-update-slice_fusion.4
  35.5 0.4 broadcast.6.clone
  36.0 0.1 collective-permute-done
  36.1 1.1 collective-permute-done.1
  37.3 1.3 %collective-permute-start.4 = (bf16[256,512]{1,0:T(8,128)(2,1)S(1)}, bf16[256,512]{1,0:T(8,128)(2,1)S(1)}, u32[]{:S(2)}, u32[]{:S(2)}) collective-permute-start(bf16[256,512]{1,0:T(8,128)(2,1)S(1)} %copy-done.16), channel_id=1, source_target_pairs={{0,8},{1,9},{2,10},{3,11},{4,12},{5,13},{6,14},{7,15},{8,16},{9,17... | collective-permute-start | bytes 786440 | tf_op jit(solution)/shard_map/ppermute | solution.py:263
  38.5 2.4 %collective-permute-start.5 = (bf16[256,512]{1,0:T(8,128)(2,1)S(1)}, bf16[256,512]{1,0:T(8,128)(2,1)S(1)}, u32[]{:S(2)}, u32[]{:S(2)}) collective-permute-start(bf16[256,512]{1,0:T(8,128)(2,1)S(1)} %copy-done.15), channel_id=1, source_target_pairs={{0,16},{1,17},{2,18},{3,19},{4,20},{5,21},{6,22},{7,23},{8,24},{9,... | collective-permute-start | bytes 786440 | tf_op jit(solution)/shard_map/ppermute | solution.py:263
  40.9 1.2 collective-permute-start.6
  42.1 5.3 %collective-permute-done.2 = bf16[4,512,128]{2,1,0:T(8,128)(2,1)S(1)} collective-permute-done((bf16[4,512,128]{2,1,0:T(8,128)(2,1)S(1)}, bf16[4,512,128]{2,1,0:T(8,128)(2,1)S(1)}, u32[]{:S(2)}, u32[]{:S(2)}) %collective-permute-start.2) | collective-permute-done | bytes 524320 | tf_op jit(solution)/shard_map/ppermute | solution.py:253
  47.4 1.1 collective-permute-done.3
  48.5 0.3 collective-permute-start.7
  48.8 1.1 collective-permute-start.8
  49.9 0.2 bitcast_dynamic-update-slice_fusion.1
  50.2 0.1 bitcast_dynamic-update-slice_fusion.2
  50.3 0.1 collective-permute-done.6.refs_3_
  50.4 10.2 %collective-permute-done.7 = bf16[4,512,128]{2,1,0:T(8,128)(2,1)S(1)} collective-permute-done((bf16[4,512,128]{2,1,0:T(8,128)(2,1)S(1)}, bf16[4,512,128]{2,1,0:T(8,128)(2,1)S(1)}, u32[]{:S(2)}, u32[]{:S(2)}) %collective-permute-start.7) | collective-permute-done | bytes 524320 | tf_op jit(solution)/shard_map/ppermute | solution.py:253
  60.6 1.6 %collective-permute-done.8 = bf16[4,512,128]{2,1,0:T(8,128)(2,1)S(1)} collective-permute-done((bf16[4,512,128]{2,1,0:T(8,128)(2,1)S(1)}, bf16[4,512,128]{2,1,0:T(8,128)(2,1)S(1)}, u32[]{:S(2)}, u32[]{:S(2)}) %collective-permute-start.8) | collective-permute-done | bytes 524320 | tf_op jit(solution)/shard_map/ppermute | solution.py:253
  62.2 2.2 %collective-permute-start.12 = (bf16[256,512]{1,0:T(8,128)(2,1)S(1)}, bf16[256,512]{1,0:T(8,128)(2,1)S(1)}, u32[]{:S(2)}, u32[]{:S(2)}) collective-permute-start(bf16[256,512]{1,0:T(8,128)(2,1)S(1)} %copy-done.13), channel_id=1, source_target_pairs={{0,1},{1,0},{2,3},{3,2},{4,5},{5,4},{6,7},{7,6},{8,9},{9,8},{10,11... | collective-permute-start | bytes 786440 | tf_op jit(solution)/shard_map/ppermute | solution.py:263
  64.4 1.2 collective-permute-start.13
  65.5 2.7 %collective-permute-start.14 = (bf16[256,512]{1,0:T(8,128)(2,1)S(1)}, bf16[256,512]{1,0:T(8,128)(2,1)S(1)}, u32[]{:S(2)}, u32[]{:S(2)}) collective-permute-start(bf16[256,512]{1,0:T(8,128)(2,1)S(1)} %copy-done.11), channel_id=1, source_target_pairs={{0,17},{1,16},{2,19},{3,18},{4,21},{5,20},{6,23},{7,22},{8,25},{9,... | collective-permute-start | bytes 786440 | tf_op jit(solution)/shard_map/ppermute | solution.py:263
  68.3 1.1 collective-permute-start.15
  69.5 16.3 %shard_map.47 = (bf16[256,512]{1,0:T(8,128)(2,1)S(1)}, bf16[256,512]{1,0:T(8,128)(2,1)S(1)}, bf16[256,512]{1,0:T(8,128)(2,1)S(1)}, bf16[256,512]{1,0:T(8,128)(2,1)S(1)}) custom-call(s32[1]{0:T(128)} %bitcast.rank, s32[16]{0:T(128)S(1)} %copy-done.1, bf16[8192,128]{1,0:T(8,128)(2,1)S(1)} %pad.4.marks, bf16[8192,128]{1,0:T(8,128)(2,1)S(1)} %bitcast.35, ...), custom_call_target="tpu_custom_call" | custom-call | flops 4294967296 | bytes 8388608 | tf_op jit(solution)/shard_map/pallas_call | solution.py:216
  85.9 0.7 copy-done
  86.6 0.3 collective-permute-start.10
  86.8 0.4 collective-permute-start.11
  87.2 2.3 %collective-permute-start.9 = (bf16[256,512]{1,0:T(8,128)(2,1)S(1)}, bf16[256,512]{1,0:T(8,128)(2,1)S(1)}, u32[]{:S(2)}, u32[]{:S(2)}) collective-permute-start(bf16[256,512]{1,0:T(8,128)(2,1)S(1)} %get-tuple-element.84), channel_id=1, source_target_pairs={{0,24},{1,25},{2,26},{3,27},{4,28},{5,29},{6,30},{7,31},{8,0},{9,1... | collective-permute-start | bytes 786440 | tf_op jit(solution)/shard_map/ppermute | solution.py:298
  89.5 14.4 %shard_map.48 = (bf16[256,512]{1,0:T(8,128)(2,1)S(1)}, bf16[256,512]{1,0:T(8,128)(2,1)S(1)}, bf16[256,512]{1,0:T(8,128)(2,1)S(1)}, bf16[256,512]{1,0:T(8,128)(2,1)S(1)}) custom-call(s32[1]{0:T(128)} %bitcast.rank, s32[16]{0:T(128)S(1)} %copy-done.1, bf16[8192,128]{1,0:T(8,128)(2,1)S(1)} %pad.4.marks, bf16[8192,128]{1,0:T(8,128)(2,1)S(1)} %bitcast.36, ...), custom_call_target="tpu_custom_call" | custom-call | flops 4294967296 | bytes 8388608 | tf_op jit(solution)/shard_map/pallas_call | solution.py:216
  103.9 1.4 %collective-permute-start.16 = (bf16[256,512]{1,0:T(8,128)(2,1)S(1)}, bf16[256,512]{1,0:T(8,128)(2,1)S(1)}, u32[]{:S(2)}, u32[]{:S(2)}) collective-permute-start(bf16[256,512]{1,0:T(8,128)(2,1)S(1)} %get-tuple-element.91), channel_id=1, source_target_pairs={{0,1},{1,0},{2,3},{3,2},{4,5},{5,4},{6,7},{7,6},{8,9},{9,8},{10,11... | collective-permute-start | bytes 786440 | tf_op jit(solution)/shard_map/ppermute | solution.py:298
  105.3 1.2 collective-permute-start.17
  106.5 0.4 collective-permute-start.18
  106.9 1.0 collective-permute-start.19
  107.9 6.2 %collective-permute-done.17.refs_5_ = bf16[256,512]{1,0:T(8,128)(2,1)S(1)} collective-permute-done((bf16[256,512]{1,0:T(8,128)(2,1)S(1)}, bf16[256,512]{1,0:T(8,128)(2,1)S(1)}, u32[]{:S(2)}, u32[]{:S(2)}) %collective-permute-start.17) | collective-permute-done | bytes 262176 | tf_op jit(solution)/shard_map/ppermute | solution.py:298
  114.2 2.5 %collective-permute-done.18.refs_6_ = bf16[256,512]{1,0:T(8,128)(2,1)S(1)} collective-permute-done((bf16[256,512]{1,0:T(8,128)(2,1)S(1)}, bf16[256,512]{1,0:T(8,128)(2,1)S(1)}, u32[]{:S(2)}, u32[]{:S(2)}) %collective-permute-start.18) | collective-permute-done | bytes 262176 | tf_op jit(solution)/shard_map/ppermute | solution.py:298
  116.6 5.6 %collective-permute-done.19.refs_7_ = bf16[256,512]{1,0:T(8,128)(2,1)S(1)} collective-permute-done((bf16[256,512]{1,0:T(8,128)(2,1)S(1)}, bf16[256,512]{1,0:T(8,128)(2,1)S(1)}, u32[]{:S(2)}, u32[]{:S(2)}) %collective-permute-start.19) | collective-permute-done | bytes 262176 | tf_op jit(solution)/shard_map/ppermute | solution.py:298
  122.3 0.7 copy-done.9
  122.9 2.9 %shard_map.49 = bf16[256,4096]{1,0:T(8,128)(2,1)} custom-call(s32[1]{0:T(128)} %bitcast.rank, bf16[256,512]{1,0:T(8,128)(2,1)} %copy-done, bf16[256,512]{1,0:T(8,128)(2,1)} %copy-done.5, bf16[256,512]{1,0:T(8,128)(2,1)} %copy-done.3, bf16[256,512]{1,0:T(8,128)(2,1)} %copy-done.4, bf16[256,512]{1,0:T(8,128)(2,1)} %copy-done.6, bf16[256,512]{1,0:T(8,128)(2,1)} %copy-done.7, ...), custom_call_target="tpu_custom_call" | custom-call | tf_op jit(solution)/shard_map/pallas_call | solution.py:97
  (48 shorter events, 0.4 us)
Async XLA Ops:
  0.0 24.3 %copy-start.1 = (s32[16]{0:T(128)S(1)}, s32[16]{0:T(128)}, u32[]{:S(2)}) copy-start(s32[16]{0:T(128)} %doc_lengths.1) | copy-start | bytes 196
  18.4 13.9 %all-to-all-start.1 = ((bf16[8,256,128]{2,1,0:T(8,128)(2,1)}), bf16[8,256,128]{2,1,0:T(8,128)(2,1)S(1)}, u32[]{:S(2)}, u32[]{:S(2)}) async-start(bf16[8,256,128]{2,1,0:T(8,128)(2,1)} %get-tuple-element.64), calls=%async_computation.1 | async-start | bytes 1048576 | tf_op jit(solution)/shard_map/all_to_all | solution.py:248
  22.8 13.3 %collective-permute-start = (bf16[4,512,128]{2,1,0:T(8,128)(2,1)S(1)}, bf16[4,512,128]{2,1,0:T(8,128)(2,1)S(1)}, u32[]{:S(2)}, u32[]{:S(2)}) collective-permute-start(bf16[4,512,128]{2,1,0:T(8,128)(2,1)S(1)} %bitcast.41), channel_id=1, source_target_pairs={{0,2},{1,3},{2,4},{3,5},{4,6},{5,7},{6,0},{7,1},{8,10},{9,11},{10,... | collective-permute-start | bytes 1572872 | tf_op jit(solution)/shard_map/ppermute | solution.py:253
  23.0 14.2 %collective-permute-start.1 = (bf16[4,512,128]{2,1,0:T(8,128)(2,1)S(1)}, bf16[4,512,128]{2,1,0:T(8,128)(2,1)S(1)}, u32[]{:S(2)}, u32[]{:S(2)}) collective-permute-start(bf16[4,512,128]{2,1,0:T(8,128)(2,1)S(1)} %bitcast.42), channel_id=1, source_target_pairs={{0,6},{1,7},{2,0},{3,1},{4,2},{5,3},{6,4},{7,5},{8,14},{9,15},{10,... | collective-permute-start | bytes 1572872 | tf_op jit(solution)/shard_map/ppermute | solution.py:253
  32.3 15.1 %collective-permute-start.2 = (bf16[4,512,128]{2,1,0:T(8,128)(2,1)S(1)}, bf16[4,512,128]{2,1,0:T(8,128)(2,1)S(1)}, u32[]{:S(2)}, u32[]{:S(2)}) collective-permute-start(bf16[4,512,128]{2,1,0:T(8,128)(2,1)S(1)} %bitcast.38), channel_id=1, source_target_pairs={{0,2},{1,3},{2,4},{3,5},{4,6},{5,7},{6,0},{7,1},{8,10},{9,11},{10,... | collective-permute-start | bytes 1572872 | tf_op jit(solution)/shard_map/ppermute | solution.py:253
  32.5 16.0 %collective-permute-start.3 = (bf16[4,512,128]{2,1,0:T(8,128)(2,1)S(1)}, bf16[4,512,128]{2,1,0:T(8,128)(2,1)S(1)}, u32[]{:S(2)}, u32[]{:S(2)}) collective-permute-start(bf16[4,512,128]{2,1,0:T(8,128)(2,1)S(1)} %bitcast.39), channel_id=1, source_target_pairs={{0,6},{1,7},{2,0},{3,1},{4,2},{5,3},{6,4},{7,5},{8,14},{9,15},{10,... | collective-permute-start | bytes 1572872 | tf_op jit(solution)/shard_map/ppermute | solution.py:253
  35.4 1.8 %copy-start.16 = (bf16[256,512]{1,0:T(8,128)(2,1)S(1)}, bf16[256,512]{1,0:T(8,128)(2,1)}, u32[]{:S(2)}) copy-start(bf16[256,512]{1,0:T(8,128)(2,1)} %get-tuple-element.68) | copy-start | bytes 786436
  35.4 3.1 %copy-start.15 = (bf16[256,512]{1,0:T(8,128)(2,1)S(1)}, bf16[256,512]{1,0:T(8,128)(2,1)}, u32[]{:S(2)}) copy-start(bf16[256,512]{1,0:T(8,128)(2,1)} %get-tuple-element.70) | copy-start | bytes 786436
  35.4 5.5 %copy-start.14 = (bf16[256,512]{1,0:T(8,128)(2,1)S(1)}, bf16[256,512]{1,0:T(8,128)(2,1)}, u32[]{:S(2)}) copy-start(bf16[256,512]{1,0:T(8,128)(2,1)} %get-tuple-element.72) | copy-start | bytes 786436
  37.2 24.9 %copy-start.13 = (bf16[256,512]{1,0:T(8,128)(2,1)S(1)}, bf16[256,512]{1,0:T(8,128)(2,1)}, u32[]{:S(2)}) copy-start(bf16[256,512]{1,0:T(8,128)(2,1)} %get-tuple-element.87) | copy-start | bytes 786436
  37.2 27.1 %copy-start.12 = (bf16[256,512]{1,0:T(8,128)(2,1)S(1)}, bf16[256,512]{1,0:T(8,128)(2,1)}, u32[]{:S(2)}) copy-start(bf16[256,512]{1,0:T(8,128)(2,1)} %get-tuple-element.88) | copy-start | bytes 786436
  37.2 28.3 %copy-start.11 = (bf16[256,512]{1,0:T(8,128)(2,1)S(1)}, bf16[256,512]{1,0:T(8,128)(2,1)}, u32[]{:S(2)}) copy-start(bf16[256,512]{1,0:T(8,128)(2,1)} %get-tuple-element.89) | copy-start | bytes 786436
  37.2 31.0 %copy-start.10 = (bf16[256,512]{1,0:T(8,128)(2,1)S(1)}, bf16[256,512]{1,0:T(8,128)(2,1)}, u32[]{:S(2)}) copy-start(bf16[256,512]{1,0:T(8,128)(2,1)} %get-tuple-element.90) | copy-start | bytes 786436
  37.3 13.0 %collective-permute-start.4 = (bf16[256,512]{1,0:T(8,128)(2,1)S(1)}, bf16[256,512]{1,0:T(8,128)(2,1)S(1)}, u32[]{:S(2)}, u32[]{:S(2)}) collective-permute-start(bf16[256,512]{1,0:T(8,128)(2,1)S(1)} %copy-done.16), channel_id=1, source_target_pairs={{0,8},{1,9},{2,10},{3,11},{4,12},{5,13},{6,14},{7,15},{8,16},{9,17... | collective-permute-start | bytes 786440 | tf_op jit(solution)/shard_map/ppermute | solution.py:263
  38.5 11.8 %collective-permute-start.5 = (bf16[256,512]{1,0:T(8,128)(2,1)S(1)}, bf16[256,512]{1,0:T(8,128)(2,1)S(1)}, u32[]{:S(2)}, u32[]{:S(2)}) collective-permute-start(bf16[256,512]{1,0:T(8,128)(2,1)S(1)} %copy-done.15), channel_id=1, source_target_pairs={{0,16},{1,17},{2,18},{3,19},{4,20},{5,21},{6,22},{7,23},{8,24},{9,... | collective-permute-start | bytes 786440 | tf_op jit(solution)/shard_map/ppermute | solution.py:263
  40.9 9.5 %collective-permute-start.6 = (bf16[256,512]{1,0:T(8,128)(2,1)S(1)}, bf16[256,512]{1,0:T(8,128)(2,1)S(1)}, u32[]{:S(2)}, u32[]{:S(2)}) collective-permute-start(bf16[256,512]{1,0:T(8,128)(2,1)S(1)} %copy-done.14), channel_id=1, source_target_pairs={{0,24},{1,25},{2,26},{3,27},{4,28},{5,29},{6,30},{7,31},{8,0},{9,1... | collective-permute-start | bytes 786440 | tf_op jit(solution)/shard_map/ppermute | solution.py:263
  48.5 12.1 %collective-permute-start.7 = (bf16[4,512,128]{2,1,0:T(8,128)(2,1)S(1)}, bf16[4,512,128]{2,1,0:T(8,128)(2,1)S(1)}, u32[]{:S(2)}, u32[]{:S(2)}) collective-permute-start(bf16[4,512,128]{2,1,0:T(8,128)(2,1)S(1)} %collective-permute-done), channel_id=1, source_target_pairs={{0,2},{1,3},{2,4},{3,5},{4,6},{5,7},{6,0},{7,1},{8,10},{9,11},{10,... | collective-permute-start | bytes 1572872 | tf_op jit(solution)/shard_map/ppermute | solution.py:253
  48.8 13.4 %collective-permute-start.8 = (bf16[4,512,128]{2,1,0:T(8,128)(2,1)S(1)}, bf16[4,512,128]{2,1,0:T(8,128)(2,1)S(1)}, u32[]{:S(2)}, u32[]{:S(2)}) collective-permute-start(bf16[4,512,128]{2,1,0:T(8,128)(2,1)S(1)} %collective-permute-done.3), channel_id=1, source_target_pairs={{0,6},{1,7},{2,0},{3,1},{4,2},{5,3},{6,4},{7,5},{8,14},{9,15},{10,... | collective-permute-start | bytes 1572872 | tf_op jit(solution)/shard_map/ppermute | solution.py:253
  50.1 19.4 %copy-start.2 = (bf16[256,512]{1,0:T(8,128)(2,1)S(1)}, bf16[256,512]{1,0:T(8,128)(2,1)}, u32[]{:S(2)}) copy-start(bf16[256,512]{1,0:T(8,128)(2,1)} %get-tuple-element.79.refs_0_) | copy-start | bytes 786436
  62.2 24.7 %collective-permute-start.12 = (bf16[256,512]{1,0:T(8,128)(2,1)S(1)}, bf16[256,512]{1,0:T(8,128)(2,1)S(1)}, u32[]{:S(2)}, u32[]{:S(2)}) collective-permute-start(bf16[256,512]{1,0:T(8,128)(2,1)S(1)} %copy-done.13), channel_id=1, source_target_pairs={{0,1},{1,0},{2,3},{3,2},{4,5},{5,4},{6,7},{7,6},{8,9},{9,8},{10,11... | collective-permute-start | bytes 786440 | tf_op jit(solution)/shard_map/ppermute | solution.py:263
  64.4 22.8 %collective-permute-start.13 = (bf16[256,512]{1,0:T(8,128)(2,1)S(1)}, bf16[256,512]{1,0:T(8,128)(2,1)S(1)}, u32[]{:S(2)}, u32[]{:S(2)}) collective-permute-start(bf16[256,512]{1,0:T(8,128)(2,1)S(1)} %copy-done.12), channel_id=1, source_target_pairs={{0,9},{1,8},{2,11},{3,10},{4,13},{5,12},{6,15},{7,14},{8,17},{9,16... | collective-permute-start | bytes 786440 | tf_op jit(solution)/shard_map/ppermute | solution.py:263
  65.5 24.0 %collective-permute-start.14 = (bf16[256,512]{1,0:T(8,128)(2,1)S(1)}, bf16[256,512]{1,0:T(8,128)(2,1)S(1)}, u32[]{:S(2)}, u32[]{:S(2)}) collective-permute-start(bf16[256,512]{1,0:T(8,128)(2,1)S(1)} %copy-done.11), channel_id=1, source_target_pairs={{0,17},{1,16},{2,19},{3,18},{4,21},{5,20},{6,23},{7,22},{8,25},{9,... | collective-permute-start | bytes 786440 | tf_op jit(solution)/shard_map/ppermute | solution.py:263
  68.3 21.3 %collective-permute-start.15 = (bf16[256,512]{1,0:T(8,128)(2,1)S(1)}, bf16[256,512]{1,0:T(8,128)(2,1)S(1)}, u32[]{:S(2)}, u32[]{:S(2)}) collective-permute-start(bf16[256,512]{1,0:T(8,128)(2,1)S(1)} %copy-done.10), channel_id=1, source_target_pairs={{0,25},{1,24},{2,27},{3,26},{4,29},{5,28},{6,31},{7,30},{8,1},{9,0... | collective-permute-start | bytes 786440 | tf_op jit(solution)/shard_map/ppermute | solution.py:263
  85.9 0.7 copy-start
  86.6 19.9 %collective-permute-start.10 = (bf16[256,512]{1,0:T(8,128)(2,1)S(1)}, bf16[256,512]{1,0:T(8,128)(2,1)S(1)}, u32[]{:S(2)}, u32[]{:S(2)}) collective-permute-start(bf16[256,512]{1,0:T(8,128)(2,1)S(1)} %get-tuple-element.85), channel_id=1, source_target_pairs={{0,16},{1,17},{2,18},{3,19},{4,20},{5,21},{6,22},{7,23},{8,24},{9,... | collective-permute-start | bytes 786440 | tf_op jit(solution)/shard_map/ppermute | solution.py:298
  86.8 20.0 %collective-permute-start.11 = (bf16[256,512]{1,0:T(8,128)(2,1)S(1)}, bf16[256,512]{1,0:T(8,128)(2,1)S(1)}, u32[]{:S(2)}, u32[]{:S(2)}) collective-permute-start(bf16[256,512]{1,0:T(8,128)(2,1)S(1)} %get-tuple-element.86), channel_id=1, source_target_pairs={{0,8},{1,9},{2,10},{3,11},{4,12},{5,13},{6,14},{7,15},{8,16},{9,17... | collective-permute-start | bytes 786440 | tf_op jit(solution)/shard_map/ppermute | solution.py:298
  87.2 20.7 %collective-permute-start.9 = (bf16[256,512]{1,0:T(8,128)(2,1)S(1)}, bf16[256,512]{1,0:T(8,128)(2,1)S(1)}, u32[]{:S(2)}, u32[]{:S(2)}) collective-permute-start(bf16[256,512]{1,0:T(8,128)(2,1)S(1)} %get-tuple-element.84), channel_id=1, source_target_pairs={{0,24},{1,25},{2,26},{3,27},{4,28},{5,29},{6,30},{7,31},{8,0},{9,1... | collective-permute-start | bytes 786440 | tf_op jit(solution)/shard_map/ppermute | solution.py:298
  103.9 4.0 %collective-permute-start.16 = (bf16[256,512]{1,0:T(8,128)(2,1)S(1)}, bf16[256,512]{1,0:T(8,128)(2,1)S(1)}, u32[]{:S(2)}, u32[]{:S(2)}) collective-permute-start(bf16[256,512]{1,0:T(8,128)(2,1)S(1)} %get-tuple-element.91), channel_id=1, source_target_pairs={{0,1},{1,0},{2,3},{3,2},{4,5},{5,4},{6,7},{7,6},{8,9},{9,8},{10,11... | collective-permute-start | bytes 786440 | tf_op jit(solution)/shard_map/ppermute | solution.py:298
  105.3 8.9 %collective-permute-start.17 = (bf16[256,512]{1,0:T(8,128)(2,1)S(1)}, bf16[256,512]{1,0:T(8,128)(2,1)S(1)}, u32[]{:S(2)}, u32[]{:S(2)}) collective-permute-start(bf16[256,512]{1,0:T(8,128)(2,1)S(1)} %get-tuple-element.92), channel_id=1, source_target_pairs={{0,25},{1,24},{2,27},{3,26},{4,29},{5,28},{6,31},{7,30},{8,1},{9,0... | collective-permute-start | bytes 786440 | tf_op jit(solution)/shard_map/ppermute | solution.py:298
  106.5 15.8 %copy-start.3 = (bf16[256,512]{1,0:T(8,128)(2,1)}, bf16[256,512]{1,0:T(8,128)(2,1)S(1)}, u32[]{:S(2)}) copy-start(bf16[256,512]{1,0:T(8,128)(2,1)S(1)} %collective-permute-done.10.refs_2_) | copy-start | bytes 786436
  106.5 10.2 %collective-permute-start.18 = (bf16[256,512]{1,0:T(8,128)(2,1)S(1)}, bf16[256,512]{1,0:T(8,128)(2,1)S(1)}, u32[]{:S(2)}, u32[]{:S(2)}) collective-permute-start(bf16[256,512]{1,0:T(8,128)(2,1)S(1)} %get-tuple-element.93), channel_id=1, source_target_pairs={{0,17},{1,16},{2,19},{3,18},{4,21},{5,20},{6,23},{7,22},{8,25},{9,... | collective-permute-start | bytes 786440 | tf_op jit(solution)/shard_map/ppermute | solution.py:298
  106.9 15.4 %copy-start.4 = (bf16[256,512]{1,0:T(8,128)(2,1)}, bf16[256,512]{1,0:T(8,128)(2,1)S(1)}, u32[]{:S(2)}) copy-start(bf16[256,512]{1,0:T(8,128)(2,1)S(1)} %collective-permute-done.11.refs_3_) | copy-start | bytes 786436
  106.9 15.4 %collective-permute-start.19 = (bf16[256,512]{1,0:T(8,128)(2,1)S(1)}, bf16[256,512]{1,0:T(8,128)(2,1)S(1)}, u32[]{:S(2)}, u32[]{:S(2)}) collective-permute-start(bf16[256,512]{1,0:T(8,128)(2,1)S(1)} %get-tuple-element.94), channel_id=1, source_target_pairs={{0,9},{1,8},{2,11},{3,10},{4,13},{5,12},{6,15},{7,14},{8,17},{9,16... | collective-permute-start | bytes 786440 | tf_op jit(solution)/shard_map/ppermute | solution.py:298
  107.9 14.3 %copy-start.5 = (bf16[256,512]{1,0:T(8,128)(2,1)}, bf16[256,512]{1,0:T(8,128)(2,1)S(1)}, u32[]{:S(2)}) copy-start(bf16[256,512]{1,0:T(8,128)(2,1)S(1)} %collective-permute-done.9.refs_1_) | copy-start | bytes 786436
  107.9 14.3 %copy-start.6 = (bf16[256,512]{1,0:T(8,128)(2,1)}, bf16[256,512]{1,0:T(8,128)(2,1)S(1)}, u32[]{:S(2)}) copy-start(bf16[256,512]{1,0:T(8,128)(2,1)S(1)} %collective-permute-done.16.refs_4_) | copy-start | bytes 786436
  114.1 8.1 %copy-start.7 = (bf16[256,512]{1,0:T(8,128)(2,1)}, bf16[256,512]{1,0:T(8,128)(2,1)S(1)}, u32[]{:S(2)}) copy-start(bf16[256,512]{1,0:T(8,128)(2,1)S(1)} %collective-permute-done.17.refs_5_) | copy-start | bytes 786436
  116.6 5.6 %copy-start.8 = (bf16[256,512]{1,0:T(8,128)(2,1)}, bf16[256,512]{1,0:T(8,128)(2,1)S(1)}, u32[]{:S(2)}) copy-start(bf16[256,512]{1,0:T(8,128)(2,1)S(1)} %collective-permute-done.18.refs_6_) | copy-start | bytes 786436
  122.2 0.7 copy-start.9

commit v2 on v1

v2 whole, which is shorter than its diff:
```python
import functools
import math

import jax
import jax.numpy as jnp
from jax import lax
from jax.experimental import pallas as pl
from jax.experimental.pallas import tpu as pltpu
from jax.sharding import PartitionSpec as P

H = 32
KVH = 8
DH = 128
QPK = H // KVH
GROUP = QPK * DH

YS = 4
XS = 4
CS = 2

UNIT = 256
TAIL = 512
WIDE = 2048
STACK = 512
MARK = 128.0
NEG_FILL = -1e30
LOG2_SCALE = math.log2(math.e) / math.sqrt(DH)


FAR = ((2, 0, YS // 2), (2, YS // 2, YS // 2))
PARTS = {"near": ((0, 0, YS), (XS - 1, 0, YS), (1, 0, YS)), "far": FAR}
PARTS["all"] = PARTS["near"] + FAR
STEPS = [(dy, dc) for dc in range(CS) for dy in range(YS)]


def ctx_index(y, x, c):
    return ((y % YS) * XS + x % XS) * CS + c % CS


def shift(dy, dx, dc):
    return [
        (ctx_index(y, x, c), ctx_index(y + dy, x + dx, c + dc))
        for y in range(YS)
        for x in range(XS)
        for c in range(CS)
    ]


def head_groups():
    return [[ctx_index(y, x, c) for y in range(YS) for c in range(CS)] for x in range(XS)]


def place(rank):
    return rank >> 3, (rank >> 1) & (XS - 1), rank & (CS - 1)


def group_at(y, c, dy, dc):
    return (((y + dy) & (YS - 1)) << 1) + (c ^ dc)


def vmem_call(kernel, out_shape, rank, *arrays):
    vmem = pl.BlockSpec(memory_space=pltpu.VMEM)
    return pl.pallas_call(
        kernel,
        out_shape=out_shape,
        in_specs=[pl.BlockSpec(memory_space=pltpu.SMEM)] + [vmem] * len(arrays),
        out_specs=[vmem] * len(out_shape),
    )(rank, *arrays)


def split_kernel(_, keys, values, out):
    for h in range(KVH):
        out[h, 0] = keys[:, h * DH : (h + 1) * DH]
        out[h, 1] = values[:, h * DH : (h + 1) * DH]


def query_kernel(rank, queries, *out):
    y, _, c = place(rank[0])
    for (dy, dc), part in zip(STEPS, out, strict=True):
        column = pl.multiple_of(group_at(y, c, dy, dc) * GROUP, GROUP)
        part[...] = queries[:, pl.ds(column, GROUP)]


def attend_kernel(pieces, dc, which, rank, doc_lengths, marks, *refs):
    parts = PARTS[which]
    part_refs, refs = refs[: len(parts)], refs[len(parts) :]
    q_refs, refs = refs[:pieces], refs[pieces:]
    if which == "far":
        acc_in, top_in, *refs = refs
    if which == "near":
        acc_out, top_out, *refs = refs
    else:
        o_refs, refs = refs[:pieces], refs[pieces:]
    q_all, o_all, acc, top, keys, values, *refs = refs
    rows = UNIT
    y, x, c = place(rank[0])

    for (dx, first_y, ys), part in zip(parts, part_refs, strict=True):
        at_x = (x + dx) & (XS - 1)
        for i in range(ys):
            for core in range(CS):
                block = first_y + i if which == "far" else (first_y + i) * XS + at_x
                at = pl.ds(pl.multiple_of((block * CS + core) * rows, rows), rows)
                keys[at, :] = part[i, core, 0]
                values[at, :] = part[i, core, 1]
    if which == "near":
        (near_marks,) = refs
        near_marks[...] = marks[...]
        for i in range(YS):
            at = pl.multiple_of((i * XS + ((x + 2) & (XS - 1))) * TAIL, TAIL)
            for whole in (near_marks, keys, values):
                whole[pl.ds(at, TAIL), :] = jnp.zeros((TAIL, DH), jnp.bfloat16)
        marks = near_marks

    for p in range(pieces):
        for h in range(QPK):
            q_all[p, h * rows : (h + 1) * rows, :DH] = q_refs[p][:, h * DH : (h + 1) * DH]

    def tile(p, start, first_key, size, hidden, at_row=None):
        at_key = pl.ds(pl.multiple_of(first_key if at_row is None else at_row, UNIT), size)
        at_mark = pl.ds(pl.multiple_of(first_key, UNIT), size)
        k_tile = jnp.concatenate([keys[at_key, :], marks[at_mark, :]], axis=1)
        v_tile = jnp.concatenate([values[at_key, :], jnp.ones((size, DH), jnp.bfloat16)], axis=1)
        count = QPK * rows // STACK
        stacks = [slice(i * STACK, (i + 1) * STACK) for i in range(count)]

        def multiply(i):
            return lax.dot_general(
                q_all[p, stacks[i], :],
                k_tile,
                (((1,), (1,)), ((), ())),
                preferred_element_type=jnp.float32,
            )

        def weigh(i, scores):
            if hidden:
                ahead = first_key + size - hidden - start
                q_row = lax.broadcasted_iota(jnp.int32, (STACK, hidden), 0) % rows - ahead
                keep = lax.broadcasted_iota(jnp.int32, (STACK, hidden), 1) <= q_row
                last = jnp.where(keep, scores[:, size - hidden :], NEG_FILL)
                if hidden == size:
                    scores = last
                else:
                    scores = jnp.concatenate([scores[:, : size - hidden], last], axis=1)
            old = top[stacks[i], :]
            new = jnp.maximum(old, jnp.max(scores, axis=1, keepdims=True))
            weights = jnp.exp2((scores - jnp.tile(new, (1, size // DH))) * LOG2_SCALE)
            top[stacks[i], :] = new
            return weights.astype(jnp.bfloat16), jnp.exp2((old - new) * LOG2_SCALE)

        def add(i, weights, rescale):
            acc[stacks[i], :] = acc[stacks[i], :] * jnp.tile(rescale, (1, 2)) + jnp.dot(
                weights, v_tile, preferred_element_type=jnp.float32
            )

        coming, ready = multiply(0), None
        for i in range(count):
            scores = coming
            if i + 1 < count:
                coming = multiply(i + 1)
            weighed = weigh(i, scores)
            if ready is not None:
                add(i - 1, *ready)
            ready = weighed
        add(count - 1, *ready)

    @pl.loop(0, pieces)
    def _(p):
        start = ((((y - p) & (YS - 1)) * XS + x) * CS + (c ^ dc)) * rows

        def document(d, so_far):
            first, end = so_far
            after = end + doc_lengths[d]
            return jnp.where(end <= start, end, first), after

        first, _ = lax.fori_loop(0, doc_lengths.shape[0], document, (0, 0), unroll=True)
        mark = marks[pl.ds(pl.multiple_of(start, UNIT), rows), :]
        for h in range(QPK):
            q_all[p, h * rows : (h + 1) * rows, DH:] = mark + mark

        if which == "far":
            top[...] = top_in[p]
            acc[...] = acc_in[p]

            @pl.loop(0, YS)
            def _(at_y):
                key = (at_y * XS + ((x + 2) & (XS - 1))) * TAIL

                @pl.when((key < start) & (key + TAIL > first))
                def _():
                    tile(p, start, key, TAIL, 0, at_y * TAIL)

        else:
            top[...] = jnp.full(top.shape, NEG_FILL, top.dtype)
            acc[...] = jnp.zeros(acc.shape, acc.dtype)

            lo, hi = first // UNIT, start // UNIT + 1
            tail, wide = TAIL // UNIT, WIDE // UNIT
            rest = jnp.maximum(hi - tail - lo, 0)
            odd = rest % tail
            begin = lo + odd
            wides = (rest - odd) // wide
            alone = jnp.where(hi == 1, 1, odd)

            @pl.loop(0, alone)
            def _(t):
                tile(p, start, lo * UNIT, UNIT, UNIT)

            @pl.loop(0, wides)
            def _(t):
                tile(p, start, (begin + t * wide) * UNIT, WIDE, 0)

            @pl.loop(0, (rest - odd - wides * wide) // tail)
            def _(t):
                tile(p, start, (begin + wides * wide + t * tail) * UNIT, TAIL, 0)

            @pl.when(hi > 1)
            def _():
                tile(p, start, (hi - tail) * UNIT, TAIL, UNIT)

        if which == "near":
            acc_out[p] = acc[...]
            top_out[p] = top[...]
        else:
            for h in range(QPK):
                at = slice(h * rows, (h + 1) * rows)
                result = acc[at, :DH] / acc[at, DH:]
                o_all[p, :, h * DH : (h + 1) * DH] = result.astype(jnp.bfloat16)

    if which != "near":
        for p in range(pieces):
            o_refs[p][...] = o_all[p]


def attend(dc, which, rank, doc_lengths, marks, parts, q_pieces, state=()):
    pieces = len(q_pieces)
    seq = marks.shape[0]
    held = seq // XS if which == "far" else seq
    stacked = QPK * UNIT
    vmem = pl.BlockSpec(memory_space=pltpu.VMEM)
    smem = pl.BlockSpec(memory_space=pltpu.SMEM)
    if which == "near":
        out_shape = [
            jax.ShapeDtypeStruct((pieces, stacked, 2 * DH), jnp.float32),
            jax.ShapeDtypeStruct((pieces, stacked, DH), jnp.float32),
        ]
    else:
        out_shape = [jax.ShapeDtypeStruct((UNIT, GROUP), jnp.bfloat16)] * pieces
    return pl.pallas_call(
        functools.partial(attend_kernel, pieces, dc, which),
        out_shape=out_shape,
        in_specs=[smem] * 2 + [vmem] * (1 + len(parts) + pieces + len(state)),
        out_specs=[vmem] * len(out_shape),
        scratch_shapes=[
            pltpu.VMEM((pieces, stacked, 2 * DH), jnp.bfloat16),
            pltpu.VMEM((pieces, UNIT, GROUP), jnp.bfloat16),
            pltpu.VMEM((stacked, 2 * DH), jnp.float32),
            pltpu.VMEM((stacked, DH), jnp.float32),
            pltpu.VMEM((held, DH), jnp.bfloat16),
            pltpu.VMEM((held, DH), jnp.bfloat16),
        ]
        + [pltpu.VMEM((seq, DH), jnp.bfloat16)] * (which == "near"),
        compiler_params=pltpu.CompilerParams(vmem_limit_bytes=32 * 1024 * 1024),
        cost_estimate=pl.CostEstimate(
            flops=pieces * 4 * stacked * seq // 4 * DH,
            bytes_accessed=8 * 1024 * 1024,
            transcendentals=pieces * stacked * seq // 4,
        ),
    )(rank, doc_lengths, marks, *parts, *q_pieces, *state)


def per_device(queries, keys, values, doc_lengths):
    rows = queries.shape[0]
    seq = rows * YS * XS * CS
    rank = lax.axis_index("ctx").astype(jnp.int32)
    y, x, c = place(rank)
    rank = rank[None]

    by_head = jax.ShapeDtypeStruct((KVH, 2, rows, DH), jnp.bfloat16)
    (pairs,) = vmem_call(split_kernel, [by_head], rank, keys, values)
    own = lax.all_to_all(
        pairs, "ctx", split_axis=0, concat_axis=0, tiled=True, axis_index_groups=head_groups()
    ).reshape(YS, CS, 2, rows, DH)
    doc_lengths, queries, own = lax.optimization_barrier((doc_lengths, queries, own))

    def along(part, dx):
        return lax.ppermute(part, "ctx", shift(0, dx, 0))

    left, right = along(own, 1), along(own, XS - 1)

    by_device = jax.ShapeDtypeStruct((rows, GROUP), jnp.bfloat16)
    sent = vmem_call(query_kernel, [by_device] * len(STEPS), rank, queries)
    sent = dict(zip(STEPS, sent, strict=True))

    def send(dy, dc):
        part = sent[dy, dc]
        return lax.ppermute(part, "ctx", shift(dy, 0, dc)) if dy or dc else part

    got = {(dy, 0): send(dy, 0) for dy in range(YS)}
    sent, got = lax.optimization_barrier((sent, got))
    got |= {(dy, 1): send(dy, 1) for dy in range(1, YS)}
    half = YS // 2
    far = (along(left[:half], 1), along(right[half:], XS - 1))

    doc_end = jnp.cumsum(doc_lengths)
    doc_first = doc_end - doc_lengths
    positions = jnp.arange(seq, dtype=jnp.int32)[:, None]
    inside = (doc_first[None, :] <= positions) & (positions < doc_end[None, :])
    marks = jnp.where(inside, MARK, 0.0).astype(jnp.bfloat16)
    marks = jnp.pad(marks, ((0, 0), (0, DH - marks.shape[1])))

    near = (own, left, right)
    pieces = [got[dy, 0] for dy in range(YS)]
    state = attend(0, "near", rank, doc_lengths, marks, near, pieces)
    sent, state = lax.optimization_barrier((sent, state))
    got[0, 1] = send(0, 1)
    done = attend(0, "far", rank, doc_lengths, marks, far, pieces, state)

    def give(done, dc):
        return [
            lax.ppermute(piece, "ctx", shift(YS - dy, 0, dc)) if dy or dc else piece
            for dy, piece in enumerate(done)
        ]

    done, got = lax.optimization_barrier((done, got))
    outs = give(done, 0)
    pieces = [got[dy, 1] for dy in range(YS)]
    done = attend(1, "all", rank, doc_lengths, marks, near + far, pieces)
    done, outs = lax.optimization_barrier((done, outs))
    outs += give(done, 1)

    whole = jnp.zeros((rows, H * DH), jnp.bfloat16)
    for (dy, dc), piece in zip(STEPS, outs, strict=True):
        column = group_at(y, c, dy, dc) * GROUP
        whole = lax.dynamic_update_slice(
            whole, piece, (0, column), allow_negative_indices=False
        )
    return whole


def solution(mesh):
    placed = (P(("dp", "ctx"), None), P(("dp", "ctx"), None), P(("dp", "ctx"), None), P("dp"))
    return jax.shard_map(
        per_device, mesh=mesh, in_specs=placed, out_specs=P(("dp", "ctx"), None), check_vma=False
    )
```

time: 126 us -> 118 us (0.937)
  waiting for transfers between devices: 41.5 us -> 30.4 us
  starting transfers between devices: 27.8 us -> 21.1 us
  blocking collectives: 14.5 us -> 20.3 us
  Pallas kernels: 37.5 us -> 41.5 us
    all_to_all x1 -> x0, waiting for transfers between devices: 7.78 us -> none  [to_heads(): lax.all_to_all(part, 'ctx', split_axis=0, concat_axis=0, tiled=True, axis...]
    all_to_all x1, blocking collectives: 14.5 us -> 20.3 us  [per_device(): lax.all_to_all(pairs, 'ctx', split_axis=0, concat_axis=0, tiled=True, axi...]
    all_to_all x1 -> x0, starting transfers between devices: 4.43 us -> none  [to_heads(): lax.all_to_all(part, 'ctx', split_axis=0, concat_axis=0, tiled=True, axis...]
    pallas_call x4 -> x5, Pallas kernels: 37.5 us -> 41.5 us  [the longest x3 36.1 us: attend(): pl.pallas_call(functools.partial(attend_kernel, pieces, dc, which), out_s...]
    ppermute x6 -> x4, waiting for transfers between devices: 19.3 us -> 16.2 us  [along(): return lax.ppermute(part, 'ctx', shift(0, dx, 0))]
    ppermute x6 -> x4, starting transfers between devices: 4.4 us -> 3.07 us  [along(): return lax.ppermute(part, 'ctx', shift(0, dx, 0))]
  transfers between devices with their start and end apart: 21 -> 18, of which waited for: 11 -> 3; matrix products, arithmetic and copies ran while one was open for 2% -> 2% of each run, Pallas kernels for 24% -> 33%
where the time goes in v2:
time: 118 us; the launch traced here: 117 us
  Pallas kernels  41.5 us (35%)
  waiting for transfers between devices  30.4 us (26%)
  starting transfers between devices  21.1 us (18%)
  blocking collectives  20.3 us (17%)
  local copies, waits for them, and re-layouts  2.19 us (2%)
    pallas_call x3, Pallas kernels, attend(): pl.pallas_call(functools.partial(attend_kernel, pieces, dc, which), out_s...  36.1 us
    all_to_all x1, blocking collectives, per_device(): lax.all_to_all(pairs, 'ctx', split_axis=0, concat_axis=0, tiled=True, axi...  20.3 us
    ppermute x4, waiting for transfers between devices, along(): return lax.ppermute(part, 'ctx', shift(0, dx, 0))  16.2 us
    ppermute x7, waiting for transfers between devices, give(): lax.ppermute(piece, 'ctx', shift(YS - dy, 0, dc))  14.3 us
    ppermute x7, starting transfers between devices, send(): return lax.ppermute(part, 'ctx', shift(dy, 0, dc)) if dy or dc else part  11.2 us
    ppermute x7, starting transfers between devices, give(): lax.ppermute(piece, 'ctx', shift(YS - dy, 0, dc))  6.82 us
    pallas_call x2, Pallas kernels, vmem_call(): pl.pallas_call(kernel, out_shape=out_shape, in_specs=[pl.BlockSpec(memory...  5.41 us
    ppermute x4, starting transfers between devices, along(): return lax.ppermute(part, 'ctx', shift(0, dx, 0))  3.07 us
  transfers between devices with their start and end apart: 18, of which 3 were waited for; matrix products, arithmetic and copies ran while one was open for 2% of the time, Pallas kernels for 33%

profile of v2, /device:TPU:103, one launch (start us, length us, event | category | flops | bytes accessed | tf_op | source)
XLA Modules:
  0.0 116.8 jit_solution(3425317220507200470)
XLA Ops:
  0.0 2.4 %shard_map.46 = bf16[8,2,256,128]{3,2,1,0:T(8,128)(2,1)} custom-call(s32[1]{0:T(128)} %bitcast._.rank, bf16[256,1024]{1,0:T(8,128)(2,1)} %keys.1, bf16[256,1024]{1,0:T(8,128)(2,1)} %values.1), custom_call_target="tpu_custom_call" | custom-call | tf_op jit(solution)/shard_map/pallas_call | solution.py:63
  2.4 20.3 %all_to_all.5 = bf16[8,2,256,128]{3,2,1,0:T(8,128)(2,1)S(1)} all-to-all(bf16[8,2,256,128]{3,2,1,0:T(8,128)(2,1)} %shard_map.46), channel_id=1, replica_groups={{0,1,8,9,16,17,24,25},{2,3,10,11,18,19,26,27},{4,5,12,13,20,21,28,29},{..., dimensions={0} | all-to-all | bytes 2097152 | tf_op jit(solution)/shard_map/all_to_all | solution.py:281
  22.7 0.2 collective-permute-start
  22.9 1.3 %collective-permute-start.1 = (bf16[4,2,2,256,128]{4,3,2,1,0:T(8,128)(2,1)S(1)}, bf16[4,2,2,256,128]{4,3,2,1,0:T(8,128)(2,1)S(1)}, u32[]{:S(2)}, u32[]{:S(2)}) collective-permute-start(bf16[4,2,2,256,128]{4,3,2,1,0:T(8,128)(2,1)S(1)} %bitcast.4), channel_id=1, source_target_pairs={{0,6},{1,7},{2,0},{3,1},{4,2},{5,3},{6,4},{7,5},{8,14},{9,15},{10,... | collective-permute-start | bytes 3145736 | tf_op jit(solution)/shard_map/ppermute | solution.py:287
  24.2 3.1 %shard_map.47 = (bf16[256,512]{1,0:T(8,128)(2,1)}, bf16[256,512]{1,0:T(8,128)(2,1)}, bf16[256,512]{1,0:T(8,128)(2,1)}, bf16[256,512]{1,0:T(8,128)(2,1)}, bf16[25...) custom-call(s32[1]{0:T(128)} %bitcast._.rank, ...), custom_call_target="tpu_custom_call" | custom-call | tf_op jit(solution)/shard_map/pallas_call | solution.py:63
  27.2 0.3 collective-permute-start.4
  27.5 1.8 %collective-permute-start.5 = (bf16[256,512]{1,0:T(8,128)(2,1)}, bf16[256,512]{1,0:T(8,128)(2,1)}, u32[]{:S(2)}, u32[]{:S(2)}) collective-permute-start(bf16[256,512]{1,0:T(8,128)(2,1)} %get-tuple-element.59), channel_id=1, source_target_pairs={{0,16},{1,17},{2,18},{3,19},{4,20},{5,21},{6,22},{7,23},{8,24},{9,... | collective-permute-start | bytes 786440 | tf_op jit(solution)/shard_map/ppermute | solution.py:297
  29.3 0.6 collective-permute-start.6
  29.9 0.1 copy.6
  30.0 0.1 reduce
  30.1 16.2 %collective-permute-done.refs_1_ = bf16[4,2,2,256,128]{4,3,2,1,0:T(8,128)(2,1)S(1)} collective-permute-done((bf16[4,2,2,256,128]{4,3,2,1,0:T(8,128)(2,1)S(1)}, bf16[4,2,2,256,128]{4,3,2,1,0:T(8,128)(2,1)S(1)}, u32[]{:S(2)}, u32[]{:S(2)}) %collective-permute-start) | collective-permute-done | bytes 1048608 | tf_op jit(solution)/shard_map/ppermute | solution.py:287
  46.3 1.5 %collective-permute-start.2 = (bf16[2,2,2,256,128]{4,3,2,1,0:T(8,128)(2,1)S(1)}, bf16[2,2,2,256,128]{4,3,2,1,0:T(8,128)(2,1)S(1)}, u32[]{:S(2)}, u32[]{:S(2)}) collective-permute-start(bf16[2,2,2,256,128]{4,3,2,1,0:T(8,128)(2,1)S(1)} %slice.8), channel_id=1, source_target_pairs={{0,2},{1,3},{2,4},{3,5},{4,6},{5,7},{6,0},{7,1},{8,10},{9,11},{10,... | collective-permute-start | bytes 1572872 | tf_op jit(solution)/shard_map/ppermute | solution.py:287
  47.8 0.0 collective-permute-done.1.refs_2_
  47.9 0.1 collective-permute-start.3
  48.0 0.8 select_convert_fusion
  48.8 0.0 copy-start.1
  48.8 0.4 pad.4.marks
  49.3 0.0 collective-permute-done.4.refs_4_.refs_3_
  49.3 0.0 collective-permute-done.5.refs_5_.refs_4_
  49.3 0.0 collective-permute-done.6.refs_6_.refs_5_
  49.3 0.5 copy-done.6
  49.8 3.3 %collective-permute-start.10 = (bf16[256,512]{1,0:T(8,128)(2,1)S(1)}, bf16[256,512]{1,0:T(8,128)(2,1)S(1)}, u32[]{:S(2)}, u32[]{:S(2)}) collective-permute-start(bf16[256,512]{1,0:T(8,128)(2,1)S(1)} %copy-done.6), channel_id=1, source_target_pairs={{0,25},{1,24},{2,27},{3,26},{4,29},{5,28},{6,31},{7,30},{8,1},{9,0... | collective-permute-start | bytes 786440 | tf_op jit(solution)/shard_map/ppermute | solution.py:297
  53.1 0.0 collective-permute-start.8
  53.1 1.4 %collective-permute-start.9 = (bf16[256,512]{1,0:T(8,128)(2,1)S(1)}, bf16[256,512]{1,0:T(8,128)(2,1)S(1)}, u32[]{:S(2)}, u32[]{:S(2)}) collective-permute-start(bf16[256,512]{1,0:T(8,128)(2,1)S(1)} %copy-done.4), channel_id=1, source_target_pairs={{0,17},{1,16},{2,19},{3,18},{4,21},{5,20},{6,23},{7,22},{8,25},{9,... | collective-permute-start | bytes 786440 | tf_op jit(solution)/shard_map/ppermute | solution.py:297
  54.5 14.1 %shard_map.48 = (f32[4,1024,256]{2,1,0:T(8,128)S(1)}, f32[4,1024,128]{2,1,0:T(8,128)S(1)}) custom-call(s32[1]{0:T(128)} %bitcast._.rank, s32[16]{0:T(128)S(1)} %copy-done, bf16[8192,128]{1,0:T(8,128)(2,1)S(1)} %pad.4.marks, bf16[4,2,2,256,128]{4,3,2,1,0:T(8,128)(2,1)S(1)} %bitcast.5, bf16[4,2,2,256,128]{4,3,2,1,0:T(8,128)(2,1)S(1)} %collective-permute-done.refs_1_, ...), custom_call_target="tpu_custom_call" | custom-call | flops 4294967296 | bytes 8388608 | tf_op jit(solution)/shard_map/pallas_call | solution.py:249
  68.6 0.0 collective-permute-done.2.refs_0_.refs_3_
  68.6 3.9 %collective-permute-start.7 = (bf16[256,512]{1,0:T(8,128)(2,1)S(1)}, bf16[256,512]{1,0:T(8,128)(2,1)S(1)}, u32[]{:S(2)}, u32[]{:S(2)}) collective-permute-start(bf16[256,512]{1,0:T(8,128)(2,1)S(1)} %copy-done.3), channel_id=1, source_target_pairs={{0,1},{1,0},{2,3},{3,2},{4,5},{5,4},{6,7},{7,6},{8,9},{9,8},{10,11... | collective-permute-start | bytes 786440 | tf_op jit(solution)/shard_map/ppermute | solution.py:297
  72.5 0.0 collective-permute-done.3.refs_1_.refs_4_
  72.5 5.2 %shard_map.49 = (bf16[256,512]{1,0:T(8,128)(2,1)S(1)}, bf16[256,512]{1,0:T(8,128)(2,1)S(1)}, bf16[256,512]{1,0:T(8,128)(2,1)S(1)}, bf16[256,512]{1,0:T(8,128)(2,1)S(1)}) custom-call(s32[1]{0:T(128)} %bitcast._.rank, s32[16]{0:T(128)S(1)} %copy-done, bf16[8192,128]{1,0:T(8,128)(2,1)S(1)} %pad.4.marks, ...), custom_call_target="tpu_custom_call" | custom-call | flops 4294967296 | bytes 8388608 | tf_op jit(solution)/shard_map/pallas_call | solution.py:249
  77.8 0.0 collective-permute-done.8.refs_6_
  77.8 0.0 collective-permute-done.9.refs_7_
  77.8 1.9 %collective-permute-start.11 = (bf16[256,512]{1,0:T(8,128)(2,1)S(1)}, bf16[256,512]{1,0:T(8,128)(2,1)S(1)}, u32[]{:S(2)}, u32[]{:S(2)}) collective-permute-start(bf16[256,512]{1,0:T(8,128)(2,1)S(1)} %get-tuple-element.90), channel_id=1, source_target_pairs={{0,24},{1,25},{2,26},{3,27},{4,28},{5,29},{6,30},{7,31},{8,0},{9,1... | collective-permute-start | bytes 786440 | tf_op jit(solution)/shard_map/ppermute | solution.py:321
  79.7 1.2 %collective-permute-start.12 = (bf16[256,512]{1,0:T(8,128)(2,1)S(1)}, bf16[256,512]{1,0:T(8,128)(2,1)S(1)}, u32[]{:S(2)}, u32[]{:S(2)}) collective-permute-start(bf16[256,512]{1,0:T(8,128)(2,1)S(1)} %get-tuple-element.91), channel_id=1, source_target_pairs={{0,16},{1,17},{2,18},{3,19},{4,20},{5,21},{6,22},{7,23},{8,24},{9,... | collective-permute-start | bytes 786440 | tf_op jit(solution)/shard_map/ppermute | solution.py:321
  80.8 0.0 collective-permute-start.13
  80.8 16.7 %shard_map.50 = (bf16[256,512]{1,0:T(8,128)(2,1)S(1)}, bf16[256,512]{1,0:T(8,128)(2,1)S(1)}, bf16[256,512]{1,0:T(8,128)(2,1)S(1)}, bf16[256,512]{1,0:T(8,128)(2,1)S(1)}) custom-call(s32[1]{0:T(128)} %bitcast._.rank, s32[16]{0:T(128)S(1)} %copy-done, bf16[8192,128]{1,0:T(8,128)(2,1)S(1)} %pad.4.marks, bf16[4,2,2,256,128]{4,3,2,1,0:T(8,128)(2,1)S(1)} %bitcast.6, ...), custom_call_target="tpu_custom_call" | custom-call | flops 4294967296 | bytes 8388608 | tf_op jit(solution)/shard_map/pallas_call | solution.py:249
  97.5 0.0 collective-permute-done.11
  97.5 0.0 collective-permute-done.13
  97.5 0.1 collective-permute-start.14
  97.6 3.1 %collective-permute-start.15 = (bf16[256,512]{1,0:T(8,128)(2,1)S(1)}, bf16[256,512]{1,0:T(8,128)(2,1)S(1)}, u32[]{:S(2)}, u32[]{:S(2)}) collective-permute-start(bf16[256,512]{1,0:T(8,128)(2,1)S(1)} %get-tuple-element.98), channel_id=1, source_target_pairs={{0,25},{1,24},{2,27},{3,26},{4,29},{5,28},{6,31},{7,30},{8,1},{9,0... | collective-permute-start | bytes 786440 | tf_op jit(solution)/shard_map/ppermute | solution.py:321
  100.7 0.6 collective-permute-start.16
  101.2 0.1 collective-permute-start.17
  101.3 0.2 broadcast_in_dim.17
  101.7 0.0 collective-permute-done.14
  101.7 10.3 %collective-permute-done.15 = bf16[256,512]{1,0:T(8,128)(2,1)S(1)} collective-permute-done((bf16[256,512]{1,0:T(8,128)(2,1)S(1)}, bf16[256,512]{1,0:T(8,128)(2,1)S(1)}, u32[]{:S(2)}, u32[]{:S(2)}) %collective-permute-start.15) | collective-permute-done | bytes 262176 | tf_op jit(solution)/shard_map/ppermute | solution.py:321
  112.1 0.0 collective-permute-done.16
  112.1 0.0 copy-start.2
  112.1 4.0 %collective-permute-done.17 = bf16[256,512]{1,0:T(8,128)(2,1)S(1)} collective-permute-done((bf16[256,512]{1,0:T(8,128)(2,1)S(1)}, bf16[256,512]{1,0:T(8,128)(2,1)S(1)}, u32[]{:S(2)}, u32[]{:S(2)}) %collective-permute-start.17) | collective-permute-done | bytes 262176 | tf_op jit(solution)/shard_map/ppermute | solution.py:321
  116.1 0.7 constant_dynamic-update-slice_fusion
  (25 shorter events, 0.3 us)
Async XLA Ops:
  2.4 27.5 %copy-start = (s32[16]{0:T(128)S(1)}, s32[16]{0:T(128)}, u32[]{:S(2)}) copy-start(s32[16]{0:T(128)} %doc_lengths.2) | copy-start | bytes 196
  22.7 23.6 %collective-permute-start = (bf16[4,2,2,256,128]{4,3,2,1,0:T(8,128)(2,1)S(1)}, bf16[4,2,2,256,128]{4,3,2,1,0:T(8,128)(2,1)S(1)}, u32[]{:S(2)}, u32[]{:S(2)}) collective-permute-start(bf16[4,2,2,256,128]{4,3,2,1,0:T(8,128)(2,1)S(1)} %bitcast.3), channel_id=1, source_target_pairs={{0,2},{1,3},{2,4},{3,5},{4,6},{5,7},{6,0},{7,1},{8,10},{9,11},{10,... | collective-permute-start | bytes 3145736 | tf_op jit(solution)/shard_map/ppermute | solution.py:287
  22.9 24.9 %collective-permute-start.1 = (bf16[4,2,2,256,128]{4,3,2,1,0:T(8,128)(2,1)S(1)}, bf16[4,2,2,256,128]{4,3,2,1,0:T(8,128)(2,1)S(1)}, u32[]{:S(2)}, u32[]{:S(2)}) collective-permute-start(bf16[4,2,2,256,128]{4,3,2,1,0:T(8,128)(2,1)S(1)} %bitcast.4), channel_id=1, source_target_pairs={{0,6},{1,7},{2,0},{3,1},{4,2},{5,3},{6,4},{7,5},{8,14},{9,15},{10,... | collective-permute-start | bytes 3145736 | tf_op jit(solution)/shard_map/ppermute | solution.py:287
  27.2 22.1 %collective-permute-start.4 = (bf16[256,512]{1,0:T(8,128)(2,1)}, bf16[256,512]{1,0:T(8,128)(2,1)S(1)}, u32[]{:S(2)}, u32[]{:S(2)}) collective-permute-start(bf16[256,512]{1,0:T(8,128)(2,1)} %get-tuple-element.57), channel_id=1, source_target_pairs={{0,8},{1,9},{2,10},{3,11},{4,12},{5,13},{6,14},{7,15},{8,16},{9,17... | collective-permute-start | bytes 786440 | tf_op jit(solution)/shard_map/ppermute | solution.py:297
  27.5 21.8 %collective-permute-start.5 = (bf16[256,512]{1,0:T(8,128)(2,1)}, bf16[256,512]{1,0:T(8,128)(2,1)}, u32[]{:S(2)}, u32[]{:S(2)}) collective-permute-start(bf16[256,512]{1,0:T(8,128)(2,1)} %get-tuple-element.59), channel_id=1, source_target_pairs={{0,16},{1,17},{2,18},{3,19},{4,20},{5,21},{6,22},{7,23},{8,24},{9,... | collective-permute-start | bytes 786440 | tf_op jit(solution)/shard_map/ppermute | solution.py:297
  29.3 20.0 %collective-permute-start.6 = (bf16[256,512]{1,0:T(8,128)(2,1)}, bf16[256,512]{1,0:T(8,128)(2,1)}, u32[]{:S(2)}, u32[]{:S(2)}) collective-permute-start(bf16[256,512]{1,0:T(8,128)(2,1)} %get-tuple-element.61), channel_id=1, source_target_pairs={{0,24},{1,25},{2,26},{3,27},{4,28},{5,29},{6,30},{7,31},{8,0},{9,1... | collective-permute-start | bytes 786440 | tf_op jit(solution)/shard_map/ppermute | solution.py:297
  46.3 22.3 %collective-permute-start.2 = (bf16[2,2,2,256,128]{4,3,2,1,0:T(8,128)(2,1)S(1)}, bf16[2,2,2,256,128]{4,3,2,1,0:T(8,128)(2,1)S(1)}, u32[]{:S(2)}, u32[]{:S(2)}) collective-permute-start(bf16[2,2,2,256,128]{4,3,2,1,0:T(8,128)(2,1)S(1)} %slice.8), channel_id=1, source_target_pairs={{0,2},{1,3},{2,4},{3,5},{4,6},{5,7},{6,0},{7,1},{8,10},{9,11},{10,... | collective-permute-start | bytes 1572872 | tf_op jit(solution)/shard_map/ppermute | solution.py:287
  47.9 24.6 %collective-permute-start.3 = (bf16[2,2,2,256,128]{4,3,2,1,0:T(8,128)(2,1)S(1)}, bf16[2,2,2,256,128]{4,3,2,1,0:T(8,128)(2,1)S(1)}, u32[]{:S(2)}, u32[]{:S(2)}) collective-permute-start(bf16[2,2,2,256,128]{4,3,2,1,0:T(8,128)(2,1)S(1)} %slice.9), channel_id=1, source_target_pairs={{0,6},{1,7},{2,0},{3,1},{4,2},{5,3},{6,4},{7,5},{8,14},{9,15},{10,... | collective-permute-start | bytes 1572872 | tf_op jit(solution)/shard_map/ppermute | solution.py:287
  48.8 1.0 copy-start.6
  48.8 4.2 %copy-start.5 = (bf16[256,512]{1,0:T(8,128)(2,1)S(1)}, bf16[256,512]{1,0:T(8,128)(2,1)}, u32[]{:S(2)}) copy-start(bf16[256,512]{1,0:T(8,128)(2,1)} %get-tuple-element.69) | copy-start | bytes 786436
  48.8 4.2 %copy-start.4 = (bf16[256,512]{1,0:T(8,128)(2,1)S(1)}, bf16[256,512]{1,0:T(8,128)(2,1)}, u32[]{:S(2)}) copy-start(bf16[256,512]{1,0:T(8,128)(2,1)} %get-tuple-element.70) | copy-start | bytes 786436
  48.8 5.6 %copy-start.1 = (bf16[256,512]{1,0:T(8,128)(2,1)S(1)}, bf16[256,512]{1,0:T(8,128)(2,1)}, u32[]{:S(2)}) copy-start(bf16[256,512]{1,0:T(8,128)(2,1)} %get-tuple-element.64.refs_3_.refs_2_) | copy-start | bytes 786436
  49.8 18.9 %copy-start.3 = (bf16[256,512]{1,0:T(8,128)(2,1)S(1)}, bf16[256,512]{1,0:T(8,128)(2,1)}, u32[]{:S(2)}) copy-start(bf16[256,512]{1,0:T(8,128)(2,1)} %get-tuple-element.80) | copy-start | bytes 786436
  49.8 28.0 %collective-permute-start.10 = (bf16[256,512]{1,0:T(8,128)(2,1)S(1)}, bf16[256,512]{1,0:T(8,128)(2,1)S(1)}, u32[]{:S(2)}, u32[]{:S(2)}) collective-permute-start(bf16[256,512]{1,0:T(8,128)(2,1)S(1)} %copy-done.6), channel_id=1, source_target_pairs={{0,25},{1,24},{2,27},{3,26},{4,29},{5,28},{6,31},{7,30},{8,1},{9,0... | collective-permute-start | bytes 786440 | tf_op jit(solution)/shard_map/ppermute | solution.py:297
  53.1 24.7 %collective-permute-start.8 = (bf16[256,512]{1,0:T(8,128)(2,1)S(1)}, bf16[256,512]{1,0:T(8,128)(2,1)S(1)}, u32[]{:S(2)}, u32[]{:S(2)}) collective-permute-start(bf16[256,512]{1,0:T(8,128)(2,1)S(1)} %copy-done.5), channel_id=1, source_target_pairs={{0,9},{1,8},{2,11},{3,10},{4,13},{5,12},{6,15},{7,14},{8,17},{9,16... | collective-permute-start | bytes 786440 | tf_op jit(solution)/shard_map/ppermute | solution.py:297
  53.1 24.7 %collective-permute-start.9 = (bf16[256,512]{1,0:T(8,128)(2,1)S(1)}, bf16[256,512]{1,0:T(8,128)(2,1)S(1)}, u32[]{:S(2)}, u32[]{:S(2)}) collective-permute-start(bf16[256,512]{1,0:T(8,128)(2,1)S(1)} %copy-done.4), channel_id=1, source_target_pairs={{0,17},{1,16},{2,19},{3,18},{4,21},{5,20},{6,23},{7,22},{8,25},{9,... | collective-permute-start | bytes 786440 | tf_op jit(solution)/shard_map/ppermute | solution.py:297
  68.6 9.2 %collective-permute-start.7 = (bf16[256,512]{1,0:T(8,128)(2,1)S(1)}, bf16[256,512]{1,0:T(8,128)(2,1)S(1)}, u32[]{:S(2)}, u32[]{:S(2)}) collective-permute-start(bf16[256,512]{1,0:T(8,128)(2,1)S(1)} %copy-done.3), channel_id=1, source_target_pairs={{0,1},{1,0},{2,3},{3,2},{4,5},{5,4},{6,7},{7,6},{8,9},{9,8},{10,11... | collective-permute-start | bytes 786440 | tf_op jit(solution)/shard_map/ppermute | solution.py:297
  77.8 19.7 %collective-permute-start.11 = (bf16[256,512]{1,0:T(8,128)(2,1)S(1)}, bf16[256,512]{1,0:T(8,128)(2,1)S(1)}, u32[]{:S(2)}, u32[]{:S(2)}) collective-permute-start(bf16[256,512]{1,0:T(8,128)(2,1)S(1)} %get-tuple-element.90), channel_id=1, source_target_pairs={{0,24},{1,25},{2,26},{3,27},{4,28},{5,29},{6,30},{7,31},{8,0},{9,1... | collective-permute-start | bytes 786440 | tf_op jit(solution)/shard_map/ppermute | solution.py:321
  79.7 17.9 %collective-permute-start.12 = (bf16[256,512]{1,0:T(8,128)(2,1)S(1)}, bf16[256,512]{1,0:T(8,128)(2,1)S(1)}, u32[]{:S(2)}, u32[]{:S(2)}) collective-permute-start(bf16[256,512]{1,0:T(8,128)(2,1)S(1)} %get-tuple-element.91), channel_id=1, source_target_pairs={{0,16},{1,17},{2,18},{3,19},{4,20},{5,21},{6,22},{7,23},{8,24},{9,... | collective-permute-start | bytes 786440 | tf_op jit(solution)/shard_map/ppermute | solution.py:321
  80.8 16.7 %collective-permute-start.13 = (bf16[256,512]{1,0:T(8,128)(2,1)S(1)}, bf16[256,512]{1,0:T(8,128)(2,1)S(1)}, u32[]{:S(2)}, u32[]{:S(2)}) collective-permute-start(bf16[256,512]{1,0:T(8,128)(2,1)S(1)} %get-tuple-element.92), channel_id=1, source_target_pairs={{0,8},{1,9},{2,10},{3,11},{4,12},{5,13},{6,14},{7,15},{8,16},{9,17... | collective-permute-start | bytes 786440 | tf_op jit(solution)/shard_map/ppermute | solution.py:321
  97.5 4.2 %collective-permute-start.14 = (bf16[256,512]{1,0:T(8,128)(2,1)S(1)}, bf16[256,512]{1,0:T(8,128)(2,1)S(1)}, u32[]{:S(2)}, u32[]{:S(2)}) collective-permute-start(bf16[256,512]{1,0:T(8,128)(2,1)S(1)} %get-tuple-element.97), channel_id=1, source_target_pairs={{0,1},{1,0},{2,3},{3,2},{4,5},{5,4},{6,7},{7,6},{8,9},{9,8},{10,11... | collective-permute-start | bytes 786440 | tf_op jit(solution)/shard_map/ppermute | solution.py:321
  97.6 14.4 %collective-permute-start.15 = (bf16[256,512]{1,0:T(8,128)(2,1)S(1)}, bf16[256,512]{1,0:T(8,128)(2,1)S(1)}, u32[]{:S(2)}, u32[]{:S(2)}) collective-permute-start(bf16[256,512]{1,0:T(8,128)(2,1)S(1)} %get-tuple-element.98), channel_id=1, source_target_pairs={{0,25},{1,24},{2,27},{3,26},{4,29},{5,28},{6,31},{7,30},{8,1},{9,0... | collective-permute-start | bytes 786440 | tf_op jit(solution)/shard_map/ppermute | solution.py:321
  100.7 11.4 %collective-permute-start.16 = (bf16[256,512]{1,0:T(8,128)(2,1)S(1)}, bf16[256,512]{1,0:T(8,128)(2,1)S(1)}, u32[]{:S(2)}, u32[]{:S(2)}) collective-permute-start(bf16[256,512]{1,0:T(8,128)(2,1)S(1)} %get-tuple-element.99), channel_id=1, source_target_pairs={{0,17},{1,16},{2,19},{3,18},{4,21},{5,20},{6,23},{7,22},{8,25},{9,... | collective-permute-start | bytes 786440 | tf_op jit(solution)/shard_map/ppermute | solution.py:321
  101.2 14.8 %collective-permute-start.17 = (bf16[256,512]{1,0:T(8,128)(2,1)S(1)}, bf16[256,512]{1,0:T(8,128)(2,1)S(1)}, u32[]{:S(2)}, u32[]{:S(2)}) collective-permute-start(bf16[256,512]{1,0:T(8,128)(2,1)S(1)} %get-tuple-element.100), channel_id=1, source_target_pairs={{0,9},{1,8},{2,11},{3,10},{4,13},{5,12},{6,15},{7,14},{8,17},{9,16... | collective-permute-start | bytes 786440 | tf_op jit(solution)/shard_map/ppermute | solution.py:321
  112.1 4.0 %copy-start.2 = (bf16[256,4096]{1,0:T(8,128)(2,1)}, bf16[256,4096]{1,0:T(8,128)(2,1)S(1)}, u32[]{:S(2)}) copy-start(bf16[256,4096]{1,0:T(8,128)(2,1)S(1)} %constant_dynamic-update-slice_fusion.1) | copy-start | bytes 6291460

commit v3 on v2

--- a/solution.py
+++ b/solution.py
@@ -23,6 +23,7 @@
 WIDE = 2048
 STACK = 512
 MARK = 128.0
+NEAR_RUN = 3
 NEG_FILL = -1e30
 LOG2_SCALE = math.log2(math.e) / math.sqrt(DH)
 
@@ -58,25 +59,26 @@
     return (((y + dy) & (YS - 1)) << 1) + (c ^ dc)
 
 
-def vmem_call(kernel, out_shape, rank, *arrays):
+def vmem_call(kernel, out_shape, scalars, *arrays):
+    smem = pl.BlockSpec(memory_space=pltpu.SMEM)
     vmem = pl.BlockSpec(memory_space=pltpu.VMEM)
     return pl.pallas_call(
         kernel,
         out_shape=out_shape,
-        in_specs=[pl.BlockSpec(memory_space=pltpu.SMEM)] + [vmem] * len(arrays),
+        in_specs=[smem] * len(scalars) + [vmem] * len(arrays),
         out_specs=[vmem] * len(out_shape),
-    )(rank, *arrays)
-
-
-def split_kernel(_, keys, values, out):
+    )(*scalars, *arrays)
+
+
+def split_kernel(keys, values, out):
     for h in range(KVH):
         out[h, 0] = keys[:, h * DH : (h + 1) * DH]
         out[h, 1] = values[:, h * DH : (h + 1) * DH]
 
 
-def query_kernel(rank, queries, *out):
+def query_kernel(rank, queries, *parts):
     y, _, c = place(rank[0])
-    for (dy, dc), part in zip(STEPS, out, strict=True):
+    for (dy, dc), part in zip(STEPS, parts, strict=True):
         column = pl.multiple_of(group_at(y, c, dy, dc) * GROUP, GROUP)
         part[...] = queries[:, pl.ds(column, GROUP)]
 
@@ -91,7 +93,7 @@
         acc_out, top_out, *refs = refs
     else:
         o_refs, refs = refs[:pieces], refs[pieces:]
-    q_all, o_all, acc, top, keys, values, *refs = refs
+    q_all, o_all, acc, top, keys, values = refs
     rows = UNIT
     y, x, c = place(rank[0])
 
@@ -103,23 +105,19 @@
                 at = pl.ds(pl.multiple_of((block * CS + core) * rows, rows), rows)
                 keys[at, :] = part[i, core, 0]
                 values[at, :] = part[i, core, 1]
-    if which == "near":
-        (near_marks,) = refs
-        near_marks[...] = marks[...]
-        for i in range(YS):
-            at = pl.multiple_of((i * XS + ((x + 2) & (XS - 1))) * TAIL, TAIL)
-            for whole in (near_marks, keys, values):
-                whole[pl.ds(at, TAIL), :] = jnp.zeros((TAIL, DH), jnp.bfloat16)
-        marks = near_marks
-
     for p in range(pieces):
         for h in range(QPK):
             q_all[p, h * rows : (h + 1) * rows, :DH] = q_refs[p][:, h * DH : (h + 1) * DH]
 
     def tile(p, start, first_key, size, hidden, at_row=None):
         at_key = pl.ds(pl.multiple_of(first_key if at_row is None else at_row, UNIT), size)
-        at_mark = pl.ds(pl.multiple_of(first_key, UNIT), size)
-        k_tile = jnp.concatenate([keys[at_key, :], marks[at_mark, :]], axis=1)
+        if at_row is None:
+            mark = marks[at_key, :]
+        else:
+            at_marks = [first_key + i * XS * TAIL for i in range(size // TAIL)]
+            mark = [marks[pl.ds(pl.multiple_of(at, TAIL), TAIL), :] for at in at_marks]
+            mark = jnp.concatenate(mark, axis=0)
+        k_tile = jnp.concatenate([keys[at_key, :], mark], axis=1)
         v_tile = jnp.concatenate([values[at_key, :], jnp.ones((size, DH), jnp.bfloat16)], axis=1)
         count = QPK * rows // STACK
         stacks = [slice(i * STACK, (i + 1) * STACK) for i in range(count)]
@@ -182,13 +180,19 @@
             top[...] = top_in[p]
             acc[...] = acc_in[p]
 
-            @pl.loop(0, YS)
-            def _(at_y):
-                key = (at_y * XS + ((x + 2) & (XS - 1))) * TAIL
-
-                @pl.when((key < start) & (key + TAIL > first))
-                def _():
-                    tile(p, start, key, TAIL, 0, at_y * TAIL)
+            at_x = (x + 2) & (XS - 1)
+            begin = jnp.maximum(first // TAIL - at_x + XS - 1, 0) // XS
+            end = jnp.maximum(start // TAIL - at_x + XS - 1, 0) // XS
+            count = jnp.maximum(end - begin, 0)
+
+            @pl.loop(0, count // 2)
+            def _(t):
+                key = ((begin + 2 * t) * XS + at_x) * TAIL
+                tile(p, start, key, 2 * TAIL, 0, (begin + 2 * t) * TAIL)
+
+            @pl.when(count % 2 == 1)
+            def _():
+                tile(p, start, ((end - 1) * XS + at_x) * TAIL, TAIL, 0, (end - 1) * TAIL)
 
         else:
             top[...] = jnp.full(top.shape, NEG_FILL, top.dtype)
@@ -196,23 +200,49 @@
 
             lo, hi = first // UNIT, start // UNIT + 1
             tail, wide = TAIL // UNIT, WIDE // UNIT
-            rest = jnp.maximum(hi - tail - lo, 0)
+            block = start // TAIL
+            low = jnp.maximum(lo, tail * (block - 1)) if which == "near" else lo
+            rest = jnp.maximum(hi - tail - low, 0)
+            if which == "all":
+                short = (wide - rest % wide) % wide
+                rest = rest + jnp.where((short <= tail) & (short <= low), short, 0)
+                low = jnp.maximum(hi - tail - rest, 0)
             odd = rest % tail
-            begin = lo + odd
+            begin = low + odd
             wides = (rest - odd) // wide
             alone = jnp.where(hi == 1, 1, odd)
 
             @pl.loop(0, alone)
             def _(t):
-                tile(p, start, lo * UNIT, UNIT, UNIT)
-
-            @pl.loop(0, wides)
-            def _(t):
-                tile(p, start, (begin + t * wide) * UNIT, WIDE, 0)
-
-            @pl.loop(0, (rest - odd - wides * wide) // tail)
-            def _(t):
-                tile(p, start, (begin + wides * wide + t * tail) * UNIT, TAIL, 0)
+                tile(p, start, low * UNIT, UNIT, UNIT)
+
+            if which == "all":
+
+                @pl.loop(0, wides)
+                def _(t):
+                    tile(p, start, (begin + t * wide) * UNIT, WIDE, 0)
+
+                @pl.loop(0, (rest - odd - wides * wide) // tail)
+                def _(t):
+                    tile(p, start, (begin + wides * wide + t * tail) * UNIT, TAIL, 0)
+
+            else:
+                @pl.loop(0, jnp.where(rest > odd, 1, 0))
+                def _(t):
+                    tile(p, start, begin * UNIT, TAIL, 0)
+
+                @pl.loop(0, YS - 1)
+                def _(n):
+                    end = block + 2 - XS * (n + 1)
+                    count = jnp.clip(end - jnp.maximum(lo // tail, 0), 0, NEAR_RUN)
+
+                    @pl.when(count == NEAR_RUN)
+                    def _():
+                        tile(p, start, (end - NEAR_RUN) * TAIL, NEAR_RUN * TAIL, 0)
+
+                    @pl.loop(0, jnp.where(count == NEAR_RUN, 0, count))
+                    def _(t):
+                        tile(p, start, (end - 1 - t) * TAIL, TAIL, 0)
 
             @pl.when(hi > 1)
             def _():
@@ -258,9 +288,8 @@
             pltpu.VMEM((stacked, DH), jnp.float32),
             pltpu.VMEM((held, DH), jnp.bfloat16),
             pltpu.VMEM((held, DH), jnp.bfloat16),
-        ]
-        + [pltpu.VMEM((seq, DH), jnp.bfloat16)] * (which == "near"),
-        compiler_params=pltpu.CompilerParams(vmem_limit_bytes=32 * 1024 * 1024),
+        ],
+        compiler_params=pltpu.CompilerParams(vmem_limit_bytes=22 * 1024 * 1024),
         cost_estimate=pl.CostEstimate(
             flops=pieces * 4 * stacked * seq // 4 * DH,
             bytes_accessed=8 * 1024 * 1024,
@@ -277,7 +306,7 @@
     rank = rank[None]
 
     by_head = jax.ShapeDtypeStruct((KVH, 2, rows, DH), jnp.bfloat16)
-    (pairs,) = vmem_call(split_kernel, [by_head], rank, keys, values)
+    (pairs,) = vmem_call(split_kernel, [by_head], (), keys, values)
     own = lax.all_to_all(
         pairs, "ctx", split_axis=0, concat_axis=0, tiled=True, axis_index_groups=head_groups()
     ).reshape(YS, CS, 2, rows, DH)
@@ -288,15 +317,17 @@
 
     left, right = along(own, 1), along(own, XS - 1)
 
-    by_device = jax.ShapeDtypeStruct((rows, GROUP), jnp.bfloat16)
-    sent = vmem_call(query_kernel, [by_device] * len(STEPS), rank, queries)
+    by_device = [jax.ShapeDtypeStruct((rows, GROUP), jnp.bfloat16)] * len(STEPS)
+    sent = vmem_call(query_kernel, by_device, (rank,), queries)
     sent = dict(zip(STEPS, sent, strict=True))
 
     def send(dy, dc):
         part = sent[dy, dc]
         return lax.ppermute(part, "ctx", shift(dy, 0, dc)) if dy or dc else part
 
-    got = {(dy, 0): send(dy, 0) for dy in range(YS)}
+    got = {(0, 1): send(0, 1)}
+    sent, got = lax.optimization_barrier((sent, got))
+    got |= {(dy, 0): send(dy, 0) for dy in range(YS)}
     sent, got = lax.optimization_barrier((sent, got))
     got |= {(dy, 1): send(dy, 1) for dy in range(1, YS)}
     half = YS // 2
@@ -312,8 +343,6 @@
     near = (own, left, right)
     pieces = [got[dy, 0] for dy in range(YS)]
     state = attend(0, "near", rank, doc_lengths, marks, near, pieces)
-    sent, state = lax.optimization_barrier((sent, state))
-    got[0, 1] = send(0, 1)
     done = attend(0, "far", rank, doc_lengths, marks, far, pieces, state)
 
     def give(done, dc):

time: 118 us -> 112 us (0.949)
  the two profiles are of different devices: /device:TPU:103 before, /device:TPU:1 now
where the time goes in v3:
time: 112 us; the launch traced here: 111 us
  Pallas kernels  35.6 us (32%)
  waiting for transfers between devices  28.8 us (26%)
  starting transfers between devices  22.2 us (20%)
  blocking collectives  21.2 us (19%)
  local copies, waits for them, and re-layouts  2.19 us (2%)
    pallas_call x3, Pallas kernels, attend(): pl.pallas_call(functools.partial(attend_kernel, pieces, dc, which), out_s...  30.2 us
    all_to_all x1, blocking collectives, per_device(): lax.all_to_all(pairs, 'ctx', split_axis=0, concat_axis=0, tiled=True, axi...  21.2 us
    ppermute x7, waiting for transfers between devices, give(): lax.ppermute(piece, 'ctx', shift(YS - dy, 0, dc))  14.2 us
    ppermute x4, waiting for transfers between devices, along(): return lax.ppermute(part, 'ctx', shift(0, dx, 0))  13.4 us
    ppermute x7, starting transfers between devices, send(): return lax.ppermute(part, 'ctx', shift(dy, 0, dc)) if dy or dc else part  8.97 us
    ppermute x7, starting transfers between devices, give(): lax.ppermute(piece, 'ctx', shift(YS - dy, 0, dc))  7.76 us
    ppermute x4, starting transfers between devices, along(): return lax.ppermute(part, 'ctx', shift(0, dx, 0))  5.47 us
    pallas_call x2, Pallas kernels, vmem_call(): pl.pallas_call(kernel, out_shape=out_shape, in_specs=[smem] * len(scalars...  5.42 us
  transfers between devices with their start and end apart: 18, of which 4 were waited for; matrix products, arithmetic and copies ran while one was open for 2% of the time, Pallas kernels for 30%

profile of v3, /device:TPU:1, one launch (start us, length us, event | category | flops | bytes accessed | tf_op | source)
XLA Modules:
  0.0 111.2 jit_solution(10628469320146052220)
XLA Ops:
  0.0 2.4 %shard_map.46 = bf16[8,2,256,128]{3,2,1,0:T(8,128)(2,1)} custom-call(bf16[256,1024]{1,0:T(8,128)(2,1)} %keys.1, bf16[256,1024]{1,0:T(8,128)(2,1)} %values.1), custom_call_target="tpu_custom_call" | custom-call | tf_op jit(solution)/shard_map/pallas_call | solution.py:65
  2.4 21.2 %all_to_all.5 = bf16[8,2,256,128]{3,2,1,0:T(8,128)(2,1)S(1)} all-to-all(bf16[8,2,256,128]{3,2,1,0:T(8,128)(2,1)} %shard_map.46), channel_id=1, replica_groups={{0,1,8,9,16,17,24,25},{2,3,10,11,18,19,26,27},{4,5,12,13,20,21,28,29},{..., dimensions={0} | all-to-all | bytes 2097152 | tf_op jit(solution)/shard_map/all_to_all | solution.py:310
  23.5 1.2 %collective-permute-start = (bf16[4,2,2,256,128]{4,3,2,1,0:T(8,128)(2,1)S(1)}, bf16[4,2,2,256,128]{4,3,2,1,0:T(8,128)(2,1)S(1)}, u32[]{:S(2)}, u32[]{:S(2)}) collective-permute-start(bf16[4,2,2,256,128]{4,3,2,1,0:T(8,128)(2,1)S(1)} %bitcast.3), channel_id=1, source_target_pairs={{0,2},{1,3},{2,4},{3,5},{4,6},{5,7},{6,0},{7,1},{8,10},{9,11},{10,... | collective-permute-start | bytes 3145736 | tf_op jit(solution)/shard_map/ppermute | solution.py:316
  24.7 1.5 %collective-permute-start.1 = (bf16[4,2,2,256,128]{4,3,2,1,0:T(8,128)(2,1)S(1)}, bf16[4,2,2,256,128]{4,3,2,1,0:T(8,128)(2,1)S(1)}, u32[]{:S(2)}, u32[]{:S(2)}) collective-permute-start(bf16[4,2,2,256,128]{4,3,2,1,0:T(8,128)(2,1)S(1)} %bitcast.4), channel_id=1, source_target_pairs={{0,6},{1,7},{2,0},{3,1},{4,2},{5,3},{6,4},{7,5},{8,14},{9,15},{10,... | collective-permute-start | bytes 3145736 | tf_op jit(solution)/shard_map/ppermute | solution.py:316
  26.2 3.1 %shard_map.47 = (bf16[256,512]{1,0:T(8,128)(2,1)}, bf16[256,512]{1,0:T(8,128)(2,1)}, bf16[256,512]{1,0:T(8,128)(2,1)}, bf16[256,512]{1,0:T(8,128)(2,1)}, bf16[25...) custom-call(s32[1]{0:T(128)} %bitcast.rank, ...), custom_call_target="tpu_custom_call" | custom-call | tf_op jit(solution)/shard_map/pallas_call | solution.py:65
  29.3 1.6 %collective-permute-start.4 = (bf16[256,512]{1,0:T(8,128)(2,1)}, bf16[256,512]{1,0:T(8,128)(2,1)S(1)}, u32[]{:S(2)}, u32[]{:S(2)}) collective-permute-start(bf16[256,512]{1,0:T(8,128)(2,1)} %get-tuple-element.62), channel_id=1, source_target_pairs={{0,1},{1,0},{2,3},{3,2},{4,5},{5,4},{6,7},{7,6},{8,9},{9,8},{10,11... | collective-permute-start | bytes 786440 | tf_op jit(solution)/shard_map/ppermute | solution.py:326
  30.9 0.1 copy.6
  31.0 0.1 reduce
  31.1 1.1 %collective-permute-done.4.refs_5_ = bf16[256,512]{1,0:T(8,128)(2,1)S(1)} collective-permute-done((bf16[256,512]{1,0:T(8,128)(2,1)}, bf16[256,512]{1,0:T(8,128)(2,1)S(1)}, u32[]{:S(2)}, u32[]{:S(2)}) %collective-permute-start.4) | collective-permute-done | bytes 262176 | tf_op jit(solution)/shard_map/ppermute | solution.py:326
  32.2 0.3 collective-permute-start.5
  32.5 1.8 %collective-permute-start.6 = (bf16[256,512]{1,0:T(8,128)(2,1)}, bf16[256,512]{1,0:T(8,128)(2,1)S(1)}, u32[]{:S(2)}, u32[]{:S(2)}) collective-permute-start(bf16[256,512]{1,0:T(8,128)(2,1)} %get-tuple-element.71), channel_id=1, source_target_pairs={{0,16},{1,17},{2,18},{3,19},{4,20},{5,21},{6,22},{7,23},{8,24},{9,... | collective-permute-start | bytes 786440 | tf_op jit(solution)/shard_map/ppermute | solution.py:326
  34.3 0.6 collective-permute-start.7
  34.9 13.4 %collective-permute-done.refs_1_ = bf16[4,2,2,256,128]{4,3,2,1,0:T(8,128)(2,1)S(1)} collective-permute-done((bf16[4,2,2,256,128]{4,3,2,1,0:T(8,128)(2,1)S(1)}, bf16[4,2,2,256,128]{4,3,2,1,0:T(8,128)(2,1)S(1)}, u32[]{:S(2)}, u32[]{:S(2)}) %collective-permute-start) | collective-permute-done | bytes 1048608 | tf_op jit(solution)/shard_map/ppermute | solution.py:316
  48.4 0.1 collective-permute-start.2
  48.5 0.0 collective-permute-done.1.refs_2_
  48.5 2.7 %collective-permute-start.3 = (bf16[2,2,2,256,128]{4,3,2,1,0:T(8,128)(2,1)S(1)}, bf16[2,2,2,256,128]{4,3,2,1,0:T(8,128)(2,1)S(1)}, u32[]{:S(2)}, u32[]{:S(2)}) collective-permute-start(bf16[2,2,2,256,128]{4,3,2,1,0:T(8,128)(2,1)S(1)} %slice.9), channel_id=1, source_target_pairs={{0,6},{1,7},{2,0},{3,1},{4,2},{5,3},{6,4},{7,5},{8,14},{9,15},{10,... | collective-permute-start | bytes 1572872 | tf_op jit(solution)/shard_map/ppermute | solution.py:316
  51.2 0.8 select_convert_fusion
  52.1 0.0 copy-start.1
  52.1 0.4 pad.4.marks
  52.5 0.0 collective-permute-done.5.refs_4_.refs_3_
  52.5 0.0 collective-permute-done.6.refs_5_.refs_4_
  52.5 0.0 collective-permute-done.7.refs_6_.refs_5_
  52.6 0.5 copy-done.5
  53.0 3.3 %collective-permute-start.10 = (bf16[256,512]{1,0:T(8,128)(2,1)S(1)}, bf16[256,512]{1,0:T(8,128)(2,1)S(1)}, u32[]{:S(2)}, u32[]{:S(2)}) collective-permute-start(bf16[256,512]{1,0:T(8,128)(2,1)S(1)} %copy-done.5), channel_id=1, source_target_pairs={{0,25},{1,24},{2,27},{3,26},{4,29},{5,28},{6,31},{7,30},{8,1},{9,0... | collective-permute-start | bytes 786440 | tf_op jit(solution)/shard_map/ppermute | solution.py:326
  56.3 0.0 collective-permute-start.8
  56.3 1.4 %collective-permute-start.9 = (bf16[256,512]{1,0:T(8,128)(2,1)S(1)}, bf16[256,512]{1,0:T(8,128)(2,1)S(1)}, u32[]{:S(2)}, u32[]{:S(2)}) collective-permute-start(bf16[256,512]{1,0:T(8,128)(2,1)S(1)} %copy-done.3), channel_id=1, source_target_pairs={{0,17},{1,16},{2,19},{3,18},{4,21},{5,20},{6,23},{7,22},{8,25},{9,... | collective-permute-start | bytes 786440 | tf_op jit(solution)/shard_map/ppermute | solution.py:326
  57.7 12.5 %shard_map.48 = (f32[4,1024,256]{2,1,0:T(8,128)S(1)}, f32[4,1024,128]{2,1,0:T(8,128)S(1)}) custom-call(s32[1]{0:T(128)} %bitcast.rank, s32[16]{0:T(128)S(1)} %copy-done, bf16[8192,128]{1,0:T(8,128)(2,1)S(1)} %pad.4.marks, bf16[4,2,2,256,128]{4,3,2,1,0:T(8,128)(2,1)S(1)} %bitcast.5, bf16[4,2,2,256,128]{4,3,2,1,0:T(8,128)(2,1)S(1)} %collective-permute-done.refs_1_, ...), custom_call_target="tpu_custom_call" | custom-call | flops 4294967296 | bytes 8388608 | tf_op jit(solution)/shard_map/pallas_call | solution.py:279
  70.3 0.0 collective-permute-done.2.refs_0_.refs_3_
  70.3 0.0 collective-permute-done.3.refs_1_.refs_4_
  70.3 4.1 %shard_map.49 = (bf16[256,512]{1,0:T(8,128)(2,1)S(1)}, bf16[256,512]{1,0:T(8,128)(2,1)S(1)}, bf16[256,512]{1,0:T(8,128)(2,1)S(1)}, bf16[256,512]{1,0:T(8,128)(2,1)S(1)}) custom-call(s32[1]{0:T(128)} %bitcast.rank, s32[16]{0:T(128)S(1)} %copy-done, bf16[8192,128]{1,0:T(8,128)(2,1)S(1)} %pad.4.marks, ...), custom_call_target="tpu_custom_call" | custom-call | flops 4294967296 | bytes 8388608 | tf_op jit(solution)/shard_map/pallas_call | solution.py:279
  74.4 0.0 collective-permute-done.10.refs_8_
  74.4 0.0 collective-permute-done.8.refs_6_
  74.5 0.0 collective-permute-done.9.refs_7_
  74.5 2.2 %collective-permute-start.11 = (bf16[256,512]{1,0:T(8,128)(2,1)S(1)}, bf16[256,512]{1,0:T(8,128)(2,1)S(1)}, u32[]{:S(2)}, u32[]{:S(2)}) collective-permute-start(bf16[256,512]{1,0:T(8,128)(2,1)S(1)} %get-tuple-element.100), channel_id=1, source_target_pairs={{0,24},{1,25},{2,26},{3,27},{4,28},{5,29},{6,30},{7,31},{8,0},{9,1... | collective-permute-start | bytes 786440 | tf_op jit(solution)/shard_map/ppermute | solution.py:350
  76.7 1.8 %collective-permute-start.12 = (bf16[256,512]{1,0:T(8,128)(2,1)S(1)}, bf16[256,512]{1,0:T(8,128)(2,1)S(1)}, u32[]{:S(2)}, u32[]{:S(2)}) collective-permute-start(bf16[256,512]{1,0:T(8,128)(2,1)S(1)} %get-tuple-element.101), channel_id=1, source_target_pairs={{0,16},{1,17},{2,18},{3,19},{4,20},{5,21},{6,22},{7,23},{8,24},{9,... | collective-permute-start | bytes 786440 | tf_op jit(solution)/shard_map/ppermute | solution.py:350
  78.4 0.0 collective-permute-start.13
  78.4 13.5 %shard_map.50 = (bf16[256,512]{1,0:T(8,128)(2,1)S(1)}, bf16[256,512]{1,0:T(8,128)(2,1)S(1)}, bf16[256,512]{1,0:T(8,128)(2,1)S(1)}, bf16[256,512]{1,0:T(8,128)(2,1)S(1)}) custom-call(s32[1]{0:T(128)} %bitcast.rank, s32[16]{0:T(128)S(1)} %copy-done, bf16[8192,128]{1,0:T(8,128)(2,1)S(1)} %pad.4.marks, bf16[4,2,2,256,128]{4,3,2,1,0:T(8,128)(2,1)S(1)} %bitcast.6, ...), custom_call_target="tpu_custom_call" | custom-call | flops 4294967296 | bytes 8388608 | tf_op jit(solution)/shard_map/pallas_call | solution.py:279
  92.0 0.0 collective-permute-done.12
  92.0 0.0 collective-permute-done.13
  92.0 0.1 collective-permute-start.14
  92.1 3.0 %collective-permute-start.15 = (bf16[256,512]{1,0:T(8,128)(2,1)S(1)}, bf16[256,512]{1,0:T(8,128)(2,1)S(1)}, u32[]{:S(2)}, u32[]{:S(2)}) collective-permute-start(bf16[256,512]{1,0:T(8,128)(2,1)S(1)} %get-tuple-element.108), channel_id=1, source_target_pairs={{0,25},{1,24},{2,27},{3,26},{4,29},{5,28},{6,31},{7,30},{8,1},{9,0... | collective-permute-start | bytes 786440 | tf_op jit(solution)/shard_map/ppermute | solution.py:350
  95.1 0.3 collective-permute-start.16
  95.4 0.4 collective-permute-start.17
  95.8 0.2 broadcast_in_dim.17
  96.2 10.3 %collective-permute-done.15 = bf16[256,512]{1,0:T(8,128)(2,1)S(1)} collective-permute-done((bf16[256,512]{1,0:T(8,128)(2,1)S(1)}, bf16[256,512]{1,0:T(8,128)(2,1)S(1)}, u32[]{:S(2)}, u32[]{:S(2)}) %collective-permute-start.15) | collective-permute-done | bytes 262176 | tf_op jit(solution)/shard_map/ppermute | solution.py:350
  106.6 0.0 copy-start.2
  106.6 3.9 %collective-permute-done.17 = bf16[256,512]{1,0:T(8,128)(2,1)S(1)} collective-permute-done((bf16[256,512]{1,0:T(8,128)(2,1)S(1)}, bf16[256,512]{1,0:T(8,128)(2,1)S(1)}, u32[]{:S(2)}, u32[]{:S(2)}) %collective-permute-start.17) | collective-permute-done | bytes 262176 | tf_op jit(solution)/shard_map/ppermute | solution.py:350
  110.5 0.7 constant_dynamic-update-slice_fusion
  (23 shorter events, 0.3 us)
Async XLA Ops:
  2.4 28.5 %copy-start = (s32[16]{0:T(128)S(1)}, s32[16]{0:T(128)}, u32[]{:S(2)}) copy-start(s32[16]{0:T(128)} %doc_lengths.2) | copy-start | bytes 196
  23.5 24.8 %collective-permute-start = (bf16[4,2,2,256,128]{4,3,2,1,0:T(8,128)(2,1)S(1)}, bf16[4,2,2,256,128]{4,3,2,1,0:T(8,128)(2,1)S(1)}, u32[]{:S(2)}, u32[]{:S(2)}) collective-permute-start(bf16[4,2,2,256,128]{4,3,2,1,0:T(8,128)(2,1)S(1)} %bitcast.3), channel_id=1, source_target_pairs={{0,2},{1,3},{2,4},{3,5},{4,6},{5,7},{6,0},{7,1},{8,10},{9,11},{10,... | collective-permute-start | bytes 3145736 | tf_op jit(solution)/shard_map/ppermute | solution.py:316
  24.7 23.7 %collective-permute-start.1 = (bf16[4,2,2,256,128]{4,3,2,1,0:T(8,128)(2,1)S(1)}, bf16[4,2,2,256,128]{4,3,2,1,0:T(8,128)(2,1)S(1)}, u32[]{:S(2)}, u32[]{:S(2)}) collective-permute-start(bf16[4,2,2,256,128]{4,3,2,1,0:T(8,128)(2,1)S(1)} %bitcast.4), channel_id=1, source_target_pairs={{0,6},{1,7},{2,0},{3,1},{4,2},{5,3},{6,4},{7,5},{8,14},{9,15},{10,... | collective-permute-start | bytes 3145736 | tf_op jit(solution)/shard_map/ppermute | solution.py:316
  29.3 3.0 %collective-permute-start.4 = (bf16[256,512]{1,0:T(8,128)(2,1)}, bf16[256,512]{1,0:T(8,128)(2,1)S(1)}, u32[]{:S(2)}, u32[]{:S(2)}) collective-permute-start(bf16[256,512]{1,0:T(8,128)(2,1)} %get-tuple-element.62), channel_id=1, source_target_pairs={{0,1},{1,0},{2,3},{3,2},{4,5},{5,4},{6,7},{7,6},{8,9},{9,8},{10,11... | collective-permute-start | bytes 786440 | tf_op jit(solution)/shard_map/ppermute | solution.py:326
  32.2 20.3 %collective-permute-start.5 = (bf16[256,512]{1,0:T(8,128)(2,1)}, bf16[256,512]{1,0:T(8,128)(2,1)S(1)}, u32[]{:S(2)}, u32[]{:S(2)}) collective-permute-start(bf16[256,512]{1,0:T(8,128)(2,1)} %get-tuple-element.69), channel_id=1, source_target_pairs={{0,8},{1,9},{2,10},{3,11},{4,12},{5,13},{6,14},{7,15},{8,16},{9,17... | collective-permute-start | bytes 786440 | tf_op jit(solution)/shard_map/ppermute | solution.py:326
  32.5 20.0 %collective-permute-start.6 = (bf16[256,512]{1,0:T(8,128)(2,1)}, bf16[256,512]{1,0:T(8,128)(2,1)S(1)}, u32[]{:S(2)}, u32[]{:S(2)}) collective-permute-start(bf16[256,512]{1,0:T(8,128)(2,1)} %get-tuple-element.71), channel_id=1, source_target_pairs={{0,16},{1,17},{2,18},{3,19},{4,20},{5,21},{6,22},{7,23},{8,24},{9,... | collective-permute-start | bytes 786440 | tf_op jit(solution)/shard_map/ppermute | solution.py:326
  34.3 18.2 %collective-permute-start.7 = (bf16[256,512]{1,0:T(8,128)(2,1)}, bf16[256,512]{1,0:T(8,128)(2,1)S(1)}, u32[]{:S(2)}, u32[]{:S(2)}) collective-permute-start(bf16[256,512]{1,0:T(8,128)(2,1)} %get-tuple-element.73), channel_id=1, source_target_pairs={{0,24},{1,25},{2,26},{3,27},{4,28},{5,29},{6,30},{7,31},{8,0},{9,1... | collective-permute-start | bytes 786440 | tf_op jit(solution)/shard_map/ppermute | solution.py:326
  48.4 21.9 %collective-permute-start.2 = (bf16[2,2,2,256,128]{4,3,2,1,0:T(8,128)(2,1)S(1)}, bf16[2,2,2,256,128]{4,3,2,1,0:T(8,128)(2,1)S(1)}, u32[]{:S(2)}, u32[]{:S(2)}) collective-permute-start(bf16[2,2,2,256,128]{4,3,2,1,0:T(8,128)(2,1)S(1)} %slice.8), channel_id=1, source_target_pairs={{0,2},{1,3},{2,4},{3,5},{4,6},{5,7},{6,0},{7,1},{8,10},{9,11},{10,... | collective-permute-start | bytes 1572872 | tf_op jit(solution)/shard_map/ppermute | solution.py:316
  48.5 21.8 %collective-permute-start.3 = (bf16[2,2,2,256,128]{4,3,2,1,0:T(8,128)(2,1)S(1)}, bf16[2,2,2,256,128]{4,3,2,1,0:T(8,128)(2,1)S(1)}, u32[]{:S(2)}, u32[]{:S(2)}) collective-permute-start(bf16[2,2,2,256,128]{4,3,2,1,0:T(8,128)(2,1)S(1)} %slice.9), channel_id=1, source_target_pairs={{0,6},{1,7},{2,0},{3,1},{4,2},{5,3},{6,4},{7,5},{8,14},{9,15},{10,... | collective-permute-start | bytes 1572872 | tf_op jit(solution)/shard_map/ppermute | solution.py:316
  52.1 1.0 copy-start.5
  52.1 4.2 %copy-start.4 = (bf16[256,512]{1,0:T(8,128)(2,1)S(1)}, bf16[256,512]{1,0:T(8,128)(2,1)}, u32[]{:S(2)}) copy-start(bf16[256,512]{1,0:T(8,128)(2,1)} %get-tuple-element.88) | copy-start | bytes 786436
  52.1 4.2 %copy-start.3 = (bf16[256,512]{1,0:T(8,128)(2,1)S(1)}, bf16[256,512]{1,0:T(8,128)(2,1)}, u32[]{:S(2)}) copy-start(bf16[256,512]{1,0:T(8,128)(2,1)} %get-tuple-element.89) | copy-start | bytes 786436
  52.1 5.6 %copy-start.1 = (bf16[256,512]{1,0:T(8,128)(2,1)S(1)}, bf16[256,512]{1,0:T(8,128)(2,1)}, u32[]{:S(2)}) copy-start(bf16[256,512]{1,0:T(8,128)(2,1)} %get-tuple-element.77.refs_3_.refs_2_) | copy-start | bytes 786436
  53.0 21.4 %collective-permute-start.10 = (bf16[256,512]{1,0:T(8,128)(2,1)S(1)}, bf16[256,512]{1,0:T(8,128)(2,1)S(1)}, u32[]{:S(2)}, u32[]{:S(2)}) collective-permute-start(bf16[256,512]{1,0:T(8,128)(2,1)S(1)} %copy-done.5), channel_id=1, source_target_pairs={{0,25},{1,24},{2,27},{3,26},{4,29},{5,28},{6,31},{7,30},{8,1},{9,0... | collective-permute-start | bytes 786440 | tf_op jit(solution)/shard_map/ppermute | solution.py:326
  56.3 18.1 %collective-permute-start.8 = (bf16[256,512]{1,0:T(8,128)(2,1)S(1)}, bf16[256,512]{1,0:T(8,128)(2,1)S(1)}, u32[]{:S(2)}, u32[]{:S(2)}) collective-permute-start(bf16[256,512]{1,0:T(8,128)(2,1)S(1)} %copy-done.4), channel_id=1, source_target_pairs={{0,9},{1,8},{2,11},{3,10},{4,13},{5,12},{6,15},{7,14},{8,17},{9,16... | collective-permute-start | bytes 786440 | tf_op jit(solution)/shard_map/ppermute | solution.py:326
  56.3 18.1 %collective-permute-start.9 = (bf16[256,512]{1,0:T(8,128)(2,1)S(1)}, bf16[256,512]{1,0:T(8,128)(2,1)S(1)}, u32[]{:S(2)}, u32[]{:S(2)}) collective-permute-start(bf16[256,512]{1,0:T(8,128)(2,1)S(1)} %copy-done.3), channel_id=1, source_target_pairs={{0,17},{1,16},{2,19},{3,18},{4,21},{5,20},{6,23},{7,22},{8,25},{9,... | collective-permute-start | bytes 786440 | tf_op jit(solution)/shard_map/ppermute | solution.py:326
  74.5 17.5 %collective-permute-start.11 = (bf16[256,512]{1,0:T(8,128)(2,1)S(1)}, bf16[256,512]{1,0:T(8,128)(2,1)S(1)}, u32[]{:S(2)}, u32[]{:S(2)}) collective-permute-start(bf16[256,512]{1,0:T(8,128)(2,1)S(1)} %get-tuple-element.100), channel_id=1, source_target_pairs={{0,24},{1,25},{2,26},{3,27},{4,28},{5,29},{6,30},{7,31},{8,0},{9,1... | collective-permute-start | bytes 786440 | tf_op jit(solution)/shard_map/ppermute | solution.py:350
  76.7 15.3 %collective-permute-start.12 = (bf16[256,512]{1,0:T(8,128)(2,1)S(1)}, bf16[256,512]{1,0:T(8,128)(2,1)S(1)}, u32[]{:S(2)}, u32[]{:S(2)}) collective-permute-start(bf16[256,512]{1,0:T(8,128)(2,1)S(1)} %get-tuple-element.101), channel_id=1, source_target_pairs={{0,16},{1,17},{2,18},{3,19},{4,20},{5,21},{6,22},{7,23},{8,24},{9,... | collective-permute-start | bytes 786440 | tf_op jit(solution)/shard_map/ppermute | solution.py:350
  78.4 13.5 %collective-permute-start.13 = (bf16[256,512]{1,0:T(8,128)(2,1)S(1)}, bf16[256,512]{1,0:T(8,128)(2,1)S(1)}, u32[]{:S(2)}, u32[]{:S(2)}) collective-permute-start(bf16[256,512]{1,0:T(8,128)(2,1)S(1)} %get-tuple-element.102), channel_id=1, source_target_pairs={{0,8},{1,9},{2,10},{3,11},{4,12},{5,13},{6,14},{7,15},{8,16},{9,17... | collective-permute-start | bytes 786440 | tf_op jit(solution)/shard_map/ppermute | solution.py:350
  92.0 4.2 %collective-permute-start.14 = (bf16[256,512]{1,0:T(8,128)(2,1)S(1)}, bf16[256,512]{1,0:T(8,128)(2,1)S(1)}, u32[]{:S(2)}, u32[]{:S(2)}) collective-permute-start(bf16[256,512]{1,0:T(8,128)(2,1)S(1)} %get-tuple-element.107), channel_id=1, source_target_pairs={{0,1},{1,0},{2,3},{3,2},{4,5},{5,4},{6,7},{7,6},{8,9},{9,8},{10,11... | collective-permute-start | bytes 786440 | tf_op jit(solution)/shard_map/ppermute | solution.py:350
  92.1 14.4 %collective-permute-start.15 = (bf16[256,512]{1,0:T(8,128)(2,1)S(1)}, bf16[256,512]{1,0:T(8,128)(2,1)S(1)}, u32[]{:S(2)}, u32[]{:S(2)}) collective-permute-start(bf16[256,512]{1,0:T(8,128)(2,1)S(1)} %get-tuple-element.108), channel_id=1, source_target_pairs={{0,25},{1,24},{2,27},{3,26},{4,29},{5,28},{6,31},{7,30},{8,1},{9,0... | collective-permute-start | bytes 786440 | tf_op jit(solution)/shard_map/ppermute | solution.py:350
  95.1 11.4 %collective-permute-start.16 = (bf16[256,512]{1,0:T(8,128)(2,1)S(1)}, bf16[256,512]{1,0:T(8,128)(2,1)S(1)}, u32[]{:S(2)}, u32[]{:S(2)}) collective-permute-start(bf16[256,512]{1,0:T(8,128)(2,1)S(1)} %get-tuple-element.109), channel_id=1, source_target_pairs={{0,17},{1,16},{2,19},{3,18},{4,21},{5,20},{6,23},{7,22},{8,25},{9,... | collective-permute-start | bytes 786440 | tf_op jit(solution)/shard_map/ppermute | solution.py:350
  95.4 15.1 %collective-permute-start.17 = (bf16[256,512]{1,0:T(8,128)(2,1)S(1)}, bf16[256,512]{1,0:T(8,128)(2,1)S(1)}, u32[]{:S(2)}, u32[]{:S(2)}) collective-permute-start(bf16[256,512]{1,0:T(8,128)(2,1)S(1)} %get-tuple-element.110), channel_id=1, source_target_pairs={{0,9},{1,8},{2,11},{3,10},{4,13},{5,12},{6,15},{7,14},{8,17},{9,16... | collective-permute-start | bytes 786440 | tf_op jit(solution)/shard_map/ppermute | solution.py:350
  106.6 4.0 %copy-start.2 = (bf16[256,4096]{1,0:T(8,128)(2,1)}, bf16[256,4096]{1,0:T(8,128)(2,1)S(1)}, u32[]{:S(2)}) copy-start(bf16[256,4096]{1,0:T(8,128)(2,1)S(1)} %constant_dynamic-update-slice_fusion.1) | copy-start | bytes 6291460

commit v4 on v3

--- a/solution.py
+++ b/solution.py
@@ -109,7 +109,11 @@
         for h in range(QPK):
             q_all[p, h * rows : (h + 1) * rows, :DH] = q_refs[p][:, h * DH : (h + 1) * DH]
 
-    def tile(p, start, first_key, size, hidden, at_row=None):
+    def tile(p, start, first_key, size, hidden=0, at_row=None, fresh=False):
+        if which == "near":
+            total, peak = acc_out.at[p], top_out.at[p]
+        else:
+            total, peak = acc, top
         at_key = pl.ds(pl.multiple_of(first_key if at_row is None else at_row, UNIT), size)
         if at_row is None:
             mark = marks[at_key, :]
@@ -140,16 +144,22 @@
                     scores = last
                 else:
                     scores = jnp.concatenate([scores[:, : size - hidden], last], axis=1)
-            old = top[stacks[i], :]
-            new = jnp.maximum(old, jnp.max(scores, axis=1, keepdims=True))
+            new = jnp.max(scores, axis=1, keepdims=True)
+            if fresh:
+                new = jnp.broadcast_to(new, (STACK, DH))
+            else:
+                old = peak[stacks[i], :]
+                new = jnp.maximum(old, new)
             weights = jnp.exp2((scores - jnp.tile(new, (1, size // DH))) * LOG2_SCALE)
-            top[stacks[i], :] = new
-            return weights.astype(jnp.bfloat16), jnp.exp2((old - new) * LOG2_SCALE)
+            peak[stacks[i], :] = new
+            rescale = None if fresh else jnp.exp2((old - new) * LOG2_SCALE)
+            return weights.astype(jnp.bfloat16), rescale
 
         def add(i, weights, rescale):
-            acc[stacks[i], :] = acc[stacks[i], :] * jnp.tile(rescale, (1, 2)) + jnp.dot(
-                weights, v_tile, preferred_element_type=jnp.float32
-            )
+            summed = jnp.dot(weights, v_tile, preferred_element_type=jnp.float32)
+            if not fresh:
+                summed = total[stacks[i], :] * jnp.tile(rescale, (1, 2)) + summed
+            total[stacks[i], :] = summed
 
         coming, ready = multiply(0), None
         for i in range(count):
@@ -188,16 +198,13 @@
             @pl.loop(0, count // 2)
             def _(t):
                 key = ((begin + 2 * t) * XS + at_x) * TAIL
-                tile(p, start, key, 2 * TAIL, 0, (begin + 2 * t) * TAIL)
+                tile(p, start, key, 2 * TAIL, at_row=(begin + 2 * t) * TAIL)
 
             @pl.when(count % 2 == 1)
             def _():
-                tile(p, start, ((end - 1) * XS + at_x) * TAIL, TAIL, 0, (end - 1) * TAIL)
+                tile(p, start, ((end - 1) * XS + at_x) * TAIL, TAIL, at_row=(end - 1) * TAIL)
 
         else:
-            top[...] = jnp.full(top.shape, NEG_FILL, top.dtype)
-            acc[...] = jnp.zeros(acc.shape, acc.dtype)
-
             lo, hi = first // UNIT, start // UNIT + 1
             tail, wide = TAIL // UNIT, WIDE // UNIT
             block = start // TAIL
@@ -210,26 +217,33 @@
             odd = rest % tail
             begin = low + odd
             wides = (rest - odd) // wide
-            alone = jnp.where(hi == 1, 1, odd)
-
-            @pl.loop(0, alone)
-            def _(t):
-                tile(p, start, low * UNIT, UNIT, UNIT)
+
+            @pl.when(hi - lo > 1)
+            def _():
+                tile(p, start, (hi - tail) * UNIT, TAIL, UNIT, fresh=True)
+
+            @pl.when(hi - lo == 1)
+            def _():
+                tile(p, start, lo * UNIT, UNIT, UNIT, fresh=True)
+
+            @pl.when(odd == 1)
+            def _():
+                tile(p, start, low * UNIT, UNIT)
 
             if which == "all":
 
                 @pl.loop(0, wides)
                 def _(t):
-                    tile(p, start, (begin + t * wide) * UNIT, WIDE, 0)
+                    tile(p, start, (begin + t * wide) * UNIT, WIDE)
 
                 @pl.loop(0, (rest - odd - wides * wide) // tail)
                 def _(t):
-                    tile(p, start, (begin + wides * wide + t * tail) * UNIT, TAIL, 0)
+                    tile(p, start, (begin + wides * wide + t * tail) * UNIT, TAIL)
 
             else:
                 @pl.loop(0, jnp.where(rest > odd, 1, 0))
                 def _(t):
-                    tile(p, start, begin * UNIT, TAIL, 0)
+                    tile(p, start, begin * UNIT, TAIL)
 
                 @pl.loop(0, YS - 1)
                 def _(n):
@@ -238,20 +252,13 @@
 
                     @pl.when(count == NEAR_RUN)
                     def _():
-                        tile(p, start, (end - NEAR_RUN) * TAIL, NEAR_RUN * TAIL, 0)
+                        tile(p, start, (end - NEAR_RUN) * TAIL, NEAR_RUN * TAIL)
 
                     @pl.loop(0, jnp.where(count == NEAR_RUN, 0, count))
                     def _(t):
-                        tile(p, start, (end - 1 - t) * TAIL, TAIL, 0)
-
-            @pl.when(hi > 1)
-            def _():
-                tile(p, start, (hi - tail) * UNIT, TAIL, UNIT)
-
-        if which == "near":
-            acc_out[p] = acc[...]
-            top_out[p] = top[...]
-        else:
+                        tile(p, start, (end - 1 - t) * TAIL, TAIL)
+
+        if which != "near":
             for h in range(QPK):
                 at = slice(h * rows, (h + 1) * rows)
                 result = acc[at, :DH] / acc[at, DH:]

time: 112 us -> 110 us (0.982)
  the two profiles are of different devices: /device:TPU:1 before, /device:TPU:65 now
where the time goes in v4:
time: 110 us
  Pallas kernels  34.8 us (32%)
  waiting for transfers between devices  29.7 us (27%)
  starting transfers between devices  21.3 us (19%)
  blocking collectives  20.3 us (18%)
  local copies, waits for them, and re-layouts  2.18 us (2%)
    pallas_call x3, Pallas kernels, attend(): pl.pallas_call(functools.partial(attend_kernel, pieces, dc, which), out_s...  29.4 us
    all_to_all x1, blocking collectives, per_device(): lax.all_to_all(pairs, 'ctx', split_axis=0, concat_axis=0, tiled=True, axi...  20.3 us
    ppermute x7, waiting for transfers between devices, give(): lax.ppermute(piece, 'ctx', shift(YS - dy, 0, dc))  15.2 us
    ppermute x4, waiting for transfers between devices, along(): return lax.ppermute(part, 'ctx', shift(0, dx, 0))  13.4 us
    ppermute x7, starting transfers between devices, send(): return lax.ppermute(part, 'ctx', shift(dy, 0, dc)) if dy or dc else part  8.97 us
    ppermute x7, starting transfers between devices, give(): lax.ppermute(piece, 'ctx', shift(YS - dy, 0, dc))  6.87 us
    ppermute x4, starting transfers between devices, along(): return lax.ppermute(part, 'ctx', shift(0, dx, 0))  5.47 us
    pallas_call x2, Pallas kernels, vmem_call(): pl.pallas_call(kernel, out_shape=out_shape, in_specs=[smem] * len(scalars...  5.42 us
  transfers between devices with their start and end apart: 18, of which 6 were waited for; matrix products, arithmetic and copies ran while one was open for 2% of the time, Pallas kernels for 30%

profile of v4, /device:TPU:65, one launch (start us, length us, event | category | flops | bytes accessed | tf_op | source)
XLA Modules:
  0.0 109.6 jit_solution(6331414704276566189)
XLA Ops:
  0.0 2.4 %shard_map.46 = bf16[8,2,256,128]{3,2,1,0:T(8,128)(2,1)} custom-call(bf16[256,1024]{1,0:T(8,128)(2,1)} %keys.1, bf16[256,1024]{1,0:T(8,128)(2,1)} %values.1), custom_call_target="tpu_custom_call" | custom-call | tf_op jit(solution)/shard_map/pallas_call | solution.py:65
  2.4 20.3 %all_to_all.5 = bf16[8,2,256,128]{3,2,1,0:T(8,128)(2,1)S(1)} all-to-all(bf16[8,2,256,128]{3,2,1,0:T(8,128)(2,1)} %shard_map.46), channel_id=1, replica_groups={{0,1,8,9,16,17,24,25},{2,3,10,11,18,19,26,27},{4,5,12,13,20,21,28,29},{..., dimensions={0} | all-to-all | bytes 2097152 | tf_op jit(solution)/shard_map/all_to_all | solution.py:317
  22.7 1.2 %collective-permute-start = (bf16[4,2,2,256,128]{4,3,2,1,0:T(8,128)(2,1)S(1)}, bf16[4,2,2,256,128]{4,3,2,1,0:T(8,128)(2,1)S(1)}, u32[]{:S(2)}, u32[]{:S(2)}) collective-permute-start(bf16[4,2,2,256,128]{4,3,2,1,0:T(8,128)(2,1)S(1)} %bitcast.3), channel_id=1, source_target_pairs={{0,2},{1,3},{2,4},{3,5},{4,6},{5,7},{6,0},{7,1},{8,10},{9,11},{10,... | collective-permute-start | bytes 3145736 | tf_op jit(solution)/shard_map/ppermute | solution.py:323
  23.9 1.5 %collective-permute-start.1 = (bf16[4,2,2,256,128]{4,3,2,1,0:T(8,128)(2,1)S(1)}, bf16[4,2,2,256,128]{4,3,2,1,0:T(8,128)(2,1)S(1)}, u32[]{:S(2)}, u32[]{:S(2)}) collective-permute-start(bf16[4,2,2,256,128]{4,3,2,1,0:T(8,128)(2,1)S(1)} %bitcast.4), channel_id=1, source_target_pairs={{0,6},{1,7},{2,0},{3,1},{4,2},{5,3},{6,4},{7,5},{8,14},{9,15},{10,... | collective-permute-start | bytes 3145736 | tf_op jit(solution)/shard_map/ppermute | solution.py:323
  25.4 3.1 %shard_map.47 = (bf16[256,512]{1,0:T(8,128)(2,1)}, bf16[256,512]{1,0:T(8,128)(2,1)}, bf16[256,512]{1,0:T(8,128)(2,1)}, bf16[256,512]{1,0:T(8,128)(2,1)}, bf16[25...) custom-call(s32[1]{0:T(128)} %bitcast.rank, ...), custom_call_target="tpu_custom_call" | custom-call | tf_op jit(solution)/shard_map/pallas_call | solution.py:65
  28.4 1.6 %collective-permute-start.4 = (bf16[256,512]{1,0:T(8,128)(2,1)}, bf16[256,512]{1,0:T(8,128)(2,1)S(1)}, u32[]{:S(2)}, u32[]{:S(2)}) collective-permute-start(bf16[256,512]{1,0:T(8,128)(2,1)} %get-tuple-element.62), channel_id=1, source_target_pairs={{0,1},{1,0},{2,3},{3,2},{4,5},{5,4},{6,7},{7,6},{8,9},{9,8},{10,11... | collective-permute-start | bytes 786440 | tf_op jit(solution)/shard_map/ppermute | solution.py:333
  30.0 0.1 copy.6
  30.2 0.1 reduce
  30.3 1.1 %collective-permute-done.4.refs_5_ = bf16[256,512]{1,0:T(8,128)(2,1)S(1)} collective-permute-done((bf16[256,512]{1,0:T(8,128)(2,1)}, bf16[256,512]{1,0:T(8,128)(2,1)S(1)}, u32[]{:S(2)}, u32[]{:S(2)}) %collective-permute-start.4) | collective-permute-done | bytes 262176 | tf_op jit(solution)/shard_map/ppermute | solution.py:333
  31.4 0.3 collective-permute-start.5
  31.7 1.8 %collective-permute-start.6 = (bf16[256,512]{1,0:T(8,128)(2,1)}, bf16[256,512]{1,0:T(8,128)(2,1)S(1)}, u32[]{:S(2)}, u32[]{:S(2)}) collective-permute-start(bf16[256,512]{1,0:T(8,128)(2,1)} %get-tuple-element.71), channel_id=1, source_target_pairs={{0,16},{1,17},{2,18},{3,19},{4,20},{5,21},{6,22},{7,23},{8,24},{9,... | collective-permute-start | bytes 786440 | tf_op jit(solution)/shard_map/ppermute | solution.py:333
  33.5 0.6 collective-permute-start.7
  34.1 13.4 %collective-permute-done.refs_1_ = bf16[4,2,2,256,128]{4,3,2,1,0:T(8,128)(2,1)S(1)} collective-permute-done((bf16[4,2,2,256,128]{4,3,2,1,0:T(8,128)(2,1)S(1)}, bf16[4,2,2,256,128]{4,3,2,1,0:T(8,128)(2,1)S(1)}, u32[]{:S(2)}, u32[]{:S(2)}) %collective-permute-start) | collective-permute-done | bytes 1048608 | tf_op jit(solution)/shard_map/ppermute | solution.py:323
  47.6 0.1 collective-permute-start.2
  47.6 0.0 collective-permute-done.1.refs_2_
  47.7 2.7 %collective-permute-start.3 = (bf16[2,2,2,256,128]{4,3,2,1,0:T(8,128)(2,1)S(1)}, bf16[2,2,2,256,128]{4,3,2,1,0:T(8,128)(2,1)S(1)}, u32[]{:S(2)}, u32[]{:S(2)}) collective-permute-start(bf16[2,2,2,256,128]{4,3,2,1,0:T(8,128)(2,1)S(1)} %slice.9), channel_id=1, source_target_pairs={{0,6},{1,7},{2,0},{3,1},{4,2},{5,3},{6,4},{7,5},{8,14},{9,15},{10,... | collective-permute-start | bytes 1572872 | tf_op jit(solution)/shard_map/ppermute | solution.py:323
  50.4 0.8 select_convert_fusion
  51.3 0.0 copy-start.1
  51.3 0.4 pad.4.marks
  51.7 0.0 collective-permute-done.6.refs_5_.refs_4_
  51.7 0.0 collective-permute-done.7.refs_6_.refs_5_
  51.7 0.5 copy-done.5
  52.2 3.3 %collective-permute-start.10 = (bf16[256,512]{1,0:T(8,128)(2,1)S(1)}, bf16[256,512]{1,0:T(8,128)(2,1)S(1)}, u32[]{:S(2)}, u32[]{:S(2)}) collective-permute-start(bf16[256,512]{1,0:T(8,128)(2,1)S(1)} %copy-done.5), channel_id=1, source_target_pairs={{0,25},{1,24},{2,27},{3,26},{4,29},{5,28},{6,31},{7,30},{8,1},{9,0... | collective-permute-start | bytes 786440 | tf_op jit(solution)/shard_map/ppermute | solution.py:333
  55.5 0.0 collective-permute-start.8
  55.5 1.4 %collective-permute-start.9 = (bf16[256,512]{1,0:T(8,128)(2,1)S(1)}, bf16[256,512]{1,0:T(8,128)(2,1)S(1)}, u32[]{:S(2)}, u32[]{:S(2)}) collective-permute-start(bf16[256,512]{1,0:T(8,128)(2,1)S(1)} %copy-done.3), channel_id=1, source_target_pairs={{0,17},{1,16},{2,19},{3,18},{4,21},{5,20},{6,23},{7,22},{8,25},{9,... | collective-permute-start | bytes 786440 | tf_op jit(solution)/shard_map/ppermute | solution.py:333
  56.9 12.7 %shard_map.48 = (f32[4,1024,256]{2,1,0:T(8,128)S(1)}, f32[4,1024,128]{2,1,0:T(8,128)S(1)}) custom-call(s32[1]{0:T(128)} %bitcast.rank, s32[16]{0:T(128)S(1)} %copy-done, bf16[8192,128]{1,0:T(8,128)(2,1)S(1)} %pad.4.marks, bf16[4,2,2,256,128]{4,3,2,1,0:T(8,128)(2,1)S(1)} %bitcast.5, bf16[4,2,2,256,128]{4,3,2,1,0:T(8,128)(2,1)S(1)} %collective-permute-done.refs_1_, ...), custom_call_target="tpu_custom_call" | custom-call | flops 4294967296 | bytes 8388608 | tf_op jit(solution)/shard_map/pallas_call | solution.py:286
  69.6 0.0 collective-permute-done.2.refs_0_.refs_3_
  69.6 0.0 collective-permute-done.3.refs_1_.refs_4_
  69.6 4.1 %shard_map.49 = (bf16[256,512]{1,0:T(8,128)(2,1)S(1)}, bf16[256,512]{1,0:T(8,128)(2,1)S(1)}, bf16[256,512]{1,0:T(8,128)(2,1)S(1)}, bf16[256,512]{1,0:T(8,128)(2,1)S(1)}) custom-call(s32[1]{0:T(128)} %bitcast.rank, s32[16]{0:T(128)S(1)} %copy-done, bf16[8192,128]{1,0:T(8,128)(2,1)S(1)} %pad.4.marks, ...), custom_call_target="tpu_custom_call" | custom-call | flops 4294967296 | bytes 8388608 | tf_op jit(solution)/shard_map/pallas_call | solution.py:286
  73.8 0.0 collective-permute-done.9.refs_7_
  73.8 2.2 %collective-permute-start.11 = (bf16[256,512]{1,0:T(8,128)(2,1)S(1)}, bf16[256,512]{1,0:T(8,128)(2,1)S(1)}, u32[]{:S(2)}, u32[]{:S(2)}) collective-permute-start(bf16[256,512]{1,0:T(8,128)(2,1)S(1)} %get-tuple-element.100), channel_id=1, source_target_pairs={{0,24},{1,25},{2,26},{3,27},{4,28},{5,29},{6,30},{7,31},{8,0},{9,1... | collective-permute-start | bytes 786440 | tf_op jit(solution)/shard_map/ppermute | solution.py:357
  76.0 1.8 %collective-permute-start.12 = (bf16[256,512]{1,0:T(8,128)(2,1)S(1)}, bf16[256,512]{1,0:T(8,128)(2,1)S(1)}, u32[]{:S(2)}, u32[]{:S(2)}) collective-permute-start(bf16[256,512]{1,0:T(8,128)(2,1)S(1)} %get-tuple-element.101), channel_id=1, source_target_pairs={{0,16},{1,17},{2,18},{3,19},{4,20},{5,21},{6,22},{7,23},{8,24},{9,... | collective-permute-start | bytes 786440 | tf_op jit(solution)/shard_map/ppermute | solution.py:357
  77.8 0.0 collective-permute-start.13
  77.8 12.5 %shard_map.50 = (bf16[256,512]{1,0:T(8,128)(2,1)S(1)}, bf16[256,512]{1,0:T(8,128)(2,1)S(1)}, bf16[256,512]{1,0:T(8,128)(2,1)S(1)}, bf16[256,512]{1,0:T(8,128)(2,1)S(1)}) custom-call(s32[1]{0:T(128)} %bitcast.rank, s32[16]{0:T(128)S(1)} %copy-done, bf16[8192,128]{1,0:T(8,128)(2,1)S(1)} %pad.4.marks, bf16[4,2,2,256,128]{4,3,2,1,0:T(8,128)(2,1)S(1)} %bitcast.6, ...), custom_call_target="tpu_custom_call" | custom-call | flops 4294967296 | bytes 8388608 | tf_op jit(solution)/shard_map/pallas_call | solution.py:286
  90.4 0.0 collective-permute-done.11
  90.4 0.0 collective-permute-done.12
  90.4 0.9 collective-permute-done.13
  91.3 0.4 collective-permute-start.14
  91.7 1.8 %collective-permute-start.15 = (bf16[256,512]{1,0:T(8,128)(2,1)S(1)}, bf16[256,512]{1,0:T(8,128)(2,1)S(1)}, u32[]{:S(2)}, u32[]{:S(2)}) collective-permute-start(bf16[256,512]{1,0:T(8,128)(2,1)S(1)} %get-tuple-element.108), channel_id=1, source_target_pairs={{0,25},{1,24},{2,27},{3,26},{4,29},{5,28},{6,31},{7,30},{8,1},{9,0... | collective-permute-start | bytes 786440 | tf_op jit(solution)/shard_map/ppermute | solution.py:357
  93.6 0.2 collective-permute-start.16
  93.7 0.4 collective-permute-start.17
  94.2 0.2 broadcast_in_dim.17
  94.6 0.0 collective-permute-done.14
  94.6 5.9 %collective-permute-done.15 = bf16[256,512]{1,0:T(8,128)(2,1)S(1)} collective-permute-done((bf16[256,512]{1,0:T(8,128)(2,1)S(1)}, bf16[256,512]{1,0:T(8,128)(2,1)S(1)}, u32[]{:S(2)}, u32[]{:S(2)}) %collective-permute-start.15) | collective-permute-done | bytes 262176 | tf_op jit(solution)/shard_map/ppermute | solution.py:357
  100.6 3.1 %collective-permute-done.16 = bf16[256,512]{1,0:T(8,128)(2,1)S(1)} collective-permute-done((bf16[256,512]{1,0:T(8,128)(2,1)S(1)}, bf16[256,512]{1,0:T(8,128)(2,1)S(1)}, u32[]{:S(2)}, u32[]{:S(2)}) %collective-permute-start.16) | collective-permute-done | bytes 262176 | tf_op jit(solution)/shard_map/ppermute | solution.py:357
  103.7 0.0 copy-start.2
  103.7 5.2 %collective-permute-done.17 = bf16[256,512]{1,0:T(8,128)(2,1)S(1)} collective-permute-done((bf16[256,512]{1,0:T(8,128)(2,1)S(1)}, bf16[256,512]{1,0:T(8,128)(2,1)S(1)}, u32[]{:S(2)}, u32[]{:S(2)}) %collective-permute-start.17) | collective-permute-done | bytes 262176 | tf_op jit(solution)/shard_map/ppermute | solution.py:357
  108.9 0.7 constant_dynamic-update-slice_fusion
  (23 shorter events, 0.3 us)
Async XLA Ops:
  2.4 27.7 %copy-start = (s32[16]{0:T(128)S(1)}, s32[16]{0:T(128)}, u32[]{:S(2)}) copy-start(s32[16]{0:T(128)} %doc_lengths.2) | copy-start | bytes 196
  22.7 24.8 %collective-permute-start = (bf16[4,2,2,256,128]{4,3,2,1,0:T(8,128)(2,1)S(1)}, bf16[4,2,2,256,128]{4,3,2,1,0:T(8,128)(2,1)S(1)}, u32[]{:S(2)}, u32[]{:S(2)}) collective-permute-start(bf16[4,2,2,256,128]{4,3,2,1,0:T(8,128)(2,1)S(1)} %bitcast.3), channel_id=1, source_target_pairs={{0,2},{1,3},{2,4},{3,5},{4,6},{5,7},{6,0},{7,1},{8,10},{9,11},{10,... | collective-permute-start | bytes 3145736 | tf_op jit(solution)/shard_map/ppermute | solution.py:323
  23.9 23.7 %collective-permute-start.1 = (bf16[4,2,2,256,128]{4,3,2,1,0:T(8,128)(2,1)S(1)}, bf16[4,2,2,256,128]{4,3,2,1,0:T(8,128)(2,1)S(1)}, u32[]{:S(2)}, u32[]{:S(2)}) collective-permute-start(bf16[4,2,2,256,128]{4,3,2,1,0:T(8,128)(2,1)S(1)} %bitcast.4), channel_id=1, source_target_pairs={{0,6},{1,7},{2,0},{3,1},{4,2},{5,3},{6,4},{7,5},{8,14},{9,15},{10,... | collective-permute-start | bytes 3145736 | tf_op jit(solution)/shard_map/ppermute | solution.py:323
  28.4 3.0 %collective-permute-start.4 = (bf16[256,512]{1,0:T(8,128)(2,1)}, bf16[256,512]{1,0:T(8,128)(2,1)S(1)}, u32[]{:S(2)}, u32[]{:S(2)}) collective-permute-start(bf16[256,512]{1,0:T(8,128)(2,1)} %get-tuple-element.62), channel_id=1, source_target_pairs={{0,1},{1,0},{2,3},{3,2},{4,5},{5,4},{6,7},{7,6},{8,9},{9,8},{10,11... | collective-permute-start | bytes 786440 | tf_op jit(solution)/shard_map/ppermute | solution.py:333
  31.4 20.3 %collective-permute-start.5 = (bf16[256,512]{1,0:T(8,128)(2,1)}, bf16[256,512]{1,0:T(8,128)(2,1)S(1)}, u32[]{:S(2)}, u32[]{:S(2)}) collective-permute-start(bf16[256,512]{1,0:T(8,128)(2,1)} %get-tuple-element.69), channel_id=1, source_target_pairs={{0,8},{1,9},{2,10},{3,11},{4,12},{5,13},{6,14},{7,15},{8,16},{9,17... | collective-permute-start | bytes 786440 | tf_op jit(solution)/shard_map/ppermute | solution.py:333
  31.7 20.0 %collective-permute-start.6 = (bf16[256,512]{1,0:T(8,128)(2,1)}, bf16[256,512]{1,0:T(8,128)(2,1)S(1)}, u32[]{:S(2)}, u32[]{:S(2)}) collective-permute-start(bf16[256,512]{1,0:T(8,128)(2,1)} %get-tuple-element.71), channel_id=1, source_target_pairs={{0,16},{1,17},{2,18},{3,19},{4,20},{5,21},{6,22},{7,23},{8,24},{9,... | collective-permute-start | bytes 786440 | tf_op jit(solution)/shard_map/ppermute | solution.py:333
  33.5 18.2 %collective-permute-start.7 = (bf16[256,512]{1,0:T(8,128)(2,1)}, bf16[256,512]{1,0:T(8,128)(2,1)S(1)}, u32[]{:S(2)}, u32[]{:S(2)}) collective-permute-start(bf16[256,512]{1,0:T(8,128)(2,1)} %get-tuple-element.73), channel_id=1, source_target_pairs={{0,24},{1,25},{2,26},{3,27},{4,28},{5,29},{6,30},{7,31},{8,0},{9,1... | collective-permute-start | bytes 786440 | tf_op jit(solution)/shard_map/ppermute | solution.py:333
  47.6 22.1 %collective-permute-start.2 = (bf16[2,2,2,256,128]{4,3,2,1,0:T(8,128)(2,1)S(1)}, bf16[2,2,2,256,128]{4,3,2,1,0:T(8,128)(2,1)S(1)}, u32[]{:S(2)}, u32[]{:S(2)}) collective-permute-start(bf16[2,2,2,256,128]{4,3,2,1,0:T(8,128)(2,1)S(1)} %slice.8), channel_id=1, source_target_pairs={{0,2},{1,3},{2,4},{3,5},{4,6},{5,7},{6,0},{7,1},{8,10},{9,11},{10,... | collective-permute-start | bytes 1572872 | tf_op jit(solution)/shard_map/ppermute | solution.py:323
  47.7 21.9 %collective-permute-start.3 = (bf16[2,2,2,256,128]{4,3,2,1,0:T(8,128)(2,1)S(1)}, bf16[2,2,2,256,128]{4,3,2,1,0:T(8,128)(2,1)S(1)}, u32[]{:S(2)}, u32[]{:S(2)}) collective-permute-start(bf16[2,2,2,256,128]{4,3,2,1,0:T(8,128)(2,1)S(1)} %slice.9), channel_id=1, source_target_pairs={{0,6},{1,7},{2,0},{3,1},{4,2},{5,3},{6,4},{7,5},{8,14},{9,15},{10,... | collective-permute-start | bytes 1572872 | tf_op jit(solution)/shard_map/ppermute | solution.py:323
  51.2 1.0 copy-start.5
  51.2 4.2 %copy-start.4 = (bf16[256,512]{1,0:T(8,128)(2,1)S(1)}, bf16[256,512]{1,0:T(8,128)(2,1)}, u32[]{:S(2)}) copy-start(bf16[256,512]{1,0:T(8,128)(2,1)} %get-tuple-element.88) | copy-start | bytes 786436
  51.3 4.2 %copy-start.3 = (bf16[256,512]{1,0:T(8,128)(2,1)S(1)}, bf16[256,512]{1,0:T(8,128)(2,1)}, u32[]{:S(2)}) copy-start(bf16[256,512]{1,0:T(8,128)(2,1)} %get-tuple-element.89) | copy-start | bytes 786436
  51.3 5.6 %copy-start.1 = (bf16[256,512]{1,0:T(8,128)(2,1)S(1)}, bf16[256,512]{1,0:T(8,128)(2,1)}, u32[]{:S(2)}) copy-start(bf16[256,512]{1,0:T(8,128)(2,1)} %get-tuple-element.77.refs_3_.refs_2_) | copy-start | bytes 786436
  52.2 21.6 %collective-permute-start.10 = (bf16[256,512]{1,0:T(8,128)(2,1)S(1)}, bf16[256,512]{1,0:T(8,128)(2,1)S(1)}, u32[]{:S(2)}, u32[]{:S(2)}) collective-permute-start(bf16[256,512]{1,0:T(8,128)(2,1)S(1)} %copy-done.5), channel_id=1, source_target_pairs={{0,25},{1,24},{2,27},{3,26},{4,29},{5,28},{6,31},{7,30},{8,1},{9,0... | collective-permute-start | bytes 786440 | tf_op jit(solution)/shard_map/ppermute | solution.py:333
  55.5 18.3 %collective-permute-start.8 = (bf16[256,512]{1,0:T(8,128)(2,1)S(1)}, bf16[256,512]{1,0:T(8,128)(2,1)S(1)}, u32[]{:S(2)}, u32[]{:S(2)}) collective-permute-start(bf16[256,512]{1,0:T(8,128)(2,1)S(1)} %copy-done.4), channel_id=1, source_target_pairs={{0,9},{1,8},{2,11},{3,10},{4,13},{5,12},{6,15},{7,14},{8,17},{9,16... | collective-permute-start | bytes 786440 | tf_op jit(solution)/shard_map/ppermute | solution.py:333
  55.5 18.3 %collective-permute-start.9 = (bf16[256,512]{1,0:T(8,128)(2,1)S(1)}, bf16[256,512]{1,0:T(8,128)(2,1)S(1)}, u32[]{:S(2)}, u32[]{:S(2)}) collective-permute-start(bf16[256,512]{1,0:T(8,128)(2,1)S(1)} %copy-done.3), channel_id=1, source_target_pairs={{0,17},{1,16},{2,19},{3,18},{4,21},{5,20},{6,23},{7,22},{8,25},{9,... | collective-permute-start | bytes 786440 | tf_op jit(solution)/shard_map/ppermute | solution.py:333
  73.8 16.5 %collective-permute-start.11 = (bf16[256,512]{1,0:T(8,128)(2,1)S(1)}, bf16[256,512]{1,0:T(8,128)(2,1)S(1)}, u32[]{:S(2)}, u32[]{:S(2)}) collective-permute-start(bf16[256,512]{1,0:T(8,128)(2,1)S(1)} %get-tuple-element.100), channel_id=1, source_target_pairs={{0,24},{1,25},{2,26},{3,27},{4,28},{5,29},{6,30},{7,31},{8,0},{9,1... | collective-permute-start | bytes 786440 | tf_op jit(solution)/shard_map/ppermute | solution.py:357
  76.0 14.3 %collective-permute-start.12 = (bf16[256,512]{1,0:T(8,128)(2,1)S(1)}, bf16[256,512]{1,0:T(8,128)(2,1)S(1)}, u32[]{:S(2)}, u32[]{:S(2)}) collective-permute-start(bf16[256,512]{1,0:T(8,128)(2,1)S(1)} %get-tuple-element.101), channel_id=1, source_target_pairs={{0,16},{1,17},{2,18},{3,19},{4,20},{5,21},{6,22},{7,23},{8,24},{9,... | collective-permute-start | bytes 786440 | tf_op jit(solution)/shard_map/ppermute | solution.py:357
  77.8 13.5 %collective-permute-start.13 = (bf16[256,512]{1,0:T(8,128)(2,1)S(1)}, bf16[256,512]{1,0:T(8,128)(2,1)S(1)}, u32[]{:S(2)}, u32[]{:S(2)}) collective-permute-start(bf16[256,512]{1,0:T(8,128)(2,1)S(1)} %get-tuple-element.102), channel_id=1, source_target_pairs={{0,8},{1,9},{2,10},{3,11},{4,12},{5,13},{6,14},{7,15},{8,16},{9,17... | collective-permute-start | bytes 786440 | tf_op jit(solution)/shard_map/ppermute | solution.py:357
  91.3 3.2 %collective-permute-start.14 = (bf16[256,512]{1,0:T(8,128)(2,1)S(1)}, bf16[256,512]{1,0:T(8,128)(2,1)S(1)}, u32[]{:S(2)}, u32[]{:S(2)}) collective-permute-start(bf16[256,512]{1,0:T(8,128)(2,1)S(1)} %get-tuple-element.107), channel_id=1, source_target_pairs={{0,1},{1,0},{2,3},{3,2},{4,5},{5,4},{6,7},{7,6},{8,9},{9,8},{10,11... | collective-permute-start | bytes 786440 | tf_op jit(solution)/shard_map/ppermute | solution.py:357
  91.7 8.8 %collective-permute-start.15 = (bf16[256,512]{1,0:T(8,128)(2,1)S(1)}, bf16[256,512]{1,0:T(8,128)(2,1)S(1)}, u32[]{:S(2)}, u32[]{:S(2)}) collective-permute-start(bf16[256,512]{1,0:T(8,128)(2,1)S(1)} %get-tuple-element.108), channel_id=1, source_target_pairs={{0,25},{1,24},{2,27},{3,26},{4,29},{5,28},{6,31},{7,30},{8,1},{9,0... | collective-permute-start | bytes 786440 | tf_op jit(solution)/shard_map/ppermute | solution.py:357
  93.6 10.1 %collective-permute-start.16 = (bf16[256,512]{1,0:T(8,128)(2,1)S(1)}, bf16[256,512]{1,0:T(8,128)(2,1)S(1)}, u32[]{:S(2)}, u32[]{:S(2)}) collective-permute-start(bf16[256,512]{1,0:T(8,128)(2,1)S(1)} %get-tuple-element.109), channel_id=1, source_target_pairs={{0,17},{1,16},{2,19},{3,18},{4,21},{5,20},{6,23},{7,22},{8,25},{9,... | collective-permute-start | bytes 786440 | tf_op jit(solution)/shard_map/ppermute | solution.py:357
  93.7 15.2 %collective-permute-start.17 = (bf16[256,512]{1,0:T(8,128)(2,1)S(1)}, bf16[256,512]{1,0:T(8,128)(2,1)S(1)}, u32[]{:S(2)}, u32[]{:S(2)}) collective-permute-start(bf16[256,512]{1,0:T(8,128)(2,1)S(1)} %get-tuple-element.110), channel_id=1, source_target_pairs={{0,9},{1,8},{2,11},{3,10},{4,13},{5,12},{6,15},{7,14},{8,17},{9,16... | collective-permute-start | bytes 786440 | tf_op jit(solution)/shard_map/ppermute | solution.py:357
  103.7 5.2 %copy-start.2 = (bf16[256,4096]{1,0:T(8,128)(2,1)}, bf16[256,4096]{1,0:T(8,128)(2,1)S(1)}, u32[]{:S(2)}) copy-start(bf16[256,4096]{1,0:T(8,128)(2,1)S(1)} %constant_dynamic-update-slice_fusion.1) | copy-start | bytes 6291460

commit v5 on v4

--- a/solution.py
+++ b/solution.py
@@ -31,7 +31,7 @@
 FAR = ((2, 0, YS // 2), (2, YS // 2, YS // 2))
 PARTS = {"near": ((0, 0, YS), (XS - 1, 0, YS), (1, 0, YS)), "far": FAR}
 PARTS["all"] = PARTS["near"] + FAR
-STEPS = [(dy, dc) for dc in range(CS) for dy in range(YS)]
+STEPS = [(dy, int(dy == 0) ^ half) for half in range(CS) for dy in range(YS)]
 
 
 def ctx_index(y, x, c):
@@ -83,7 +83,7 @@
         part[...] = queries[:, pl.ds(column, GROUP)]
 
 
-def attend_kernel(pieces, dc, which, rank, doc_lengths, marks, *refs):
+def attend_kernel(pieces, half, which, rank, doc_lengths, marks, *refs):
     parts = PARTS[which]
     part_refs, refs = refs[: len(parts)], refs[len(parts) :]
     q_refs, refs = refs[:pieces], refs[pieces:]
@@ -174,6 +174,7 @@
 
     @pl.loop(0, pieces)
     def _(p):
+        dc = jnp.where(p == 0, 1 - half, half)
         start = ((((y - p) & (YS - 1)) * XS + x) * CS + (c ^ dc)) * rows
 
         def document(d, so_far):
@@ -269,7 +270,7 @@
             o_refs[p][...] = o_all[p]
 
 
-def attend(dc, which, rank, doc_lengths, marks, parts, q_pieces, state=()):
+def attend(half, which, rank, doc_lengths, marks, parts, q_pieces, state=()):
     pieces = len(q_pieces)
     seq = marks.shape[0]
     held = seq // XS if which == "far" else seq
@@ -284,7 +285,7 @@
     else:
         out_shape = [jax.ShapeDtypeStruct((UNIT, GROUP), jnp.bfloat16)] * pieces
     return pl.pallas_call(
-        functools.partial(attend_kernel, pieces, dc, which),
+        functools.partial(attend_kernel, pieces, half, which),
         out_shape=out_shape,
         in_specs=[smem] * 2 + [vmem] * (1 + len(parts) + pieces + len(state)),
         out_specs=[vmem] * len(out_shape),
@@ -332,13 +333,14 @@
         part = sent[dy, dc]
         return lax.ppermute(part, "ctx", shift(dy, 0, dc)) if dy or dc else part
 
+    first_half, second_half = STEPS[:YS], STEPS[YS:]
     got = {(0, 1): send(0, 1)}
     sent, got = lax.optimization_barrier((sent, got))
-    got |= {(dy, 0): send(dy, 0) for dy in range(YS)}
+    got |= {step: send(*step) for step in first_half if step not in got}
     sent, got = lax.optimization_barrier((sent, got))
-    got |= {(dy, 1): send(dy, 1) for dy in range(1, YS)}
-    half = YS // 2
-    far = (along(left[:half], 1), along(right[half:], XS - 1))
+    got |= {step: send(*step) for step in second_half}
+    some = YS // 2
+    far = (along(left[:some], 1), along(right[some:], XS - 1))
 
     doc_end = jnp.cumsum(doc_lengths)
     doc_first = doc_end - doc_lengths
@@ -348,22 +350,23 @@
     marks = jnp.pad(marks, ((0, 0), (0, DH - marks.shape[1])))
 
     near = (own, left, right)
-    pieces = [got[dy, 0] for dy in range(YS)]
+    pieces = [got[step] for step in first_half]
     state = attend(0, "near", rank, doc_lengths, marks, near, pieces)
     done = attend(0, "far", rank, doc_lengths, marks, far, pieces, state)
 
-    def give(done, dc):
+    def give(done, steps):
         return [
             lax.ppermute(piece, "ctx", shift(YS - dy, 0, dc)) if dy or dc else piece
-            for dy, piece in enumerate(done)
+            for (dy, dc), piece in zip(steps, done, strict=True)
         ]
 
     done, got = lax.optimization_barrier((done, got))
-    outs = give(done, 0)
-    pieces = [got[dy, 1] for dy in range(YS)]
+    outs = give(done, first_half)
+    pieces = [got[step] for step in second_half]
     done = attend(1, "all", rank, doc_lengths, marks, near + far, pieces)
-    done, outs = lax.optimization_barrier((done, outs))
-    outs += give(done, 1)
+    in_chip, *across = outs
+    done, across = lax.optimization_barrier((done, across))
+    outs = [in_chip, *across, *give(done, second_half)]
 
     whole = jnp.zeros((rows, H * DH), jnp.bfloat16)
     for (dy, dc), piece in zip(STEPS, outs, strict=True):

time: 110 us -> 112 us (1.018); the launches traced: 110 us -> 113 us
  Pallas kernels: 34.8 us -> 38.7 us
    pallas_call x3, Pallas kernels: 29.4 us -> 33.3 us  [attend(): pl.pallas_call(functools.partial(attend_kernel, pieces, half, which), out...]
  transfers between devices with their start and end apart: 18 -> 18, of which waited for: 6 -> 4; matrix products, arithmetic and copies ran while one was open for 2% -> 2% of each run, Pallas kernels for 30% -> 32%
where the time goes in v5:
time: 112 us; the launch traced here: 113 us
  Pallas kernels  38.7 us (35%)
  waiting for transfers between devices  28.7 us (26%)
  starting transfers between devices  22.1 us (20%)
  blocking collectives  20.3 us (18%)
  local copies, waits for them, and re-layouts  2.2 us (2%)
    pallas_call x3, Pallas kernels, attend(): pl.pallas_call(functools.partial(attend_kernel, pieces, half, which), out...  33.3 us
    all_to_all x1, blocking collectives, per_device(): lax.all_to_all(pairs, 'ctx', split_axis=0, concat_axis=0, tiled=True, axi...  20.3 us
    ppermute x7, waiting for transfers between devices, give(): lax.ppermute(piece, 'ctx', shift(YS - dy, 0, dc))  14.1 us
    ppermute x4, waiting for transfers between devices, along(): return lax.ppermute(part, 'ctx', shift(0, dx, 0))  13.4 us
    ppermute x7, starting transfers between devices, send(): return lax.ppermute(part, 'ctx', shift(dy, 0, dc)) if dy or dc else part  8.97 us
    ppermute x7, starting transfers between devices, give(): lax.ppermute(piece, 'ctx', shift(YS - dy, 0, dc))  7.71 us
    ppermute x4, starting transfers between devices, along(): return lax.ppermute(part, 'ctx', shift(0, dx, 0))  5.47 us
    pallas_call x2, Pallas kernels, vmem_call(): pl.pallas_call(kernel, out_shape=out_shape, in_specs=[smem] * len(scalars...  5.42 us
  transfers between devices with their start and end apart: 18, of which 4 were waited for; matrix products, arithmetic and copies ran while one was open for 2% of the time, Pallas kernels for 32%

profile of v5, /device:TPU:65, one launch (start us, length us, event | category | flops | bytes accessed | tf_op | source)
XLA Modules:
  0.0 113.4 jit_solution(18427948136191156308)
XLA Ops:
  0.0 2.4 %shard_map.46 = bf16[8,2,256,128]{3,2,1,0:T(8,128)(2,1)} custom-call(bf16[256,1024]{1,0:T(8,128)(2,1)} %keys.1, bf16[256,1024]{1,0:T(8,128)(2,1)} %values.1), custom_call_target="tpu_custom_call" | custom-call | tf_op jit(solution)/shard_map/pallas_call | solution.py:65
  2.4 20.3 %all_to_all.5 = bf16[8,2,256,128]{3,2,1,0:T(8,128)(2,1)S(1)} all-to-all(bf16[8,2,256,128]{3,2,1,0:T(8,128)(2,1)} %shard_map.46), channel_id=1, replica_groups={{0,1,8,9,16,17,24,25},{2,3,10,11,18,19,26,27},{4,5,12,13,20,21,28,29},{..., dimensions={0} | all-to-all | bytes 2097152 | tf_op jit(solution)/shard_map/all_to_all | solution.py:318
  22.7 1.2 %collective-permute-start = (bf16[4,2,2,256,128]{4,3,2,1,0:T(8,128)(2,1)S(1)}, bf16[4,2,2,256,128]{4,3,2,1,0:T(8,128)(2,1)S(1)}, u32[]{:S(2)}, u32[]{:S(2)}) collective-permute-start(bf16[4,2,2,256,128]{4,3,2,1,0:T(8,128)(2,1)S(1)} %bitcast.3), channel_id=1, source_target_pairs={{0,2},{1,3},{2,4},{3,5},{4,6},{5,7},{6,0},{7,1},{8,10},{9,11},{10,... | collective-permute-start | bytes 3145736 | tf_op jit(solution)/shard_map/ppermute | solution.py:324
  23.9 1.5 %collective-permute-start.2 = (bf16[4,2,2,256,128]{4,3,2,1,0:T(8,128)(2,1)S(1)}, bf16[4,2,2,256,128]{4,3,2,1,0:T(8,128)(2,1)S(1)}, u32[]{:S(2)}, u32[]{:S(2)}) collective-permute-start(bf16[4,2,2,256,128]{4,3,2,1,0:T(8,128)(2,1)S(1)} %bitcast.4), channel_id=1, source_target_pairs={{0,6},{1,7},{2,0},{3,1},{4,2},{5,3},{6,4},{7,5},{8,14},{9,15},{10,... | collective-permute-start | bytes 3145736 | tf_op jit(solution)/shard_map/ppermute | solution.py:324
  25.4 3.1 %shard_map.47 = (bf16[256,512]{1,0:T(8,128)(2,1)}, bf16[256,512]{1,0:T(8,128)(2,1)}, bf16[256,512]{1,0:T(8,128)(2,1)}, bf16[256,512]{1,0:T(8,128)(2,1)}, bf16[25...) custom-call(s32[1]{0:T(128)} %bitcast.rank, ...), custom_call_target="tpu_custom_call" | custom-call | tf_op jit(solution)/shard_map/pallas_call | solution.py:65
  28.4 1.6 %collective-permute-start.4 = (bf16[256,512]{1,0:T(8,128)(2,1)}, bf16[256,512]{1,0:T(8,128)(2,1)S(1)}, u32[]{:S(2)}, u32[]{:S(2)}) collective-permute-start(bf16[256,512]{1,0:T(8,128)(2,1)} %get-tuple-element.61), channel_id=1, source_target_pairs={{0,1},{1,0},{2,3},{3,2},{4,5},{5,4},{6,7},{7,6},{8,9},{9,8},{10,11... | collective-permute-start | bytes 786440 | tf_op jit(solution)/shard_map/ppermute | solution.py:334
  30.0 0.1 copy.6
  30.2 0.1 reduce
  30.3 1.1 collective-permute-done.4.refs_3_.refs_2_
  31.4 0.3 collective-permute-start.5
  31.7 1.8 %collective-permute-start.6 = (bf16[256,512]{1,0:T(8,128)(2,1)}, bf16[256,512]{1,0:T(8,128)(2,1)S(1)}, u32[]{:S(2)}, u32[]{:S(2)}) collective-permute-start(bf16[256,512]{1,0:T(8,128)(2,1)} %get-tuple-element.71), channel_id=1, source_target_pairs={{0,16},{1,17},{2,18},{3,19},{4,20},{5,21},{6,22},{7,23},{8,24},{9,... | collective-permute-start | bytes 786440 | tf_op jit(solution)/shard_map/ppermute | solution.py:334
  33.5 0.6 collective-permute-start.7
  34.1 13.4 %collective-permute-done.refs_1_ = bf16[4,2,2,256,128]{4,3,2,1,0:T(8,128)(2,1)S(1)} collective-permute-done((bf16[4,2,2,256,128]{4,3,2,1,0:T(8,128)(2,1)S(1)}, bf16[4,2,2,256,128]{4,3,2,1,0:T(8,128)(2,1)S(1)}, u32[]{:S(2)}, u32[]{:S(2)}) %collective-permute-start) | collective-permute-done | bytes 1048608 | tf_op jit(solution)/shard_map/ppermute | solution.py:324
  47.6 0.1 collective-permute-start.1
  47.6 0.0 collective-permute-done.2.refs_2_
  47.7 2.7 %collective-permute-start.3 = (bf16[2,2,2,256,128]{4,3,2,1,0:T(8,128)(2,1)S(1)}, bf16[2,2,2,256,128]{4,3,2,1,0:T(8,128)(2,1)S(1)}, u32[]{:S(2)}, u32[]{:S(2)}) collective-permute-start(bf16[2,2,2,256,128]{4,3,2,1,0:T(8,128)(2,1)S(1)} %slice.9), channel_id=1, source_target_pairs={{0,6},{1,7},{2,0},{3,1},{4,2},{5,3},{6,4},{7,5},{8,14},{9,15},{10,... | collective-permute-start | bytes 1572872 | tf_op jit(solution)/shard_map/ppermute | solution.py:324
  50.4 0.8 select_convert_fusion
  51.3 0.4 pad.4.marks
  51.7 0.0 collective-permute-done.5.refs_4_.refs_3_
  51.7 0.0 collective-permute-done.6.refs_5_.refs_4_
  51.7 0.0 collective-permute-done.7.refs_6_.refs_5_
  51.7 0.5 copy-done.5
  52.2 3.3 %collective-permute-start.10 = (bf16[256,512]{1,0:T(8,128)(2,1)S(1)}, bf16[256,512]{1,0:T(8,128)(2,1)S(1)}, u32[]{:S(2)}, u32[]{:S(2)}) collective-permute-start(bf16[256,512]{1,0:T(8,128)(2,1)S(1)} %copy-done.5), channel_id=1, source_target_pairs={{0,25},{1,24},{2,27},{3,26},{4,29},{5,28},{6,31},{7,30},{8,1},{9,0... | collective-permute-start | bytes 786440 | tf_op jit(solution)/shard_map/ppermute | solution.py:334
  55.5 0.0 collective-permute-start.8
  55.5 1.4 %collective-permute-start.9 = (bf16[256,512]{1,0:T(8,128)(2,1)S(1)}, bf16[256,512]{1,0:T(8,128)(2,1)S(1)}, u32[]{:S(2)}, u32[]{:S(2)}) collective-permute-start(bf16[256,512]{1,0:T(8,128)(2,1)S(1)} %copy-done.3), channel_id=1, source_target_pairs={{0,17},{1,16},{2,19},{3,18},{4,21},{5,20},{6,23},{7,22},{8,25},{9,... | collective-permute-start | bytes 786440 | tf_op jit(solution)/shard_map/ppermute | solution.py:334
  56.9 13.3 %shard_map.48 = (f32[4,1024,256]{2,1,0:T(8,128)S(1)}, f32[4,1024,128]{2,1,0:T(8,128)S(1)}) custom-call(s32[1]{0:T(128)} %bitcast.rank, s32[16]{0:T(128)S(1)} %copy-done, bf16[8192,128]{1,0:T(8,128)(2,1)S(1)} %pad.4.marks, bf16[4,2,2,256,128]{4,3,2,1,0:T(8,128)(2,1)S(1)} %bitcast.5, bf16[4,2,2,256,128]{4,3,2,1,0:T(8,128)(2,1)S(1)} %collective-permute-done.refs_1_, ...), custom_call_target="tpu_custom_call" | custom-call | flops 4294967296 | bytes 8388608 | tf_op jit(solution)/shard_map/pallas_call | solution.py:287
  70.2 0.0 collective-permute-done.1.refs_0_.refs_3_
  70.2 0.0 collective-permute-done.3.refs_1_.refs_4_
  70.2 5.1 %shard_map.49 = (bf16[256,512]{1,0:T(8,128)(2,1)S(1)}, bf16[256,512]{1,0:T(8,128)(2,1)S(1)}, bf16[256,512]{1,0:T(8,128)(2,1)S(1)}, bf16[256,512]{1,0:T(8,128)(2,1)S(1)}) custom-call(s32[1]{0:T(128)} %bitcast.rank, s32[16]{0:T(128)S(1)} %copy-done, bf16[8192,128]{1,0:T(8,128)(2,1)S(1)} %pad.4.marks, ...), custom_call_target="tpu_custom_call" | custom-call | flops 4294967296 | bytes 8388608 | tf_op jit(solution)/shard_map/pallas_call | solution.py:287
  75.3 0.0 collective-permute-done.10.refs_8_
  75.3 0.0 collective-permute-done.8.refs_6_
  75.3 0.0 collective-permute-done.9.refs_7_
  75.3 2.3 %collective-permute-start.12 = (bf16[256,512]{1,0:T(8,128)(2,1)S(1)}, bf16[256,512]{1,0:T(8,128)(2,1)S(1)}, u32[]{:S(2)}, u32[]{:S(2)}) collective-permute-start(bf16[256,512]{1,0:T(8,128)(2,1)S(1)} %get-tuple-element.99), channel_id=1, source_target_pairs={{0,24},{1,25},{2,26},{3,27},{4,28},{5,29},{6,30},{7,31},{8,0},{9,1... | collective-permute-start | bytes 786440 | tf_op jit(solution)/shard_map/ppermute | solution.py:359
  77.6 1.8 %collective-permute-start.13 = (bf16[256,512]{1,0:T(8,128)(2,1)S(1)}, bf16[256,512]{1,0:T(8,128)(2,1)S(1)}, u32[]{:S(2)}, u32[]{:S(2)}) collective-permute-start(bf16[256,512]{1,0:T(8,128)(2,1)S(1)} %get-tuple-element.100), channel_id=1, source_target_pairs={{0,16},{1,17},{2,18},{3,19},{4,20},{5,21},{6,22},{7,23},{8,24},{9,... | collective-permute-start | bytes 786440 | tf_op jit(solution)/shard_map/ppermute | solution.py:359
  79.4 0.0 collective-permute-start.14
  79.4 0.0 collective-permute-start.11
  79.4 15.0 %shard_map.50 = (bf16[256,512]{1,0:T(8,128)(2,1)S(1)}, bf16[256,512]{1,0:T(8,128)(2,1)S(1)}, bf16[256,512]{1,0:T(8,128)(2,1)S(1)}, bf16[256,512]{1,0:T(8,128)(2,1)S(1)}) custom-call(s32[1]{0:T(128)} %bitcast.rank, s32[16]{0:T(128)S(1)} %copy-done, bf16[8192,128]{1,0:T(8,128)(2,1)S(1)} %pad.4.marks, bf16[4,2,2,256,128]{4,3,2,1,0:T(8,128)(2,1)S(1)} %bitcast.6, ...), custom_call_target="tpu_custom_call" | custom-call | flops 4294967296 | bytes 8388608 | tf_op jit(solution)/shard_map/pallas_call | solution.py:287
  94.4 0.0 collective-permute-done.12
  94.4 0.0 collective-permute-done.13
  94.4 2.6 %collective-permute-start.15 = (bf16[256,512]{1,0:T(8,128)(2,1)S(1)}, bf16[256,512]{1,0:T(8,128)(2,1)S(1)}, u32[]{:S(2)}, u32[]{:S(2)}) collective-permute-start(bf16[256,512]{1,0:T(8,128)(2,1)S(1)} %get-tuple-element.106), channel_id=1, source_target_pairs={{0,25},{1,24},{2,27},{3,26},{4,29},{5,28},{6,31},{7,30},{8,1},{9,0... | collective-permute-start | bytes 786440 | tf_op jit(solution)/shard_map/ppermute | solution.py:359
  97.0 0.1 collective-permute-start.16
  97.1 1.0 collective-permute-start.17
  98.0 0.0 collective-permute-done.11
  98.0 0.2 broadcast_in_dim.17
  98.5 9.5 %collective-permute-done.15 = bf16[256,512]{1,0:T(8,128)(2,1)S(1)} collective-permute-done((bf16[256,512]{1,0:T(8,128)(2,1)S(1)}, bf16[256,512]{1,0:T(8,128)(2,1)S(1)}, u32[]{:S(2)}, u32[]{:S(2)}) %collective-permute-start.15) | collective-permute-done | bytes 262176 | tf_op jit(solution)/shard_map/ppermute | solution.py:359
  108.0 0.0 copy-start.2
  108.0 4.6 %collective-permute-done.17 = bf16[256,512]{1,0:T(8,128)(2,1)S(1)} collective-permute-done((bf16[256,512]{1,0:T(8,128)(2,1)S(1)}, bf16[256,512]{1,0:T(8,128)(2,1)S(1)}, u32[]{:S(2)}, u32[]{:S(2)}) %collective-permute-start.17) | collective-permute-done | bytes 262176 | tf_op jit(solution)/shard_map/ppermute | solution.py:359
  112.6 0.7 constant_dynamic-update-slice_fusion
  (23 shorter events, 0.3 us)
Async XLA Ops:
  2.4 27.7 %copy-start = (s32[16]{0:T(128)S(1)}, s32[16]{0:T(128)}, u32[]{:S(2)}) copy-start(s32[16]{0:T(128)} %doc_lengths.2) | copy-start | bytes 196
  22.7 24.8 %collective-permute-start = (bf16[4,2,2,256,128]{4,3,2,1,0:T(8,128)(2,1)S(1)}, bf16[4,2,2,256,128]{4,3,2,1,0:T(8,128)(2,1)S(1)}, u32[]{:S(2)}, u32[]{:S(2)}) collective-permute-start(bf16[4,2,2,256,128]{4,3,2,1,0:T(8,128)(2,1)S(1)} %bitcast.3), channel_id=1, source_target_pairs={{0,2},{1,3},{2,4},{3,5},{4,6},{5,7},{6,0},{7,1},{8,10},{9,11},{10,... | collective-permute-start | bytes 3145736 | tf_op jit(solution)/shard_map/ppermute | solution.py:324
  23.9 23.7 %collective-permute-start.2 = (bf16[4,2,2,256,128]{4,3,2,1,0:T(8,128)(2,1)S(1)}, bf16[4,2,2,256,128]{4,3,2,1,0:T(8,128)(2,1)S(1)}, u32[]{:S(2)}, u32[]{:S(2)}) collective-permute-start(bf16[4,2,2,256,128]{4,3,2,1,0:T(8,128)(2,1)S(1)} %bitcast.4), channel_id=1, source_target_pairs={{0,6},{1,7},{2,0},{3,1},{4,2},{5,3},{6,4},{7,5},{8,14},{9,15},{10,... | collective-permute-start | bytes 3145736 | tf_op jit(solution)/shard_map/ppermute | solution.py:324
  28.4 3.0 %collective-permute-start.4 = (bf16[256,512]{1,0:T(8,128)(2,1)}, bf16[256,512]{1,0:T(8,128)(2,1)S(1)}, u32[]{:S(2)}, u32[]{:S(2)}) collective-permute-start(bf16[256,512]{1,0:T(8,128)(2,1)} %get-tuple-element.61), channel_id=1, source_target_pairs={{0,1},{1,0},{2,3},{3,2},{4,5},{5,4},{6,7},{7,6},{8,9},{9,8},{10,11... | collective-permute-start | bytes 786440 | tf_op jit(solution)/shard_map/ppermute | solution.py:334
  31.4 20.3 %collective-permute-start.5 = (bf16[256,512]{1,0:T(8,128)(2,1)}, bf16[256,512]{1,0:T(8,128)(2,1)S(1)}, u32[]{:S(2)}, u32[]{:S(2)}) collective-permute-start(bf16[256,512]{1,0:T(8,128)(2,1)} %get-tuple-element.69), channel_id=1, source_target_pairs={{0,8},{1,9},{2,10},{3,11},{4,12},{5,13},{6,14},{7,15},{8,16},{9,17... | collective-permute-start | bytes 786440 | tf_op jit(solution)/shard_map/ppermute | solution.py:334
  31.7 20.0 %collective-permute-start.6 = (bf16[256,512]{1,0:T(8,128)(2,1)}, bf16[256,512]{1,0:T(8,128)(2,1)S(1)}, u32[]{:S(2)}, u32[]{:S(2)}) collective-permute-start(bf16[256,512]{1,0:T(8,128)(2,1)} %get-tuple-element.71), channel_id=1, source_target_pairs={{0,16},{1,17},{2,18},{3,19},{4,20},{5,21},{6,22},{7,23},{8,24},{9,... | collective-permute-start | bytes 786440 | tf_op jit(solution)/shard_map/ppermute | solution.py:334
  33.5 18.2 %collective-permute-start.7 = (bf16[256,512]{1,0:T(8,128)(2,1)}, bf16[256,512]{1,0:T(8,128)(2,1)S(1)}, u32[]{:S(2)}, u32[]{:S(2)}) collective-permute-start(bf16[256,512]{1,0:T(8,128)(2,1)} %get-tuple-element.73), channel_id=1, source_target_pairs={{0,24},{1,25},{2,26},{3,27},{4,28},{5,29},{6,30},{7,31},{8,0},{9,1... | collective-permute-start | bytes 786440 | tf_op jit(solution)/shard_map/ppermute | solution.py:334
  47.6 22.6 %collective-permute-start.1 = (bf16[2,2,2,256,128]{4,3,2,1,0:T(8,128)(2,1)S(1)}, bf16[2,2,2,256,128]{4,3,2,1,0:T(8,128)(2,1)S(1)}, u32[]{:S(2)}, u32[]{:S(2)}) collective-permute-start(bf16[2,2,2,256,128]{4,3,2,1,0:T(8,128)(2,1)S(1)} %slice.8), channel_id=1, source_target_pairs={{0,2},{1,3},{2,4},{3,5},{4,6},{5,7},{6,0},{7,1},{8,10},{9,11},{10,... | collective-permute-start | bytes 1572872 | tf_op jit(solution)/shard_map/ppermute | solution.py:324
  47.7 22.5 %collective-permute-start.3 = (bf16[2,2,2,256,128]{4,3,2,1,0:T(8,128)(2,1)S(1)}, bf16[2,2,2,256,128]{4,3,2,1,0:T(8,128)(2,1)S(1)}, u32[]{:S(2)}, u32[]{:S(2)}) collective-permute-start(bf16[2,2,2,256,128]{4,3,2,1,0:T(8,128)(2,1)S(1)} %slice.9), channel_id=1, source_target_pairs={{0,6},{1,7},{2,0},{3,1},{4,2},{5,3},{6,4},{7,5},{8,14},{9,15},{10,... | collective-permute-start | bytes 1572872 | tf_op jit(solution)/shard_map/ppermute | solution.py:324
  51.2 1.0 copy-start.5
  51.2 4.2 %copy-start.4 = (bf16[256,512]{1,0:T(8,128)(2,1)S(1)}, bf16[256,512]{1,0:T(8,128)(2,1)}, u32[]{:S(2)}) copy-start(bf16[256,512]{1,0:T(8,128)(2,1)} %get-tuple-element.87) | copy-start | bytes 786436
  51.3 4.2 %copy-start.3 = (bf16[256,512]{1,0:T(8,128)(2,1)S(1)}, bf16[256,512]{1,0:T(8,128)(2,1)}, u32[]{:S(2)}) copy-start(bf16[256,512]{1,0:T(8,128)(2,1)} %get-tuple-element.88) | copy-start | bytes 786436
  52.2 23.1 %collective-permute-start.10 = (bf16[256,512]{1,0:T(8,128)(2,1)S(1)}, bf16[256,512]{1,0:T(8,128)(2,1)S(1)}, u32[]{:S(2)}, u32[]{:S(2)}) collective-permute-start(bf16[256,512]{1,0:T(8,128)(2,1)S(1)} %copy-done.5), channel_id=1, source_target_pairs={{0,25},{1,24},{2,27},{3,26},{4,29},{5,28},{6,31},{7,30},{8,1},{9,0... | collective-permute-start | bytes 786440 | tf_op jit(solution)/shard_map/ppermute | solution.py:334
  55.5 19.8 %collective-permute-start.8 = (bf16[256,512]{1,0:T(8,128)(2,1)S(1)}, bf16[256,512]{1,0:T(8,128)(2,1)S(1)}, u32[]{:S(2)}, u32[]{:S(2)}) collective-permute-start(bf16[256,512]{1,0:T(8,128)(2,1)S(1)} %copy-done.4), channel_id=1, source_target_pairs={{0,9},{1,8},{2,11},{3,10},{4,13},{5,12},{6,15},{7,14},{8,17},{9,16... | collective-permute-start | bytes 786440 | tf_op jit(solution)/shard_map/ppermute | solution.py:334
  55.5 19.8 %collective-permute-start.9 = (bf16[256,512]{1,0:T(8,128)(2,1)S(1)}, bf16[256,512]{1,0:T(8,128)(2,1)S(1)}, u32[]{:S(2)}, u32[]{:S(2)}) collective-permute-start(bf16[256,512]{1,0:T(8,128)(2,1)S(1)} %copy-done.3), channel_id=1, source_target_pairs={{0,17},{1,16},{2,19},{3,18},{4,21},{5,20},{6,23},{7,22},{8,25},{9,... | collective-permute-start | bytes 786440 | tf_op jit(solution)/shard_map/ppermute | solution.py:334
  70.2 9.2 %copy-start.1 = (bf16[256,512]{1,0:T(8,128)(2,1)S(1)}, bf16[256,512]{1,0:T(8,128)(2,1)}, u32[]{:S(2)}) copy-start(bf16[256,512]{1,0:T(8,128)(2,1)} %get-tuple-element.91.refs_5_) | copy-start | bytes 786436
  75.3 19.0 %collective-permute-start.12 = (bf16[256,512]{1,0:T(8,128)(2,1)S(1)}, bf16[256,512]{1,0:T(8,128)(2,1)S(1)}, u32[]{:S(2)}, u32[]{:S(2)}) collective-permute-start(bf16[256,512]{1,0:T(8,128)(2,1)S(1)} %get-tuple-element.99), channel_id=1, source_target_pairs={{0,24},{1,25},{2,26},{3,27},{4,28},{5,29},{6,30},{7,31},{8,0},{9,1... | collective-permute-start | bytes 786440 | tf_op jit(solution)/shard_map/ppermute | solution.py:359
  77.6 16.8 %collective-permute-start.13 = (bf16[256,512]{1,0:T(8,128)(2,1)S(1)}, bf16[256,512]{1,0:T(8,128)(2,1)S(1)}, u32[]{:S(2)}, u32[]{:S(2)}) collective-permute-start(bf16[256,512]{1,0:T(8,128)(2,1)S(1)} %get-tuple-element.100), channel_id=1, source_target_pairs={{0,16},{1,17},{2,18},{3,19},{4,20},{5,21},{6,22},{7,23},{8,24},{9,... | collective-permute-start | bytes 786440 | tf_op jit(solution)/shard_map/ppermute | solution.py:359
  79.4 15.0 %collective-permute-start.14 = (bf16[256,512]{1,0:T(8,128)(2,1)S(1)}, bf16[256,512]{1,0:T(8,128)(2,1)S(1)}, u32[]{:S(2)}, u32[]{:S(2)}) collective-permute-start(bf16[256,512]{1,0:T(8,128)(2,1)S(1)} %get-tuple-element.101), channel_id=1, source_target_pairs={{0,8},{1,9},{2,10},{3,11},{4,12},{5,13},{6,14},{7,15},{8,16},{9,17... | collective-permute-start | bytes 786440 | tf_op jit(solution)/shard_map/ppermute | solution.py:359
  79.4 18.7 %collective-permute-start.11 = (bf16[256,512]{1,0:T(8,128)(2,1)S(1)}, bf16[256,512]{1,0:T(8,128)(2,1)S(1)}, u32[]{:S(2)}, u32[]{:S(2)}) collective-permute-start(bf16[256,512]{1,0:T(8,128)(2,1)S(1)} %get-tuple-element.90), channel_id=1, source_target_pairs={{0,1},{1,0},{2,3},{3,2},{4,5},{5,4},{6,7},{7,6},{8,9},{9,8},{10,11... | collective-permute-start | bytes 786440 | tf_op jit(solution)/shard_map/ppermute | solution.py:359
  94.4 13.5 %collective-permute-start.15 = (bf16[256,512]{1,0:T(8,128)(2,1)S(1)}, bf16[256,512]{1,0:T(8,128)(2,1)S(1)}, u32[]{:S(2)}, u32[]{:S(2)}) collective-permute-start(bf16[256,512]{1,0:T(8,128)(2,1)S(1)} %get-tuple-element.106), channel_id=1, source_target_pairs={{0,25},{1,24},{2,27},{3,26},{4,29},{5,28},{6,31},{7,30},{8,1},{9,0... | collective-permute-start | bytes 786440 | tf_op jit(solution)/shard_map/ppermute | solution.py:359
  97.0 11.0 %collective-permute-start.16 = (bf16[256,512]{1,0:T(8,128)(2,1)S(1)}, bf16[256,512]{1,0:T(8,128)(2,1)S(1)}, u32[]{:S(2)}, u32[]{:S(2)}) collective-permute-start(bf16[256,512]{1,0:T(8,128)(2,1)S(1)} %get-tuple-element.107), channel_id=1, source_target_pairs={{0,17},{1,16},{2,19},{3,18},{4,21},{5,20},{6,23},{7,22},{8,25},{9,... | collective-permute-start | bytes 786440 | tf_op jit(solution)/shard_map/ppermute | solution.py:359
  97.1 15.6 %collective-permute-start.17 = (bf16[256,512]{1,0:T(8,128)(2,1)S(1)}, bf16[256,512]{1,0:T(8,128)(2,1)S(1)}, u32[]{:S(2)}, u32[]{:S(2)}) collective-permute-start(bf16[256,512]{1,0:T(8,128)(2,1)S(1)} %get-tuple-element.108), channel_id=1, source_target_pairs={{0,9},{1,8},{2,11},{3,10},{4,13},{5,12},{6,15},{7,14},{8,17},{9,16... | collective-permute-start | bytes 786440 | tf_op jit(solution)/shard_map/ppermute | solution.py:359
  108.0 4.6 %copy-start.2 = (bf16[256,4096]{1,0:T(8,128)(2,1)}, bf16[256,4096]{1,0:T(8,128)(2,1)S(1)}, u32[]{:S(2)}) copy-start(bf16[256,4096]{1,0:T(8,128)(2,1)S(1)} %constant_dynamic-update-slice_fusion.1) | copy-start | bytes 6291460

commit v6 on v5

--- a/solution.py
+++ b/solution.py
@@ -343,11 +343,12 @@
     far = (along(left[:some], 1), along(right[some:], XS - 1))
 
     doc_end = jnp.cumsum(doc_lengths)
-    doc_first = doc_end - doc_lengths
+    none = jnp.zeros((DH - doc_end.shape[0],), jnp.int32)
+    doc_first = jnp.concatenate([doc_end - doc_lengths, none])
+    doc_end = jnp.concatenate([doc_end, none])
     positions = jnp.arange(seq, dtype=jnp.int32)[:, None]
     inside = (doc_first[None, :] <= positions) & (positions < doc_end[None, :])
     marks = jnp.where(inside, MARK, 0.0).astype(jnp.bfloat16)
-    marks = jnp.pad(marks, ((0, 0), (0, DH - marks.shape[1])))
 
     near = (own, left, right)
     pieces = [got[step] for step in first_half]

time: 112 us -> 110 us (0.982); the launches traced: 113 us -> 109 us
  Pallas kernels: 38.7 us -> 34.4 us
    pallas_call x3, Pallas kernels: 33.3 us -> 29 us  [attend(): pl.pallas_call(functools.partial(attend_kernel, pieces, half, which), out...]
  transfers between devices with their start and end apart: 18 -> 18, of which waited for: 4 -> 5; matrix products, arithmetic and copies ran while one was open for 2% -> 1% of each run, Pallas kernels for 32% -> 29%
where the time goes in v6:
time: 110 us; the launch traced here: 109 us
  Pallas kernels  34.4 us (31%)
  waiting for transfers between devices  29.1 us (26%)
  starting transfers between devices  22.3 us (20%)
  blocking collectives  20.3 us (18%)
  local copies, waits for them, and re-layouts  1.33 us (1%)
    pallas_call x3, Pallas kernels, attend(): pl.pallas_call(functools.partial(attend_kernel, pieces, half, which), out...  29 us
    all_to_all x1, blocking collectives, per_device(): lax.all_to_all(pairs, 'ctx', split_axis=0, concat_axis=0, tiled=True, axi...  20.3 us
    ppermute x7, waiting for transfers between devices, give(): lax.ppermute(piece, 'ctx', shift(YS - dy, 0, dc))  14.6 us
    ppermute x4, waiting for transfers between devices, along(): return lax.ppermute(part, 'ctx', shift(0, dx, 0))  13.3 us
    ppermute x7, starting transfers between devices, send(): return lax.ppermute(part, 'ctx', shift(dy, 0, dc)) if dy or dc else part  9.12 us
    ppermute x7, starting transfers between devices, give(): lax.ppermute(piece, 'ctx', shift(YS - dy, 0, dc))  7.67 us
    ppermute x4, starting transfers between devices, along(): return lax.ppermute(part, 'ctx', shift(0, dx, 0))  5.47 us
    pallas_call x2, Pallas kernels, vmem_call(): pl.pallas_call(kernel, out_shape=out_shape, in_specs=[smem] * len(scalars...  5.42 us
  transfers between devices with their start and end apart: 18, of which 5 were waited for; matrix products, arithmetic and copies ran while one was open for 1% of the time, Pallas kernels for 29%

profile of v6, /device:TPU:65, one launch (start us, length us, event | category | flops | bytes accessed | tf_op | source)
XLA Modules:
  0.0 108.7 jit_solution(728460007475991392)
XLA Ops:
  0.0 2.4 %shard_map.46 = bf16[8,2,256,128]{3,2,1,0:T(8,128)(2,1)} custom-call(bf16[256,1024]{1,0:T(8,128)(2,1)} %keys.1, bf16[256,1024]{1,0:T(8,128)(2,1)} %values.1), custom_call_target="tpu_custom_call" | custom-call | tf_op jit(solution)/shard_map/pallas_call | solution.py:65
  2.4 20.3 %all_to_all.5 = bf16[8,2,256,128]{3,2,1,0:T(8,128)(2,1)S(1)} all-to-all(bf16[8,2,256,128]{3,2,1,0:T(8,128)(2,1)} %shard_map.46), channel_id=1, replica_groups={{0,1,8,9,16,17,24,25},{2,3,10,11,18,19,26,27},{4,5,12,13,20,21,28,29},{..., dimensions={0} | all-to-all | bytes 2097152 | tf_op jit(solution)/shard_map/all_to_all | solution.py:318
  22.7 1.2 %collective-permute-start = (bf16[4,2,2,256,128]{4,3,2,1,0:T(8,128)(2,1)S(1)}, bf16[4,2,2,256,128]{4,3,2,1,0:T(8,128)(2,1)S(1)}, u32[]{:S(2)}, u32[]{:S(2)}) collective-permute-start(bf16[4,2,2,256,128]{4,3,2,1,0:T(8,128)(2,1)S(1)} %bitcast.3), channel_id=1, source_target_pairs={{0,2},{1,3},{2,4},{3,5},{4,6},{5,7},{6,0},{7,1},{8,10},{9,11},{10,... | collective-permute-start | bytes 3145736 | tf_op jit(solution)/shard_map/ppermute | solution.py:324
  23.9 1.5 %collective-permute-start.2 = (bf16[4,2,2,256,128]{4,3,2,1,0:T(8,128)(2,1)S(1)}, bf16[4,2,2,256,128]{4,3,2,1,0:T(8,128)(2,1)S(1)}, u32[]{:S(2)}, u32[]{:S(2)}) collective-permute-start(bf16[4,2,2,256,128]{4,3,2,1,0:T(8,128)(2,1)S(1)} %bitcast.4), channel_id=1, source_target_pairs={{0,6},{1,7},{2,0},{3,1},{4,2},{5,3},{6,4},{7,5},{8,14},{9,15},{10,... | collective-permute-start | bytes 3145736 | tf_op jit(solution)/shard_map/ppermute | solution.py:324
  25.4 3.1 %shard_map.47 = (bf16[256,512]{1,0:T(8,128)(2,1)}, bf16[256,512]{1,0:T(8,128)(2,1)}, bf16[256,512]{1,0:T(8,128)(2,1)}, bf16[256,512]{1,0:T(8,128)(2,1)}, bf16[25...) custom-call(s32[1]{0:T(128)} %bitcast.rank, ...), custom_call_target="tpu_custom_call" | custom-call | tf_op jit(solution)/shard_map/pallas_call | solution.py:65
  28.4 1.6 %collective-permute-start.4 = (bf16[256,512]{1,0:T(8,128)(2,1)}, bf16[256,512]{1,0:T(8,128)(2,1)S(1)}, u32[]{:S(2)}, u32[]{:S(2)}) collective-permute-start(bf16[256,512]{1,0:T(8,128)(2,1)} %get-tuple-element.61), channel_id=1, source_target_pairs={{0,1},{1,0},{2,3},{3,2},{4,5},{5,4},{6,7},{7,6},{8,9},{9,8},{10,11... | collective-permute-start | bytes 786440 | tf_op jit(solution)/shard_map/ppermute | solution.py:334
  30.0 0.1 copy.6
  30.2 0.1 reduce
  30.3 1.1 %collective-permute-done.4.refs_3_.refs_2_ = bf16[256,512]{1,0:T(8,128)(2,1)S(1)} collective-permute-done((bf16[256,512]{1,0:T(8,128)(2,1)}, bf16[256,512]{1,0:T(8,128)(2,1)S(1)}, u32[]{:S(2)}, u32[]{:S(2)}) %collective-permute-start.4) | collective-permute-done | bytes 262176 | tf_op jit(solution)/shard_map/ppermute | solution.py:334
  31.4 0.3 collective-permute-start.5
  31.7 1.8 %collective-permute-start.6 = (bf16[256,512]{1,0:T(8,128)(2,1)}, bf16[256,512]{1,0:T(8,128)(2,1)S(1)}, u32[]{:S(2)}, u32[]{:S(2)}) collective-permute-start(bf16[256,512]{1,0:T(8,128)(2,1)} %get-tuple-element.71), channel_id=1, source_target_pairs={{0,16},{1,17},{2,18},{3,19},{4,20},{5,21},{6,22},{7,23},{8,24},{9,... | collective-permute-start | bytes 786440 | tf_op jit(solution)/shard_map/ppermute | solution.py:334
  33.5 0.7 collective-permute-start.7
  34.2 13.3 %collective-permute-done.refs_1_ = bf16[4,2,2,256,128]{4,3,2,1,0:T(8,128)(2,1)S(1)} collective-permute-done((bf16[4,2,2,256,128]{4,3,2,1,0:T(8,128)(2,1)S(1)}, bf16[4,2,2,256,128]{4,3,2,1,0:T(8,128)(2,1)S(1)}, u32[]{:S(2)}, u32[]{:S(2)}) %collective-permute-start) | collective-permute-done | bytes 1048608 | tf_op jit(solution)/shard_map/ppermute | solution.py:324
  47.6 0.1 collective-permute-start.1
  47.6 0.0 collective-permute-done.2.refs_2_
  47.7 2.7 %collective-permute-start.3 = (bf16[2,2,2,256,128]{4,3,2,1,0:T(8,128)(2,1)S(1)}, bf16[2,2,2,256,128]{4,3,2,1,0:T(8,128)(2,1)S(1)}, u32[]{:S(2)}, u32[]{:S(2)}) collective-permute-start(bf16[2,2,2,256,128]{4,3,2,1,0:T(8,128)(2,1)S(1)} %slice.9), channel_id=1, source_target_pairs={{0,6},{1,7},{2,0},{3,1},{4,2},{5,3},{6,4},{7,5},{8,14},{9,15},{10,... | collective-permute-start | bytes 1572872 | tf_op jit(solution)/shard_map/ppermute | solution.py:324
  50.4 0.8 select_convert_fusion.marks
  51.2 0.0 collective-permute-done.5.refs_4_.refs_3_
  51.2 0.0 collective-permute-done.6.refs_5_.refs_4_
  51.3 0.0 collective-permute-done.7.refs_6_.refs_5_
  51.3 3.4 %collective-permute-start.10 = (bf16[256,512]{1,0:T(8,128)(2,1)S(1)}, bf16[256,512]{1,0:T(8,128)(2,1)S(1)}, u32[]{:S(2)}, u32[]{:S(2)}) collective-permute-start(bf16[256,512]{1,0:T(8,128)(2,1)S(1)} %copy-done.5), channel_id=1, source_target_pairs={{0,25},{1,24},{2,27},{3,26},{4,29},{5,28},{6,31},{7,30},{8,1},{9,0... | collective-permute-start | bytes 786440 | tf_op jit(solution)/shard_map/ppermute | solution.py:334
  54.6 0.0 collective-permute-start.8
  54.6 1.4 %collective-permute-start.9 = (bf16[256,512]{1,0:T(8,128)(2,1)S(1)}, bf16[256,512]{1,0:T(8,128)(2,1)S(1)}, u32[]{:S(2)}, u32[]{:S(2)}) collective-permute-start(bf16[256,512]{1,0:T(8,128)(2,1)S(1)} %copy-done.3), channel_id=1, source_target_pairs={{0,17},{1,16},{2,19},{3,18},{4,21},{5,20},{6,23},{7,22},{8,25},{9,... | collective-permute-start | bytes 786440 | tf_op jit(solution)/shard_map/ppermute | solution.py:334
  56.0 11.5 %shard_map.48 = (f32[4,1024,256]{2,1,0:T(8,128)S(1)}, f32[4,1024,128]{2,1,0:T(8,128)S(1)}) custom-call(s32[1]{0:T(128)} %bitcast.rank, s32[16]{0:T(128)S(1)} %copy-done, bf16[8192,128]{1,0:T(8,128)(2,1)S(1)} %select_convert_fusion.marks, bf16[4,2,2,256,128]{4,3,2,1,0:T(8,128)(2,1)S(1)} %bitcast.5, ...), custom_call_target="tpu_custom_call" | custom-call | flops 4294967296 | bytes 8388608 | tf_op jit(solution)/shard_map/pallas_call | solution.py:287
  67.5 0.0 collective-permute-done.1.refs_0_.refs_3_
  67.5 0.0 collective-permute-done.3.refs_1_.refs_4_
  67.5 5.1 %shard_map.49 = (bf16[256,512]{1,0:T(8,128)(2,1)S(1)}, bf16[256,512]{1,0:T(8,128)(2,1)S(1)}, bf16[256,512]{1,0:T(8,128)(2,1)S(1)}, bf16[256,512]{1,0:T(8,128)(2,1)S(1)}) custom-call(s32[1]{0:T(128)} %bitcast.rank, s32[16]{0:T(128)S(1)} %copy-done, bf16[8192,128]{1,0:T(8,128)(2,1)S(1)} %select_convert_fusion.marks, ...), custom_call_target="tpu_custom_call" | custom-call | flops 4294967296 | bytes 8388608 | tf_op jit(solution)/shard_map/pallas_call | solution.py:287
  72.6 0.0 collective-permute-done.10.refs_8_
  72.6 0.0 collective-permute-done.8.refs_6_
  72.6 0.0 collective-permute-done.9.refs_7_
  72.6 2.3 %collective-permute-start.12 = (bf16[256,512]{1,0:T(8,128)(2,1)S(1)}, bf16[256,512]{1,0:T(8,128)(2,1)S(1)}, u32[]{:S(2)}, u32[]{:S(2)}) collective-permute-start(bf16[256,512]{1,0:T(8,128)(2,1)S(1)} %get-tuple-element.99), channel_id=1, source_target_pairs={{0,24},{1,25},{2,26},{3,27},{4,28},{5,29},{6,30},{7,31},{8,0},{9,1... | collective-permute-start | bytes 786440 | tf_op jit(solution)/shard_map/ppermute | solution.py:360
  74.9 1.8 %collective-permute-start.13 = (bf16[256,512]{1,0:T(8,128)(2,1)S(1)}, bf16[256,512]{1,0:T(8,128)(2,1)S(1)}, u32[]{:S(2)}, u32[]{:S(2)}) collective-permute-start(bf16[256,512]{1,0:T(8,128)(2,1)S(1)} %get-tuple-element.100), channel_id=1, source_target_pairs={{0,16},{1,17},{2,18},{3,19},{4,20},{5,21},{6,22},{7,23},{8,24},{9,... | collective-permute-start | bytes 786440 | tf_op jit(solution)/shard_map/ppermute | solution.py:360
  76.7 0.0 collective-permute-start.14
  76.7 0.0 collective-permute-start.11
  76.7 12.5 %shard_map.50 = (bf16[256,512]{1,0:T(8,128)(2,1)S(1)}, bf16[256,512]{1,0:T(8,128)(2,1)S(1)}, bf16[256,512]{1,0:T(8,128)(2,1)S(1)}, bf16[256,512]{1,0:T(8,128)(2,1)S(1)}) custom-call(s32[1]{0:T(128)} %bitcast.rank, s32[16]{0:T(128)S(1)} %copy-done, bf16[8192,128]{1,0:T(8,128)(2,1)S(1)} %select_convert_fusion.marks, bf16[4,2,2,256,128]{4,3,2,1,0:T(8,128)(2,1)S(1)} %bitcast.6, ...), custom_call_target="tpu_custom_call" | custom-call | flops 4294967296 | bytes 8388608 | tf_op jit(solution)/shard_map/pallas_call | solution.py:287
  89.2 0.0 collective-permute-done.12
  89.2 0.0 collective-permute-done.13
  89.2 1.1 %collective-permute-done.14 = bf16[256,512]{1,0:T(8,128)(2,1)S(1)} collective-permute-done((bf16[256,512]{1,0:T(8,128)(2,1)S(1)}, bf16[256,512]{1,0:T(8,128)(2,1)S(1)}, u32[]{:S(2)}, u32[]{:S(2)}) %collective-permute-start.14) | collective-permute-done | bytes 262176 | tf_op jit(solution)/shard_map/ppermute | solution.py:360
  90.3 3.3 %collective-permute-start.15 = (bf16[256,512]{1,0:T(8,128)(2,1)S(1)}, bf16[256,512]{1,0:T(8,128)(2,1)S(1)}, u32[]{:S(2)}, u32[]{:S(2)}) collective-permute-start(bf16[256,512]{1,0:T(8,128)(2,1)S(1)} %get-tuple-element.106), channel_id=1, source_target_pairs={{0,25},{1,24},{2,27},{3,26},{4,29},{5,28},{6,31},{7,30},{8,1},{9,0... | collective-permute-start | bytes 786440 | tf_op jit(solution)/shard_map/ppermute | solution.py:360
  93.6 0.0 collective-permute-start.16
  93.6 0.3 collective-permute-start.17
  93.9 0.0 collective-permute-done.11
  93.9 0.2 broadcast_in_dim.18
  94.4 10.2 %collective-permute-done.15 = bf16[256,512]{1,0:T(8,128)(2,1)S(1)} collective-permute-done((bf16[256,512]{1,0:T(8,128)(2,1)S(1)}, bf16[256,512]{1,0:T(8,128)(2,1)S(1)}, u32[]{:S(2)}, u32[]{:S(2)}) %collective-permute-start.15) | collective-permute-done | bytes 262176 | tf_op jit(solution)/shard_map/ppermute | solution.py:360
  104.6 0.0 collective-permute-done.16
  104.6 0.0 copy-start.2
  104.6 3.3 %collective-permute-done.17 = bf16[256,512]{1,0:T(8,128)(2,1)S(1)} collective-permute-done((bf16[256,512]{1,0:T(8,128)(2,1)S(1)}, bf16[256,512]{1,0:T(8,128)(2,1)S(1)}, u32[]{:S(2)}, u32[]{:S(2)}) %collective-permute-start.17) | collective-permute-done | bytes 262176 | tf_op jit(solution)/shard_map/ppermute | solution.py:360
  107.9 0.7 constant_dynamic-update-slice_fusion
  (24 shorter events, 0.3 us)
Async XLA Ops:
  2.4 27.7 %copy-start = (s32[16]{0:T(128)S(1)}, s32[16]{0:T(128)}, u32[]{:S(2)}) copy-start(s32[16]{0:T(128)} %doc_lengths.2) | copy-start | bytes 196
  22.7 24.8 %collective-permute-start = (bf16[4,2,2,256,128]{4,3,2,1,0:T(8,128)(2,1)S(1)}, bf16[4,2,2,256,128]{4,3,2,1,0:T(8,128)(2,1)S(1)}, u32[]{:S(2)}, u32[]{:S(2)}) collective-permute-start(bf16[4,2,2,256,128]{4,3,2,1,0:T(8,128)(2,1)S(1)} %bitcast.3), channel_id=1, source_target_pairs={{0,2},{1,3},{2,4},{3,5},{4,6},{5,7},{6,0},{7,1},{8,10},{9,11},{10,... | collective-permute-start | bytes 3145736 | tf_op jit(solution)/shard_map/ppermute | solution.py:324
  23.9 23.7 %collective-permute-start.2 = (bf16[4,2,2,256,128]{4,3,2,1,0:T(8,128)(2,1)S(1)}, bf16[4,2,2,256,128]{4,3,2,1,0:T(8,128)(2,1)S(1)}, u32[]{:S(2)}, u32[]{:S(2)}) collective-permute-start(bf16[4,2,2,256,128]{4,3,2,1,0:T(8,128)(2,1)S(1)} %bitcast.4), channel_id=1, source_target_pairs={{0,6},{1,7},{2,0},{3,1},{4,2},{5,3},{6,4},{7,5},{8,14},{9,15},{10,... | collective-permute-start | bytes 3145736 | tf_op jit(solution)/shard_map/ppermute | solution.py:324
  28.4 3.0 %collective-permute-start.4 = (bf16[256,512]{1,0:T(8,128)(2,1)}, bf16[256,512]{1,0:T(8,128)(2,1)S(1)}, u32[]{:S(2)}, u32[]{:S(2)}) collective-permute-start(bf16[256,512]{1,0:T(8,128)(2,1)} %get-tuple-element.61), channel_id=1, source_target_pairs={{0,1},{1,0},{2,3},{3,2},{4,5},{5,4},{6,7},{7,6},{8,9},{9,8},{10,11... | collective-permute-start | bytes 786440 | tf_op jit(solution)/shard_map/ppermute | solution.py:334
  31.4 19.9 %copy-start.5 = (bf16[256,512]{1,0:T(8,128)(2,1)S(1)}, bf16[256,512]{1,0:T(8,128)(2,1)}, u32[]{:S(2)}) copy-start(bf16[256,512]{1,0:T(8,128)(2,1)} %get-tuple-element.89) | copy-start | bytes 786436
  31.4 23.2 %copy-start.4 = (bf16[256,512]{1,0:T(8,128)(2,1)S(1)}, bf16[256,512]{1,0:T(8,128)(2,1)}, u32[]{:S(2)}) copy-start(bf16[256,512]{1,0:T(8,128)(2,1)} %get-tuple-element.87) | copy-start | bytes 786436
  31.4 23.2 %copy-start.3 = (bf16[256,512]{1,0:T(8,128)(2,1)S(1)}, bf16[256,512]{1,0:T(8,128)(2,1)}, u32[]{:S(2)}) copy-start(bf16[256,512]{1,0:T(8,128)(2,1)} %get-tuple-element.88) | copy-start | bytes 786436
  31.4 19.8 %collective-permute-start.5 = (bf16[256,512]{1,0:T(8,128)(2,1)}, bf16[256,512]{1,0:T(8,128)(2,1)S(1)}, u32[]{:S(2)}, u32[]{:S(2)}) collective-permute-start(bf16[256,512]{1,0:T(8,128)(2,1)} %get-tuple-element.69), channel_id=1, source_target_pairs={{0,8},{1,9},{2,10},{3,11},{4,12},{5,13},{6,14},{7,15},{8,16},{9,17... | collective-permute-start | bytes 786440 | tf_op jit(solution)/shard_map/ppermute | solution.py:334
  31.7 19.6 %collective-permute-start.6 = (bf16[256,512]{1,0:T(8,128)(2,1)}, bf16[256,512]{1,0:T(8,128)(2,1)S(1)}, u32[]{:S(2)}, u32[]{:S(2)}) collective-permute-start(bf16[256,512]{1,0:T(8,128)(2,1)} %get-tuple-element.71), channel_id=1, source_target_pairs={{0,16},{1,17},{2,18},{3,19},{4,20},{5,21},{6,22},{7,23},{8,24},{9,... | collective-permute-start | bytes 786440 | tf_op jit(solution)/shard_map/ppermute | solution.py:334
  33.5 17.8 %collective-permute-start.7 = (bf16[256,512]{1,0:T(8,128)(2,1)}, bf16[256,512]{1,0:T(8,128)(2,1)S(1)}, u32[]{:S(2)}, u32[]{:S(2)}) collective-permute-start(bf16[256,512]{1,0:T(8,128)(2,1)} %get-tuple-element.73), channel_id=1, source_target_pairs={{0,24},{1,25},{2,26},{3,27},{4,28},{5,29},{6,30},{7,31},{8,0},{9,1... | collective-permute-start | bytes 786440 | tf_op jit(solution)/shard_map/ppermute | solution.py:334
  47.6 19.9 %collective-permute-start.1 = (bf16[2,2,2,256,128]{4,3,2,1,0:T(8,128)(2,1)S(1)}, bf16[2,2,2,256,128]{4,3,2,1,0:T(8,128)(2,1)S(1)}, u32[]{:S(2)}, u32[]{:S(2)}) collective-permute-start(bf16[2,2,2,256,128]{4,3,2,1,0:T(8,128)(2,1)S(1)} %slice.8), channel_id=1, source_target_pairs={{0,2},{1,3},{2,4},{3,5},{4,6},{5,7},{6,0},{7,1},{8,10},{9,11},{10,... | collective-permute-start | bytes 1572872 | tf_op jit(solution)/shard_map/ppermute | solution.py:324
  47.7 19.8 %collective-permute-start.3 = (bf16[2,2,2,256,128]{4,3,2,1,0:T(8,128)(2,1)S(1)}, bf16[2,2,2,256,128]{4,3,2,1,0:T(8,128)(2,1)S(1)}, u32[]{:S(2)}, u32[]{:S(2)}) collective-permute-start(bf16[2,2,2,256,128]{4,3,2,1,0:T(8,128)(2,1)S(1)} %slice.9), channel_id=1, source_target_pairs={{0,6},{1,7},{2,0},{3,1},{4,2},{5,3},{6,4},{7,5},{8,14},{9,15},{10,... | collective-permute-start | bytes 1572872 | tf_op jit(solution)/shard_map/ppermute | solution.py:324
  51.3 21.3 %collective-permute-start.10 = (bf16[256,512]{1,0:T(8,128)(2,1)S(1)}, bf16[256,512]{1,0:T(8,128)(2,1)S(1)}, u32[]{:S(2)}, u32[]{:S(2)}) collective-permute-start(bf16[256,512]{1,0:T(8,128)(2,1)S(1)} %copy-done.5), channel_id=1, source_target_pairs={{0,25},{1,24},{2,27},{3,26},{4,29},{5,28},{6,31},{7,30},{8,1},{9,0... | collective-permute-start | bytes 786440 | tf_op jit(solution)/shard_map/ppermute | solution.py:334
  54.6 18.0 %collective-permute-start.8 = (bf16[256,512]{1,0:T(8,128)(2,1)S(1)}, bf16[256,512]{1,0:T(8,128)(2,1)S(1)}, u32[]{:S(2)}, u32[]{:S(2)}) collective-permute-start(bf16[256,512]{1,0:T(8,128)(2,1)S(1)} %copy-done.4), channel_id=1, source_target_pairs={{0,9},{1,8},{2,11},{3,10},{4,13},{5,12},{6,15},{7,14},{8,17},{9,16... | collective-permute-start | bytes 786440 | tf_op jit(solution)/shard_map/ppermute | solution.py:334
  54.6 18.0 %collective-permute-start.9 = (bf16[256,512]{1,0:T(8,128)(2,1)S(1)}, bf16[256,512]{1,0:T(8,128)(2,1)S(1)}, u32[]{:S(2)}, u32[]{:S(2)}) collective-permute-start(bf16[256,512]{1,0:T(8,128)(2,1)S(1)} %copy-done.3), channel_id=1, source_target_pairs={{0,17},{1,16},{2,19},{3,18},{4,21},{5,20},{6,23},{7,22},{8,25},{9,... | collective-permute-start | bytes 786440 | tf_op jit(solution)/shard_map/ppermute | solution.py:334
  67.5 9.2 %copy-start.1 = (bf16[256,512]{1,0:T(8,128)(2,1)S(1)}, bf16[256,512]{1,0:T(8,128)(2,1)}, u32[]{:S(2)}) copy-start(bf16[256,512]{1,0:T(8,128)(2,1)} %get-tuple-element.91.refs_5_) | copy-start | bytes 786436
  72.6 16.6 %collective-permute-start.12 = (bf16[256,512]{1,0:T(8,128)(2,1)S(1)}, bf16[256,512]{1,0:T(8,128)(2,1)S(1)}, u32[]{:S(2)}, u32[]{:S(2)}) collective-permute-start(bf16[256,512]{1,0:T(8,128)(2,1)S(1)} %get-tuple-element.99), channel_id=1, source_target_pairs={{0,24},{1,25},{2,26},{3,27},{4,28},{5,29},{6,30},{7,31},{8,0},{9,1... | collective-permute-start | bytes 786440 | tf_op jit(solution)/shard_map/ppermute | solution.py:360
  74.9 14.3 %collective-permute-start.13 = (bf16[256,512]{1,0:T(8,128)(2,1)S(1)}, bf16[256,512]{1,0:T(8,128)(2,1)S(1)}, u32[]{:S(2)}, u32[]{:S(2)}) collective-permute-start(bf16[256,512]{1,0:T(8,128)(2,1)S(1)} %get-tuple-element.100), channel_id=1, source_target_pairs={{0,16},{1,17},{2,18},{3,19},{4,20},{5,21},{6,22},{7,23},{8,24},{9,... | collective-permute-start | bytes 786440 | tf_op jit(solution)/shard_map/ppermute | solution.py:360
  76.7 13.6 %collective-permute-start.14 = (bf16[256,512]{1,0:T(8,128)(2,1)S(1)}, bf16[256,512]{1,0:T(8,128)(2,1)S(1)}, u32[]{:S(2)}, u32[]{:S(2)}) collective-permute-start(bf16[256,512]{1,0:T(8,128)(2,1)S(1)} %get-tuple-element.101), channel_id=1, source_target_pairs={{0,8},{1,9},{2,10},{3,11},{4,12},{5,13},{6,14},{7,15},{8,16},{9,17... | collective-permute-start | bytes 786440 | tf_op jit(solution)/shard_map/ppermute | solution.py:360
  76.7 17.2 %collective-permute-start.11 = (bf16[256,512]{1,0:T(8,128)(2,1)S(1)}, bf16[256,512]{1,0:T(8,128)(2,1)S(1)}, u32[]{:S(2)}, u32[]{:S(2)}) collective-permute-start(bf16[256,512]{1,0:T(8,128)(2,1)S(1)} %get-tuple-element.90), channel_id=1, source_target_pairs={{0,1},{1,0},{2,3},{3,2},{4,5},{5,4},{6,7},{7,6},{8,9},{9,8},{10,11... | collective-permute-start | bytes 786440 | tf_op jit(solution)/shard_map/ppermute | solution.py:360
  90.3 14.2 %collective-permute-start.15 = (bf16[256,512]{1,0:T(8,128)(2,1)S(1)}, bf16[256,512]{1,0:T(8,128)(2,1)S(1)}, u32[]{:S(2)}, u32[]{:S(2)}) collective-permute-start(bf16[256,512]{1,0:T(8,128)(2,1)S(1)} %get-tuple-element.106), channel_id=1, source_target_pairs={{0,25},{1,24},{2,27},{3,26},{4,29},{5,28},{6,31},{7,30},{8,1},{9,0... | collective-permute-start | bytes 786440 | tf_op jit(solution)/shard_map/ppermute | solution.py:360
  93.6 11.0 %collective-permute-start.16 = (bf16[256,512]{1,0:T(8,128)(2,1)S(1)}, bf16[256,512]{1,0:T(8,128)(2,1)S(1)}, u32[]{:S(2)}, u32[]{:S(2)}) collective-permute-start(bf16[256,512]{1,0:T(8,128)(2,1)S(1)} %get-tuple-element.107), channel_id=1, source_target_pairs={{0,17},{1,16},{2,19},{3,18},{4,21},{5,20},{6,23},{7,22},{8,25},{9,... | collective-permute-start | bytes 786440 | tf_op jit(solution)/shard_map/ppermute | solution.py:360
  93.6 14.3 %collective-permute-start.17 = (bf16[256,512]{1,0:T(8,128)(2,1)S(1)}, bf16[256,512]{1,0:T(8,128)(2,1)S(1)}, u32[]{:S(2)}, u32[]{:S(2)}) collective-permute-start(bf16[256,512]{1,0:T(8,128)(2,1)S(1)} %get-tuple-element.108), channel_id=1, source_target_pairs={{0,9},{1,8},{2,11},{3,10},{4,13},{5,12},{6,15},{7,14},{8,17},{9,16... | collective-permute-start | bytes 786440 | tf_op jit(solution)/shard_map/ppermute | solution.py:360
  104.6 3.3 %copy-start.2 = (bf16[256,4096]{1,0:T(8,128)(2,1)}, bf16[256,4096]{1,0:T(8,128)(2,1)S(1)}, u32[]{:S(2)}) copy-start(bf16[256,4096]{1,0:T(8,128)(2,1)S(1)} %constant_dynamic-update-slice_fusion.1) | copy-start | bytes 6291460

commit v7 on v6

--- a/solution.py
+++ b/solution.py
@@ -237,9 +237,15 @@
                 def _(t):
                     tile(p, start, (begin + t * wide) * UNIT, WIDE)
 
-                @pl.loop(0, (rest - odd - wides * wide) // tail)
+                left = (rest - odd - wides * wide) // tail
+
+                @pl.loop(0, left // 2)
                 def _(t):
-                    tile(p, start, (begin + wides * wide + t * tail) * UNIT, TAIL)
+                    tile(p, start, (begin + wides * wide + t * 2 * tail) * UNIT, 2 * TAIL)
+
+                @pl.when(left % 2 == 1)
+                def _():
+                    tile(p, start, (hi - 2 * tail) * UNIT, TAIL)
 
             else:
                 @pl.loop(0, jnp.where(rest > odd, 1, 0))
@@ -255,9 +261,13 @@
                     def _():
                         tile(p, start, (end - NEAR_RUN) * TAIL, NEAR_RUN * TAIL)
 
-                    @pl.loop(0, jnp.where(count == NEAR_RUN, 0, count))
-                    def _(t):
-                        tile(p, start, (end - 1 - t) * TAIL, TAIL)
+                    @pl.when(count == 2)
+                    def _():
+                        tile(p, start, (end - 2) * TAIL, 2 * TAIL)
+
+                    @pl.when(count == 1)
+                    def _():
+                        tile(p, start, (end - 1) * TAIL, TAIL)
 
         if which != "near":
             for h in range(QPK):

time: 110 us -> 109 us (level); the launches traced: 109 us -> 109 us
  Pallas kernels: 34.4 us -> 35.6 us
    pallas_call x3, Pallas kernels: 29 us -> 30.2 us  [attend(): pl.pallas_call(functools.partial(attend_kernel, pieces, half, which), out...]
  transfers between devices with their start and end apart: 18 -> 18, of which waited for: 5 -> 5; matrix products, arithmetic and copies ran while one was open for 1% -> 1% of each run, Pallas kernels for 29% -> 30%
where the time goes in v7:
time: 109 us
  Pallas kernels  35.6 us (33%)
  waiting for transfers between devices  28.2 us (26%)
  starting transfers between devices  22.6 us (21%)
  blocking collectives  20.3 us (19%)
  local copies, waits for them, and re-layouts  1.33 us (1%)
    pallas_call x3, Pallas kernels, attend(): pl.pallas_call(functools.partial(attend_kernel, pieces, half, which), out...  30.2 us
    all_to_all x1, blocking collectives, per_device(): lax.all_to_all(pairs, 'ctx', split_axis=0, concat_axis=0, tiled=True, axi...  20.3 us
    ppermute x7, waiting for transfers between devices, give(): lax.ppermute(piece, 'ctx', shift(YS - dy, 0, dc))  13.8 us
    ppermute x4, waiting for transfers between devices, along(): return lax.ppermute(part, 'ctx', shift(0, dx, 0))  13.3 us
    ppermute x7, starting transfers between devices, send(): return lax.ppermute(part, 'ctx', shift(dy, 0, dc)) if dy or dc else part  9.12 us
    ppermute x7, starting transfers between devices, give(): lax.ppermute(piece, 'ctx', shift(YS - dy, 0, dc))  8.01 us
    ppermute x4, starting transfers between devices, along(): return lax.ppermute(part, 'ctx', shift(0, dx, 0))  5.47 us
    pallas_call x2, Pallas kernels, vmem_call(): pl.pallas_call(kernel, out_shape=out_shape, in_specs=[smem] * len(scalars...  5.42 us
  transfers between devices with their start and end apart: 18, of which 5 were waited for; matrix products, arithmetic and copies ran while one was open for 1% of the time, Pallas kernels for 30%

profile of v7, /device:TPU:65, one launch (start us, length us, event | category | flops | bytes accessed | tf_op | source)
XLA Modules:
  0.0 109.3 jit_solution(7166429616789332446)
XLA Ops:
  0.0 2.4 %shard_map.46 = bf16[8,2,256,128]{3,2,1,0:T(8,128)(2,1)} custom-call(bf16[256,1024]{1,0:T(8,128)(2,1)} %keys.1, bf16[256,1024]{1,0:T(8,128)(2,1)} %values.1), custom_call_target="tpu_custom_call" | custom-call | tf_op jit(solution)/shard_map/pallas_call | solution.py:65
  2.4 20.3 %all_to_all.5 = bf16[8,2,256,128]{3,2,1,0:T(8,128)(2,1)S(1)} all-to-all(bf16[8,2,256,128]{3,2,1,0:T(8,128)(2,1)} %shard_map.46), channel_id=1, replica_groups={{0,1,8,9,16,17,24,25},{2,3,10,11,18,19,26,27},{4,5,12,13,20,21,28,29},{..., dimensions={0} | all-to-all | bytes 2097152 | tf_op jit(solution)/shard_map/all_to_all | solution.py:328
  22.7 1.2 %collective-permute-start = (bf16[4,2,2,256,128]{4,3,2,1,0:T(8,128)(2,1)S(1)}, bf16[4,2,2,256,128]{4,3,2,1,0:T(8,128)(2,1)S(1)}, u32[]{:S(2)}, u32[]{:S(2)}) collective-permute-start(bf16[4,2,2,256,128]{4,3,2,1,0:T(8,128)(2,1)S(1)} %bitcast.3), channel_id=1, source_target_pairs={{0,2},{1,3},{2,4},{3,5},{4,6},{5,7},{6,0},{7,1},{8,10},{9,11},{10,... | collective-permute-start | bytes 3145736 | tf_op jit(solution)/shard_map/ppermute | solution.py:334
  23.9 1.5 %collective-permute-start.2 = (bf16[4,2,2,256,128]{4,3,2,1,0:T(8,128)(2,1)S(1)}, bf16[4,2,2,256,128]{4,3,2,1,0:T(8,128)(2,1)S(1)}, u32[]{:S(2)}, u32[]{:S(2)}) collective-permute-start(bf16[4,2,2,256,128]{4,3,2,1,0:T(8,128)(2,1)S(1)} %bitcast.4), channel_id=1, source_target_pairs={{0,6},{1,7},{2,0},{3,1},{4,2},{5,3},{6,4},{7,5},{8,14},{9,15},{10,... | collective-permute-start | bytes 3145736 | tf_op jit(solution)/shard_map/ppermute | solution.py:334
  25.4 3.1 %shard_map.47 = (bf16[256,512]{1,0:T(8,128)(2,1)}, bf16[256,512]{1,0:T(8,128)(2,1)}, bf16[256,512]{1,0:T(8,128)(2,1)}, bf16[256,512]{1,0:T(8,128)(2,1)}, bf16[25...) custom-call(s32[1]{0:T(128)} %bitcast.rank, ...), custom_call_target="tpu_custom_call" | custom-call | tf_op jit(solution)/shard_map/pallas_call | solution.py:65
  28.4 1.6 %collective-permute-start.4 = (bf16[256,512]{1,0:T(8,128)(2,1)}, bf16[256,512]{1,0:T(8,128)(2,1)S(1)}, u32[]{:S(2)}, u32[]{:S(2)}) collective-permute-start(bf16[256,512]{1,0:T(8,128)(2,1)} %get-tuple-element.61), channel_id=1, source_target_pairs={{0,1},{1,0},{2,3},{3,2},{4,5},{5,4},{6,7},{7,6},{8,9},{9,8},{10,11... | collective-permute-start | bytes 786440 | tf_op jit(solution)/shard_map/ppermute | solution.py:344
  30.0 0.1 copy.6
  30.2 0.1 reduce
  30.3 1.1 %collective-permute-done.4.refs_3_.refs_2_ = bf16[256,512]{1,0:T(8,128)(2,1)S(1)} collective-permute-done((bf16[256,512]{1,0:T(8,128)(2,1)}, bf16[256,512]{1,0:T(8,128)(2,1)S(1)}, u32[]{:S(2)}, u32[]{:S(2)}) %collective-permute-start.4) | collective-permute-done | bytes 262176 | tf_op jit(solution)/shard_map/ppermute | solution.py:344
  31.4 0.3 collective-permute-start.5
  31.7 1.8 %collective-permute-start.6 = (bf16[256,512]{1,0:T(8,128)(2,1)}, bf16[256,512]{1,0:T(8,128)(2,1)S(1)}, u32[]{:S(2)}, u32[]{:S(2)}) collective-permute-start(bf16[256,512]{1,0:T(8,128)(2,1)} %get-tuple-element.71), channel_id=1, source_target_pairs={{0,16},{1,17},{2,18},{3,19},{4,20},{5,21},{6,22},{7,23},{8,24},{9,... | collective-permute-start | bytes 786440 | tf_op jit(solution)/shard_map/ppermute | solution.py:344
  33.5 0.7 collective-permute-start.7
  34.2 13.3 %collective-permute-done.refs_1_ = bf16[4,2,2,256,128]{4,3,2,1,0:T(8,128)(2,1)S(1)} collective-permute-done((bf16[4,2,2,256,128]{4,3,2,1,0:T(8,128)(2,1)S(1)}, bf16[4,2,2,256,128]{4,3,2,1,0:T(8,128)(2,1)S(1)}, u32[]{:S(2)}, u32[]{:S(2)}) %collective-permute-start) | collective-permute-done | bytes 1048608 | tf_op jit(solution)/shard_map/ppermute | solution.py:334
  47.6 0.1 collective-permute-start.1
  47.6 0.0 collective-permute-done.2.refs_2_
  47.7 2.7 %collective-permute-start.3 = (bf16[2,2,2,256,128]{4,3,2,1,0:T(8,128)(2,1)S(1)}, bf16[2,2,2,256,128]{4,3,2,1,0:T(8,128)(2,1)S(1)}, u32[]{:S(2)}, u32[]{:S(2)}) collective-permute-start(bf16[2,2,2,256,128]{4,3,2,1,0:T(8,128)(2,1)S(1)} %slice.9), channel_id=1, source_target_pairs={{0,6},{1,7},{2,0},{3,1},{4,2},{5,3},{6,4},{7,5},{8,14},{9,15},{10,... | collective-permute-start | bytes 1572872 | tf_op jit(solution)/shard_map/ppermute | solution.py:334
  50.4 0.8 select_convert_fusion.marks
  51.2 0.0 collective-permute-done.5.refs_4_.refs_3_
  51.2 0.0 collective-permute-done.6.refs_5_.refs_4_
  51.3 0.0 collective-permute-done.7.refs_6_.refs_5_
  51.3 3.4 %collective-permute-start.10 = (bf16[256,512]{1,0:T(8,128)(2,1)S(1)}, bf16[256,512]{1,0:T(8,128)(2,1)S(1)}, u32[]{:S(2)}, u32[]{:S(2)}) collective-permute-start(bf16[256,512]{1,0:T(8,128)(2,1)S(1)} %copy-done.5), channel_id=1, source_target_pairs={{0,25},{1,24},{2,27},{3,26},{4,29},{5,28},{6,31},{7,30},{8,1},{9,0... | collective-permute-start | bytes 786440 | tf_op jit(solution)/shard_map/ppermute | solution.py:344
  54.6 0.0 collective-permute-start.8
  54.6 1.4 %collective-permute-start.9 = (bf16[256,512]{1,0:T(8,128)(2,1)S(1)}, bf16[256,512]{1,0:T(8,128)(2,1)S(1)}, u32[]{:S(2)}, u32[]{:S(2)}) collective-permute-start(bf16[256,512]{1,0:T(8,128)(2,1)S(1)} %copy-done.3), channel_id=1, source_target_pairs={{0,17},{1,16},{2,19},{3,18},{4,21},{5,20},{6,23},{7,22},{8,25},{9,... | collective-permute-start | bytes 786440 | tf_op jit(solution)/shard_map/ppermute | solution.py:344
  56.0 12.2 %shard_map.48 = (f32[4,1024,256]{2,1,0:T(8,128)S(1)}, f32[4,1024,128]{2,1,0:T(8,128)S(1)}) custom-call(s32[1]{0:T(128)} %bitcast.rank, s32[16]{0:T(128)S(1)} %copy-done, bf16[8192,128]{1,0:T(8,128)(2,1)S(1)} %select_convert_fusion.marks, bf16[4,2,2,256,128]{4,3,2,1,0:T(8,128)(2,1)S(1)} %bitcast.5, ...), custom_call_target="tpu_custom_call" | custom-call | flops 4294967296 | bytes 8388608 | tf_op jit(solution)/shard_map/pallas_call | solution.py:297
  68.2 0.0 collective-permute-done.1.refs_0_.refs_3_
  68.3 0.0 collective-permute-done.3.refs_1_.refs_4_
  68.3 4.1 %shard_map.49 = (bf16[256,512]{1,0:T(8,128)(2,1)S(1)}, bf16[256,512]{1,0:T(8,128)(2,1)S(1)}, bf16[256,512]{1,0:T(8,128)(2,1)S(1)}, bf16[256,512]{1,0:T(8,128)(2,1)S(1)}) custom-call(s32[1]{0:T(128)} %bitcast.rank, s32[16]{0:T(128)S(1)} %copy-done, bf16[8192,128]{1,0:T(8,128)(2,1)S(1)} %select_convert_fusion.marks, ...), custom_call_target="tpu_custom_call" | custom-call | flops 4294967296 | bytes 8388608 | tf_op jit(solution)/shard_map/pallas_call | solution.py:297
  72.4 0.0 collective-permute-done.10.refs_8_
  72.4 0.0 collective-permute-done.8.refs_6_
  72.5 0.0 collective-permute-done.9.refs_7_
  72.5 1.9 %collective-permute-start.12 = (bf16[256,512]{1,0:T(8,128)(2,1)S(1)}, bf16[256,512]{1,0:T(8,128)(2,1)S(1)}, u32[]{:S(2)}, u32[]{:S(2)}) collective-permute-start(bf16[256,512]{1,0:T(8,128)(2,1)S(1)} %get-tuple-element.99), channel_id=1, source_target_pairs={{0,24},{1,25},{2,26},{3,27},{4,28},{5,29},{6,30},{7,31},{8,0},{9,1... | collective-permute-start | bytes 786440 | tf_op jit(solution)/shard_map/ppermute | solution.py:370
  74.4 2.1 %collective-permute-start.13 = (bf16[256,512]{1,0:T(8,128)(2,1)S(1)}, bf16[256,512]{1,0:T(8,128)(2,1)S(1)}, u32[]{:S(2)}, u32[]{:S(2)}) collective-permute-start(bf16[256,512]{1,0:T(8,128)(2,1)S(1)} %get-tuple-element.100), channel_id=1, source_target_pairs={{0,16},{1,17},{2,18},{3,19},{4,20},{5,21},{6,22},{7,23},{8,24},{9,... | collective-permute-start | bytes 786440 | tf_op jit(solution)/shard_map/ppermute | solution.py:370
  76.5 0.0 collective-permute-start.14
  76.5 0.0 collective-permute-start.11
  76.5 13.8 %shard_map.50 = (bf16[256,512]{1,0:T(8,128)(2,1)S(1)}, bf16[256,512]{1,0:T(8,128)(2,1)S(1)}, bf16[256,512]{1,0:T(8,128)(2,1)S(1)}, bf16[256,512]{1,0:T(8,128)(2,1)S(1)}) custom-call(s32[1]{0:T(128)} %bitcast.rank, s32[16]{0:T(128)S(1)} %copy-done, bf16[8192,128]{1,0:T(8,128)(2,1)S(1)} %select_convert_fusion.marks, bf16[4,2,2,256,128]{4,3,2,1,0:T(8,128)(2,1)S(1)} %bitcast.6, ...), custom_call_target="tpu_custom_call" | custom-call | flops 4294967296 | bytes 8388608 | tf_op jit(solution)/shard_map/pallas_call | solution.py:297
  90.3 0.0 collective-permute-done.12
  90.3 0.0 collective-permute-done.13
  90.4 0.0 collective-permute-done.14
  90.4 2.2 %collective-permute-start.15 = (bf16[256,512]{1,0:T(8,128)(2,1)S(1)}, bf16[256,512]{1,0:T(8,128)(2,1)S(1)}, u32[]{:S(2)}, u32[]{:S(2)}) collective-permute-start(bf16[256,512]{1,0:T(8,128)(2,1)S(1)} %get-tuple-element.106), channel_id=1, source_target_pairs={{0,25},{1,24},{2,27},{3,26},{4,29},{5,28},{6,31},{7,30},{8,1},{9,0... | collective-permute-start | bytes 786440 | tf_op jit(solution)/shard_map/ppermute | solution.py:370
  92.6 0.4 collective-permute-start.16
  93.0 1.4 %collective-permute-start.17 = (bf16[256,512]{1,0:T(8,128)(2,1)S(1)}, bf16[256,512]{1,0:T(8,128)(2,1)S(1)}, u32[]{:S(2)}, u32[]{:S(2)}) collective-permute-start(bf16[256,512]{1,0:T(8,128)(2,1)S(1)} %get-tuple-element.108), channel_id=1, source_target_pairs={{0,9},{1,8},{2,11},{3,10},{4,13},{5,12},{6,15},{7,14},{8,17},{9,16... | collective-permute-start | bytes 786440 | tf_op jit(solution)/shard_map/ppermute | solution.py:370
  94.3 0.0 collective-permute-done.11
  94.3 0.2 broadcast_in_dim.18
  94.8 4.5 %collective-permute-done.15 = bf16[256,512]{1,0:T(8,128)(2,1)S(1)} collective-permute-done((bf16[256,512]{1,0:T(8,128)(2,1)S(1)}, bf16[256,512]{1,0:T(8,128)(2,1)S(1)}, u32[]{:S(2)}, u32[]{:S(2)}) %collective-permute-start.15) | collective-permute-done | bytes 262176 | tf_op jit(solution)/shard_map/ppermute | solution.py:370
  99.3 3.3 %collective-permute-done.16 = bf16[256,512]{1,0:T(8,128)(2,1)S(1)} collective-permute-done((bf16[256,512]{1,0:T(8,128)(2,1)S(1)}, bf16[256,512]{1,0:T(8,128)(2,1)S(1)}, u32[]{:S(2)}, u32[]{:S(2)}) %collective-permute-start.16) | collective-permute-done | bytes 262176 | tf_op jit(solution)/shard_map/ppermute | solution.py:370
  102.6 0.0 copy-start.2
  102.6 6.0 %collective-permute-done.17 = bf16[256,512]{1,0:T(8,128)(2,1)S(1)} collective-permute-done((bf16[256,512]{1,0:T(8,128)(2,1)S(1)}, bf16[256,512]{1,0:T(8,128)(2,1)S(1)}, u32[]{:S(2)}, u32[]{:S(2)}) %collective-permute-start.17) | collective-permute-done | bytes 262176 | tf_op jit(solution)/shard_map/ppermute | solution.py:370
  108.6 0.7 constant_dynamic-update-slice_fusion
  (24 shorter events, 0.3 us)
Async XLA Ops:
  2.4 27.7 %copy-start = (s32[16]{0:T(128)S(1)}, s32[16]{0:T(128)}, u32[]{:S(2)}) copy-start(s32[16]{0:T(128)} %doc_lengths.2) | copy-start | bytes 196
  22.7 24.8 %collective-permute-start = (bf16[4,2,2,256,128]{4,3,2,1,0:T(8,128)(2,1)S(1)}, bf16[4,2,2,256,128]{4,3,2,1,0:T(8,128)(2,1)S(1)}, u32[]{:S(2)}, u32[]{:S(2)}) collective-permute-start(bf16[4,2,2,256,128]{4,3,2,1,0:T(8,128)(2,1)S(1)} %bitcast.3), channel_id=1, source_target_pairs={{0,2},{1,3},{2,4},{3,5},{4,6},{5,7},{6,0},{7,1},{8,10},{9,11},{10,... | collective-permute-start | bytes 3145736 | tf_op jit(solution)/shard_map/ppermute | solution.py:334
  23.9 23.7 %collective-permute-start.2 = (bf16[4,2,2,256,128]{4,3,2,1,0:T(8,128)(2,1)S(1)}, bf16[4,2,2,256,128]{4,3,2,1,0:T(8,128)(2,1)S(1)}, u32[]{:S(2)}, u32[]{:S(2)}) collective-permute-start(bf16[4,2,2,256,128]{4,3,2,1,0:T(8,128)(2,1)S(1)} %bitcast.4), channel_id=1, source_target_pairs={{0,6},{1,7},{2,0},{3,1},{4,2},{5,3},{6,4},{7,5},{8,14},{9,15},{10,... | collective-permute-start | bytes 3145736 | tf_op jit(solution)/shard_map/ppermute | solution.py:334
  28.4 3.0 %collective-permute-start.4 = (bf16[256,512]{1,0:T(8,128)(2,1)}, bf16[256,512]{1,0:T(8,128)(2,1)S(1)}, u32[]{:S(2)}, u32[]{:S(2)}) collective-permute-start(bf16[256,512]{1,0:T(8,128)(2,1)} %get-tuple-element.61), channel_id=1, source_target_pairs={{0,1},{1,0},{2,3},{3,2},{4,5},{5,4},{6,7},{7,6},{8,9},{9,8},{10,11... | collective-permute-start | bytes 786440 | tf_op jit(solution)/shard_map/ppermute | solution.py:344
  31.4 19.9 %copy-start.5 = (bf16[256,512]{1,0:T(8,128)(2,1)S(1)}, bf16[256,512]{1,0:T(8,128)(2,1)}, u32[]{:S(2)}) copy-start(bf16[256,512]{1,0:T(8,128)(2,1)} %get-tuple-element.89) | copy-start | bytes 786436
  31.4 23.2 %copy-start.4 = (bf16[256,512]{1,0:T(8,128)(2,1)S(1)}, bf16[256,512]{1,0:T(8,128)(2,1)}, u32[]{:S(2)}) copy-start(bf16[256,512]{1,0:T(8,128)(2,1)} %get-tuple-element.87) | copy-start | bytes 786436
  31.4 23.2 %copy-start.3 = (bf16[256,512]{1,0:T(8,128)(2,1)S(1)}, bf16[256,512]{1,0:T(8,128)(2,1)}, u32[]{:S(2)}) copy-start(bf16[256,512]{1,0:T(8,128)(2,1)} %get-tuple-element.88) | copy-start | bytes 786436
  31.4 19.8 %collective-permute-start.5 = (bf16[256,512]{1,0:T(8,128)(2,1)}, bf16[256,512]{1,0:T(8,128)(2,1)S(1)}, u32[]{:S(2)}, u32[]{:S(2)}) collective-permute-start(bf16[256,512]{1,0:T(8,128)(2,1)} %get-tuple-element.69), channel_id=1, source_target_pairs={{0,8},{1,9},{2,10},{3,11},{4,12},{5,13},{6,14},{7,15},{8,16},{9,17... | collective-permute-start | bytes 786440 | tf_op jit(solution)/shard_map/ppermute | solution.py:344
  31.7 19.6 %collective-permute-start.6 = (bf16[256,512]{1,0:T(8,128)(2,1)}, bf16[256,512]{1,0:T(8,128)(2,1)S(1)}, u32[]{:S(2)}, u32[]{:S(2)}) collective-permute-start(bf16[256,512]{1,0:T(8,128)(2,1)} %get-tuple-element.71), channel_id=1, source_target_pairs={{0,16},{1,17},{2,18},{3,19},{4,20},{5,21},{6,22},{7,23},{8,24},{9,... | collective-permute-start | bytes 786440 | tf_op jit(solution)/shard_map/ppermute | solution.py:344
  33.5 17.8 %collective-permute-start.7 = (bf16[256,512]{1,0:T(8,128)(2,1)}, bf16[256,512]{1,0:T(8,128)(2,1)S(1)}, u32[]{:S(2)}, u32[]{:S(2)}) collective-permute-start(bf16[256,512]{1,0:T(8,128)(2,1)} %get-tuple-element.73), channel_id=1, source_target_pairs={{0,24},{1,25},{2,26},{3,27},{4,28},{5,29},{6,30},{7,31},{8,0},{9,1... | collective-permute-start | bytes 786440 | tf_op jit(solution)/shard_map/ppermute | solution.py:344
  47.6 20.7 %collective-permute-start.1 = (bf16[2,2,2,256,128]{4,3,2,1,0:T(8,128)(2,1)S(1)}, bf16[2,2,2,256,128]{4,3,2,1,0:T(8,128)(2,1)S(1)}, u32[]{:S(2)}, u32[]{:S(2)}) collective-permute-start(bf16[2,2,2,256,128]{4,3,2,1,0:T(8,128)(2,1)S(1)} %slice.8), channel_id=1, source_target_pairs={{0,2},{1,3},{2,4},{3,5},{4,6},{5,7},{6,0},{7,1},{8,10},{9,11},{10,... | collective-permute-start | bytes 1572872 | tf_op jit(solution)/shard_map/ppermute | solution.py:334
  47.7 20.6 %collective-permute-start.3 = (bf16[2,2,2,256,128]{4,3,2,1,0:T(8,128)(2,1)S(1)}, bf16[2,2,2,256,128]{4,3,2,1,0:T(8,128)(2,1)S(1)}, u32[]{:S(2)}, u32[]{:S(2)}) collective-permute-start(bf16[2,2,2,256,128]{4,3,2,1,0:T(8,128)(2,1)S(1)} %slice.9), channel_id=1, source_target_pairs={{0,6},{1,7},{2,0},{3,1},{4,2},{5,3},{6,4},{7,5},{8,14},{9,15},{10,... | collective-permute-start | bytes 1572872 | tf_op jit(solution)/shard_map/ppermute | solution.py:334
  51.3 21.2 %collective-permute-start.10 = (bf16[256,512]{1,0:T(8,128)(2,1)S(1)}, bf16[256,512]{1,0:T(8,128)(2,1)S(1)}, u32[]{:S(2)}, u32[]{:S(2)}) collective-permute-start(bf16[256,512]{1,0:T(8,128)(2,1)S(1)} %copy-done.5), channel_id=1, source_target_pairs={{0,25},{1,24},{2,27},{3,26},{4,29},{5,28},{6,31},{7,30},{8,1},{9,0... | collective-permute-start | bytes 786440 | tf_op jit(solution)/shard_map/ppermute | solution.py:344
  54.6 17.8 %collective-permute-start.8 = (bf16[256,512]{1,0:T(8,128)(2,1)S(1)}, bf16[256,512]{1,0:T(8,128)(2,1)S(1)}, u32[]{:S(2)}, u32[]{:S(2)}) collective-permute-start(bf16[256,512]{1,0:T(8,128)(2,1)S(1)} %copy-done.4), channel_id=1, source_target_pairs={{0,9},{1,8},{2,11},{3,10},{4,13},{5,12},{6,15},{7,14},{8,17},{9,16... | collective-permute-start | bytes 786440 | tf_op jit(solution)/shard_map/ppermute | solution.py:344
  54.6 17.8 %collective-permute-start.9 = (bf16[256,512]{1,0:T(8,128)(2,1)S(1)}, bf16[256,512]{1,0:T(8,128)(2,1)S(1)}, u32[]{:S(2)}, u32[]{:S(2)}) collective-permute-start(bf16[256,512]{1,0:T(8,128)(2,1)S(1)} %copy-done.3), channel_id=1, source_target_pairs={{0,17},{1,16},{2,19},{3,18},{4,21},{5,20},{6,23},{7,22},{8,25},{9,... | collective-permute-start | bytes 786440 | tf_op jit(solution)/shard_map/ppermute | solution.py:344
  68.3 8.2 %copy-start.1 = (bf16[256,512]{1,0:T(8,128)(2,1)S(1)}, bf16[256,512]{1,0:T(8,128)(2,1)}, u32[]{:S(2)}) copy-start(bf16[256,512]{1,0:T(8,128)(2,1)} %get-tuple-element.91.refs_5_) | copy-start | bytes 786436
  72.5 17.9 %collective-permute-start.12 = (bf16[256,512]{1,0:T(8,128)(2,1)S(1)}, bf16[256,512]{1,0:T(8,128)(2,1)S(1)}, u32[]{:S(2)}, u32[]{:S(2)}) collective-permute-start(bf16[256,512]{1,0:T(8,128)(2,1)S(1)} %get-tuple-element.99), channel_id=1, source_target_pairs={{0,24},{1,25},{2,26},{3,27},{4,28},{5,29},{6,30},{7,31},{8,0},{9,1... | collective-permute-start | bytes 786440 | tf_op jit(solution)/shard_map/ppermute | solution.py:370
  74.4 16.0 %collective-permute-start.13 = (bf16[256,512]{1,0:T(8,128)(2,1)S(1)}, bf16[256,512]{1,0:T(8,128)(2,1)S(1)}, u32[]{:S(2)}, u32[]{:S(2)}) collective-permute-start(bf16[256,512]{1,0:T(8,128)(2,1)S(1)} %get-tuple-element.100), channel_id=1, source_target_pairs={{0,16},{1,17},{2,18},{3,19},{4,20},{5,21},{6,22},{7,23},{8,24},{9,... | collective-permute-start | bytes 786440 | tf_op jit(solution)/shard_map/ppermute | solution.py:370
  76.5 13.9 %collective-permute-start.14 = (bf16[256,512]{1,0:T(8,128)(2,1)S(1)}, bf16[256,512]{1,0:T(8,128)(2,1)S(1)}, u32[]{:S(2)}, u32[]{:S(2)}) collective-permute-start(bf16[256,512]{1,0:T(8,128)(2,1)S(1)} %get-tuple-element.101), channel_id=1, source_target_pairs={{0,8},{1,9},{2,10},{3,11},{4,12},{5,13},{6,14},{7,15},{8,16},{9,17... | collective-permute-start | bytes 786440 | tf_op jit(solution)/shard_map/ppermute | solution.py:370
  76.5 17.8 %collective-permute-start.11 = (bf16[256,512]{1,0:T(8,128)(2,1)S(1)}, bf16[256,512]{1,0:T(8,128)(2,1)S(1)}, u32[]{:S(2)}, u32[]{:S(2)}) collective-permute-start(bf16[256,512]{1,0:T(8,128)(2,1)S(1)} %get-tuple-element.90), channel_id=1, source_target_pairs={{0,1},{1,0},{2,3},{3,2},{4,5},{5,4},{6,7},{7,6},{8,9},{9,8},{10,11... | collective-permute-start | bytes 786440 | tf_op jit(solution)/shard_map/ppermute | solution.py:370
  90.4 8.9 %collective-permute-start.15 = (bf16[256,512]{1,0:T(8,128)(2,1)S(1)}, bf16[256,512]{1,0:T(8,128)(2,1)S(1)}, u32[]{:S(2)}, u32[]{:S(2)}) collective-permute-start(bf16[256,512]{1,0:T(8,128)(2,1)S(1)} %get-tuple-element.106), channel_id=1, source_target_pairs={{0,25},{1,24},{2,27},{3,26},{4,29},{5,28},{6,31},{7,30},{8,1},{9,0... | collective-permute-start | bytes 786440 | tf_op jit(solution)/shard_map/ppermute | solution.py:370
  92.6 10.0 %collective-permute-start.16 = (bf16[256,512]{1,0:T(8,128)(2,1)S(1)}, bf16[256,512]{1,0:T(8,128)(2,1)S(1)}, u32[]{:S(2)}, u32[]{:S(2)}) collective-permute-start(bf16[256,512]{1,0:T(8,128)(2,1)S(1)} %get-tuple-element.107), channel_id=1, source_target_pairs={{0,17},{1,16},{2,19},{3,18},{4,21},{5,20},{6,23},{7,22},{8,25},{9,... | collective-permute-start | bytes 786440 | tf_op jit(solution)/shard_map/ppermute | solution.py:370
  93.0 15.6 %collective-permute-start.17 = (bf16[256,512]{1,0:T(8,128)(2,1)S(1)}, bf16[256,512]{1,0:T(8,128)(2,1)S(1)}, u32[]{:S(2)}, u32[]{:S(2)}) collective-permute-start(bf16[256,512]{1,0:T(8,128)(2,1)S(1)} %get-tuple-element.108), channel_id=1, source_target_pairs={{0,9},{1,8},{2,11},{3,10},{4,13},{5,12},{6,15},{7,14},{8,17},{9,16... | collective-permute-start | bytes 786440 | tf_op jit(solution)/shard_map/ppermute | solution.py:370
  102.6 6.0 %copy-start.2 = (bf16[256,4096]{1,0:T(8,128)(2,1)}, bf16[256,4096]{1,0:T(8,128)(2,1)S(1)}, u32[]{:S(2)}) copy-start(bf16[256,4096]{1,0:T(8,128)(2,1)S(1)} %constant_dynamic-update-slice_fusion.1) | copy-start | bytes 6291460
